TPU v7x, 32 devices: a whole 2x2x4 slice. The times are simulated.
32 devices in a mesh: dp: 8 (over z, y), blk: 4 (over x, core).
Axes of the slice: x: 2, y: 2, z: 4, core: 2. Of those that a mesh axis runs over, the one named last changes fastest.
Arguments:
- tokens: bfloat16 [768, 8, 768], P('blk', 'dp'), may hold values from -6 to 6
- w_query: bfloat16 [768, 768], replicated, may hold values from -0.3125 to 0.3125
- w_key: bfloat16 [768, 768], replicated, may hold values from -0.21875 to 0.21875
- w_value: bfloat16 [768, 768], replicated, may hold values from -0.21875 to 0.21875
- w_out: bfloat16 [768, 768], replicated, may hold values from -1.75 to 1.75
- w_inner: bfloat16 [768, 3072], replicated, may hold values from -0.21875 to 0.21875
- w_outer: bfloat16 [3072, 768], replicated, may hold values from -0.109375 to 0.109375
- down_one: bfloat16 [768, 64], replicated, may hold values from -0.21875 to 0.21875
- dbias_one: float32 [64], replicated, may hold values from -3 to 3
- up_one: bfloat16 [64, 768], replicated, may hold values from -0.75 to 0.75
- ubias_one: float32 [768], replicated, may hold values from -2 to 2
- gain_one: float32 [768], replicated, may hold values from 0.25 to 1.75
- shift_one: float32 [768], replicated, may hold values from -2 to 2
- down_two: bfloat16 [768, 64], replicated, may hold values from -0.21875 to 0.21875
- dbias_two: float32 [64], replicated, may hold values from -3 to 3
- up_two: bfloat16 [64, 768], replicated, may hold values from -0.75 to 0.75
- ubias_two: float32 [768], replicated, may hold values from -2 to 2
- gain_two: float32 [768], replicated, may hold values from 0.25 to 1.75
- shift_two: float32 [768], replicated, may hold values from -2 to 2
- seg_len: int32 [8, 6], P('dp'), may hold values from 0 to 512, as said below
- seg_valid: int32 [8, 6], P('dp'), may hold values from 0 to 512, as said below
- cotangent: bfloat16 [768, 8, 768], P('blk', 'dp'), may hold values from -6 to 6
Outputs:
- mixed: bfloat16 [768, 8, 768], P('blk', 'dp')
- input_grad: bfloat16 [768, 8, 768], P('blk', 'dp')
- grad_down_one: float32 [768, 64], replicated
- grad_dbias_one: float32 [64], replicated
- grad_up_one: float32 [64, 768], replicated
- grad_ubias_one: float32 [768], replicated
- grad_gain_one: float32 [768], replicated
- grad_shift_one: float32 [768], replicated
- grad_down_two: float32 [768, 64], replicated
- grad_dbias_two: float32 [64], replicated
- grad_up_two: float32 [64, 768], replicated
- grad_ubias_two: float32 [768], replicated
- grad_gain_two: float32 [768], replicated
- grad_shift_two: float32 [768], replicated
Inputs may be any that keep to these rules, and one draw needn't show every extreme that they name: `seg_len`: each row packs three or four sequences in order into its 6 slots, used slots first, the last two slots always unused (0). Used lengths are 64, 128 or 512 and sum to 768; exactly one slot has 512 and it begins at position 128. `seg_valid`: real tokens at the start of each slot, the rest of the slot being padding: 0 for an unused slot, else from half the slot's length to its length; for the slot of 512 more than 448.
All inputs are finite; a program needn't handle non-finite values.
Results may differ from a plain program's by a relative error of at most 0.02.
Values may be sent and summed in bfloat16 or wider, within the bound.
No kernel may reach another device: no remote copies, remote signals or barrier semaphores. Data moves between devices by JAX's collectives and lax.ppermute only.
A program may use at most 128 MiB of HBM per device.

v0:
```python
import jax
import jax.numpy as jnp
from jax import lax
from jax.sharding import PartitionSpec as P

HEADS = 12
HEAD = 64


def layer_norm(values, gain, shift):
    centre = jnp.mean(values, axis=-1, keepdims=True)
    centred = values - centre
    spread = jnp.mean(centred * centred, axis=-1, keepdims=True)
    return centred * lax.rsqrt(spread + 1e-06) * gain + shift


def gelu_exact(values):
    return jax.nn.gelu(values, approximate=False)


def project(left, weight):
    return jnp.einsum("sbk,kn->sbn", left, weight, preferred_element_type=jnp.float32)


def project_back(incoming, weight):
    return jnp.einsum("sbn,kn->sbk", incoming, weight, preferred_element_type=jnp.float32)


def weight_grad(left, incoming):
    return jnp.einsum("sbk,sbn->kn", left, incoming, preferred_element_type=jnp.float32)


def labels(lengths, counts, positions):
    slot_ends = jnp.cumsum(lengths, axis=1)
    slot_starts = slot_ends - lengths
    places = positions[:, None, None]
    segment = jnp.sum((places >= slot_ends[None]).astype(jnp.int32), axis=2)
    inside = (places >= slot_starts[None]) & (places < (slot_starts + counts)[None])
    is_live = jnp.sum(inside.astype(jnp.int32), axis=2) > 0
    return (segment, is_live)


def allowed_of(query_seg, key_seg, key_live):
    same = query_seg.T[:, None, :, None] == key_seg.T[:, None, None, :]
    return same & key_live.T[:, None, None, :]


def scores_of(query_heads, key_heads):
    return jnp.einsum("sbhe,tbhe->bhst", query_heads, key_heads, preferred_element_type=jnp.float32)


def weights_of(query_heads, log_total, query_seg, key_heads, key_seg, key_live):
    shifted = scores_of(query_heads, key_heads) - jnp.transpose(log_total, (1, 2, 0))[..., None]
    return jnp.where(allowed_of(query_seg, key_seg, key_live), jnp.exp(shifted), 0.0)


def block_grads(
    query_heads,
    grad_heads,
    log_total,
    delta_sum,
    query_seg,
    key_heads,
    value_heads,
    key_seg,
    key_live,
):
    weights_f = weights_of(query_heads, log_total, query_seg, key_heads, key_seg, key_live)
    grad_weights = jnp.einsum(
        "sbhe,tbhe->bhst", grad_heads, value_heads, preferred_element_type=jnp.float32
    )
    grad_scores = weights_f * (grad_weights - jnp.transpose(delta_sum, (1, 2, 0))[..., None])
    return (weights_f.astype(jnp.bfloat16), grad_scores.astype(jnp.bfloat16))


def adapter_forward(values, down, down_bias, up_proj, up_bias):
    inner_pre = project(values, down) + down_bias
    inner = gelu_exact(inner_pre).astype(jnp.bfloat16)
    return (inner_pre, inner, project(inner, up_proj) + up_bias)


def adapter_backward(values, down, up_proj, inner_pre, inner, incoming):
    out_grad = incoming.astype(jnp.bfloat16)
    grad_up = weight_grad(inner, out_grad)
    grad_ubias = jnp.sum(out_grad.astype(jnp.float32), axis=(0, 1))
    grad_inner = project_back(out_grad, up_proj)
    gelu_pull = jax.vjp(gelu_exact, inner_pre)[1]
    grad_pre = gelu_pull(grad_inner)[0].astype(jnp.bfloat16)
    grad_down = weight_grad(values, grad_pre)
    grad_dbias = jnp.sum(grad_pre.astype(jnp.float32), axis=(0, 1))
    return (project_back(grad_pre, down), (grad_down, grad_dbias, grad_up, grad_ubias))


def body(
    tokens,
    w_query,
    w_key,
    w_value,
    w_out,
    w_inner,
    w_outer,
    down_one,
    dbias_one,
    up_one,
    ubias_one,
    gain_one,
    shift_one,
    down_two,
    dbias_two,
    up_two,
    ubias_two,
    gain_two,
    shift_two,
    seg_len,
    seg_valid,
    cotangent,
):
    local_len, row_count, model_width = tokens.shape
    blocks = lax.axis_size("blk")
    blk_index = lax.axis_index("blk")
    head_shape = (local_len, row_count, HEADS, HEAD)
    stat_shape = (row_count, HEADS, local_len)
    query_b = (project(tokens, w_query) * 0.125).astype(jnp.bfloat16)
    key_b = project(tokens, w_key).astype(jnp.bfloat16)
    value_b = project(tokens, w_value).astype(jnp.bfloat16)
    query_heads = query_b.reshape(head_shape)
    own_pos = blk_index * local_len + jnp.arange(local_len, dtype=jnp.int32)
    query_seg, query_live = labels(seg_len, seg_valid, own_pos)

    def as_heads(array):
        return array.reshape((array.shape[0], row_count, HEADS, HEAD))

    key_blocks = []
    keys_all, values_all = (
        lax.all_gather(key_b, "blk", axis=0, tiled=True),
        lax.all_gather(value_b, "blk", axis=0, tiled=True),
    )
    all_seg, all_live = labels(seg_len, seg_valid, jnp.arange(local_len * blocks, dtype=jnp.int32))
    for block in range(blocks):
        first_row = block * local_len
        after_row = first_row + local_len
        key_blocks.append(
            (
                as_heads(keys_all[first_row:after_row]),
                as_heads(values_all[first_row:after_row]),
                all_seg[first_row:after_row],
                all_live[first_row:after_row],
            )
        )
    running_max = jnp.full(stat_shape, -1e30, jnp.float32)
    running_sum = jnp.zeros(stat_shape, jnp.float32)
    for key_heads, value_heads, key_seg, key_live in key_blocks:
        allowed = allowed_of(query_seg, key_seg, key_live)
        scores = jnp.where(allowed, scores_of(query_heads, key_heads), -1e30)
        new_max = jnp.maximum(running_max, jnp.max(scores, axis=-1))
        fresh = jnp.sum(jnp.where(allowed, jnp.exp(scores - new_max[..., None]), 0.0), axis=-1)
        running_sum = running_sum * jnp.exp(running_max - new_max) + fresh
        running_max = new_max
    log_total = jnp.transpose(running_max + jnp.log(running_sum), (2, 0, 1))
    attended_f = jnp.zeros(head_shape, jnp.float32)
    for key_heads, value_heads, key_seg, key_live in key_blocks:
        weights_b = weights_of(
            query_heads, log_total, query_seg, key_heads, key_seg, key_live
        ).astype(jnp.bfloat16)
        attended_f = attended_f + jnp.einsum(
            "bhst,tbhe->sbhe", weights_b, value_heads, preferred_element_type=jnp.float32
        )
    attended_b = attended_f.reshape(tokens.shape).astype(jnp.bfloat16)
    branch_b = project(attended_b, w_out).astype(jnp.bfloat16)
    pre_one, inner_one, adapter_one = adapter_forward(
        branch_b, down_one, dbias_one, up_one, ubias_one
    )
    summed_one = tokens.astype(jnp.float32) + branch_b.astype(jnp.float32) + adapter_one
    mid_f, norm_one_pull = jax.vjp(layer_norm, summed_one, gain_one, shift_one)
    mid_b = mid_f.astype(jnp.bfloat16)
    hidden_pre = project(mid_b, w_inner)
    hidden_b = gelu_exact(hidden_pre).astype(jnp.bfloat16)
    ffn_b = project(hidden_b, w_outer).astype(jnp.bfloat16)
    pre_two, inner_two, adapter_two = adapter_forward(ffn_b, down_two, dbias_two, up_two, ubias_two)
    summed_two = mid_b.astype(jnp.float32) + ffn_b.astype(jnp.float32) + adapter_two
    result, norm_two_pull = jax.vjp(layer_norm, summed_two, gain_two, shift_two)
    mixed = result.astype(jnp.bfloat16)
    grad_two, grad_gain_two, grad_shift_two = norm_two_pull(cotangent.astype(jnp.float32))
    adapt_two_back, grads_two = adapter_backward(
        ffn_b, down_two, up_two, pre_two, inner_two, grad_two
    )
    grad_ffn = (grad_two + adapt_two_back).astype(jnp.bfloat16)
    hidden_pull = jax.vjp(gelu_exact, hidden_pre)[1]
    grad_hidden = hidden_pull(project_back(grad_ffn, w_outer))[0].astype(jnp.bfloat16)
    grad_mid = grad_two + project_back(grad_hidden, w_inner)
    grad_one, grad_gain_one, grad_shift_one = norm_one_pull(grad_mid)
    adapt_one_back, grads_one = adapter_backward(
        branch_b, down_one, up_one, pre_one, inner_one, grad_one
    )
    grad_branch = (grad_one + adapt_one_back).astype(jnp.bfloat16)
    grad_attended = project_back(grad_branch, w_out).astype(jnp.bfloat16)
    grad_heads = grad_attended.reshape(head_shape)
    delta_sum = jnp.sum(grad_attended.astype(jnp.float32).reshape(head_shape) * attended_f, axis=-1)
    grad_query = jnp.zeros(head_shape, jnp.float32)
    key_terms = []
    value_terms = []
    for key_heads, value_heads, key_seg, key_live in key_blocks:
        weights_b, grad_scores = block_grads(
            query_heads,
            grad_heads,
            log_total,
            delta_sum,
            query_seg,
            key_heads,
            value_heads,
            key_seg,
            key_live,
        )
        grad_query = grad_query + jnp.einsum(
            "bhst,tbhe->sbhe", grad_scores, key_heads, preferred_element_type=jnp.float32
        )
        term_rows = (key_heads.shape[0], row_count, model_width)
        key_terms.append(
            jnp.einsum(
                "bhst,sbhe->tbhe", grad_scores, query_heads, preferred_element_type=jnp.float32
            ).reshape(term_rows)
        )
        value_terms.append(
            jnp.einsum(
                "bhst,sbhe->tbhe", weights_b, grad_heads, preferred_element_type=jnp.float32
            ).reshape(term_rows)
        )
    grad_key, grad_value = (
        lax.psum_scatter(
            jnp.concatenate(key_terms, 0).astype(jnp.bfloat16),
            "blk",
            scatter_dimension=0,
            tiled=True,
        ).astype(jnp.float32),
        lax.psum_scatter(
            jnp.concatenate(value_terms, 0).astype(jnp.bfloat16),
            "blk",
            scatter_dimension=0,
            tiled=True,
        ).astype(jnp.float32),
    )
    grad_query_b = grad_query.reshape(tokens.shape).astype(jnp.bfloat16)
    input_f = grad_one + project_back(grad_query_b, w_query) * 0.125
    input_f = (
        input_f
        + project_back(grad_key.astype(jnp.bfloat16), w_key)
        + project_back(grad_value.astype(jnp.bfloat16), w_value)
    )
    input_grad = input_f.astype(jnp.bfloat16)
    summed = lax.psum(
        (
            grads_one[0],
            grads_one[1],
            grads_one[2],
            grads_one[3],
            grad_gain_one,
            grad_shift_one,
            grads_two[0],
            grads_two[1],
            grads_two[2],
            grads_two[3],
            grad_gain_two,
            grad_shift_two,
        ),
        ("dp", "blk"),
    )
    return (mixed, input_grad) + tuple(summed)


def solution(mesh):
    in_specs = (
        P("blk", "dp", None),
        P(),
        P(),
        P(),
        P(),
        P(),
        P(),
        P(),
        P(),
        P(),
        P(),
        P(),
        P(),
        P(),
        P(),
        P(),
        P(),
        P(),
        P(),
        P("dp", None),
        P("dp", None),
        P("blk", "dp", None),
    )
    out_specs = (
        P("blk", "dp", None),
        P("blk", "dp", None),
        P(),
        P(),
        P(),
        P(),
        P(),
        P(),
        P(),
        P(),
        P(),
        P(),
        P(),
        P(),
    )
    return jax.shard_map(body, mesh=mesh, in_specs=in_specs, out_specs=out_specs, check_vma=False)
```

profile of v0, /device:TPU:1, one launch (start us, length us, event | category | flops | bytes accessed | tf_op | source)
XLA Modules:
  0.0 328.9 jit_solution(10559097162856177178)
XLA Ops:
  7.3 2.6 convolution_convert_fusion.11
  10.0 2.5 convolution_convert_fusion.12
  15.5 14.6 %all-gather.7.cloned.1.call-done = bf16[768,768]{1,0:T(8,128)(2,1)} async-done(((bf16[192,768]{1,0:T(8,128)(2,1)}), bf16[768,768]{1,0:T(8,128)(2,1)}) %all-gather.7.cloned.1.call-update) | async-done | bytes 1179664 | tf_op jit(solution)/shard_map/all_gather | solution.py:135
  32.4 17.4 %all-gather.5.cloned.1.call-done = bf16[768,768]{1,0:T(8,128)(2,1)} async-done(((bf16[192,768]{1,0:T(8,128)(2,1)}), bf16[768,768]{1,0:T(8,128)(2,1)}) %all-gather.5.cloned.1.call-update) | async-done | bytes 1179664 | tf_op jit(solution)/shard_map/all_gather | solution.py:136
  57.6 1.7 select_reduce_fusion.4
  72.7 6.5 %convolution_convert_fusion.9 = bf16[192,768]{1,0:T(8,128)(2,1)S(1)} fusion(bf16[3072,768]{1,0:T(8,128)(2,1)S(1)} %bitcast.262, f32[192,3072]{1,0:T(8,128)S(1)} %fusion.47), kind=kOutput, calls=%fused_computation.78 | convolution fusion | flops 944455680 | bytes 7372800 | tf_op jit(solution)/shard_map/sbk,kn->sbn/dot_general | solution.py:22
  86.0 5.8 %fusion.34 = f32[192,3072]{1,0:T(8,128)} fusion(bf16[3072,768]{1,0:T(8,128)(2,1)} %param.28, bf16[192,64]{0,1:T(8,128)(2,1)} %get-tuple-element.85, bf16[768,64]{0,1:T(8,128)(2,1)} %param.35, f32[192,1,768]{2,0,1:T(8,128)} %copy-done.25, f32[192]{0:T(256)} %copy-done.88), kind=kOutput, calls=%fused_computation.99 | convolution fusion | flops 925286400 | bytes 7791360 | tf_op jit(solution)/shard_map/sbn,kn->sbk/dot_general | solution.py:26
  91.7 11.1 %multiply_reduce_fusion.1 = (f32[768]{0:T(1024)}, f32[192]{0:T(256)S(1)}, f32[768]{0:T(1024)}, f32[192,1,768]{2,0,1:T(8,128)S(1)}) fusion(f32[192,1,768]{2,0,1:T(8,128)} %copy-done.23, f32[192]{0:T(256)} %copy-done.77, f32[192]{0:T(256)} %copy-done.75, f32[768]{0:T(1024)} %param.33, bf16[768,3072]{1,0:T(8,128)(2,1)} %param.27, f32[192,3072]{1,0:T(8,128)} %fusion.34, ...), kind=kOutput, calls=%fused_computation.105 | convolution fusion | flops 949909824 | bytes 11218944 | tf_op jit(solution)/shard_map/sbn,kn->sbk/dot_general | solution.py:26
  107.0 2.6 convolution_convert_fusion.8
  109.6 1.9 copy.164
  111.5 2.4 convolution_convert_fusion
  118.9 2.0 copy.165
  120.9 2.9 maximum_bitcast_fusion.1
  123.8 2.4 copy.208
  127.9 2.8 multiply_convert_fusion.3
  142.5 2.1 fusion.39
  149.7 39.2 %all-reduce = (f32[64]{0:T(128)}, f32[768]{0:T(1024)}, f32[768]{0:T(1024)}, f32[768]{0:T(1024)}, f32[64]{0:T(128)}, /*index=5*/f32[768]{0:T(1024)}, f32[768]{0:T(1024)}, f32[768]{0:T(1024)}) all-reduce(f32[64]{0:T(128)} %get-tuple-element.82, f32[768]{0:T(1024)S(1)} %copy-done.85, ...), channel_id=1, replica_groups=mesh['dp'=8,'blk'=4] {'dp','blk'}, use_global_device_ids=true, to_apply=%region_25.26 | all-reduce | flops 4736 | bytes 37888 | tf_op jit(solution)/shard_map/psum | solution.py:250
  189.0 2.3 convolution_bitcast_fusion
  191.3 2.6 fusion.24
  193.9 122.0 %all-reduce.4.cloned.1.call-done = (f32[768,64]{0,1:T(8,128)}, f32[64,768]{1,0:T(8,128)}, f32[768,64]{0,1:T(8,128)}, f32[64,768]{1,0:T(8,128)}) async-done(((f32[768,64]{0,1:T(8,128)}, f32[64,768]{1,0:T(8,128)}, f32[768,64]{0,1:T(8,128)}, f32[64,768]{1,0:T(8,128)}), (f32[768,64]{0,1:T(8,128)}, f32[64,768]{1,0:T(8,128)}, f32[768,64]{0,1:T(8,128)}, f32[64,768]{1,0:T(8,128)})) %all-reduce.4.cloned.1.call-update) | async-done | bytes 786448 | tf_op jit(solution)/shard_map/psum | solution.py:250
  315.9 1.6 copy.214
  317.5 1.6 copy.215
  319.1 1.6 copy.216
  320.7 1.6 copy.217
  (297 shorter events, 59.9 us)
Async XLA Ops:
  7.2 61.9 %copy-start = (bf16[768,768]{1,0:T(8,128)(2,1)S(1)}, bf16[768,768]{1,0:T(8,128)(2,1)}, u32[]{:S(2)}) copy-start(bf16[768,768]{1,0:T(8,128)(2,1)} %param.26) | copy-start | bytes 3538948
  7.2 5.3 %copy-start.43 = (bf16[192,1,768]{2,0,1:T(8,128)(2,1)S(1)}, bf16[192,1,768]{2,0,1:T(8,128)(2,1)}, u32[]{:S(2)}) copy-start(bf16[192,1,768]{2,0,1:T(8,128)(2,1)} %param.22) | copy-start | bytes 884740
  7.2 5.3 %copy-start.26 = (bf16[768,768]{1,0:T(8,128)(2,1)S(1)}, bf16[768,768]{1,0:T(8,128)(2,1)}, u32[]{:S(2)}) copy-start(bf16[768,768]{1,0:T(8,128)(2,1)} %param.23) | copy-start | bytes 3538948
  7.2 22.9 %all-gather.7.cloned.1.call-start = ((), (), s32[]{:S(2)}) async-start(), calls=%async_computation.3 | async-start | bytes 1474560 | tf_op jit(solution)/shard_map/all_gather | solution.py:135
  9.9 39.9 %all-gather.5.cloned.1.call-start = ((), (), s32[]{:S(2)}) async-start(), calls=%async_computation.2 | async-start | bytes 1474560 | tf_op jit(solution)/shard_map/all_gather | solution.py:136
  12.5 176.5 %reduce-scatter.9.cloned.1.call-start = ((), (), s32[]{:S(2)}) async-start(), calls=%async_computation.5 | async-start | bytes 1474560 | tf_op jit(solution)/shard_map/reshape.222
  61.6 5.0 %copy-start.1 = (f32[12,192,192]{1,2,0:T(8,128)}, f32[12,192,192]{1,2,0:T(8,128)S(1)}, u32[]{:S(2)}) copy-start(f32[12,192,192]{1,2,0:T(8,128)S(1)} %get-tuple-element.70) | copy-start | bytes 5308420
  70.4 9.1 %copy-start.23 = (f32[192,1,768]{2,0,1:T(8,128)}, f32[192,1,768]{2,0,1:T(8,128)S(1)}, u32[]{:S(2)}) copy-start(f32[192,1,768]{2,0,1:T(8,128)S(1)} %get-tuple-element.78) | copy-start | bytes 1769476
  70.5 9.0 %copy-start.75 = (f32[192]{0:T(256)}, f32[192]{0:T(256)S(1)}, u32[]{:S(2)}) copy-start(f32[192]{0:T(256)S(1)} %broadcast_multiply_fusion.1) | copy-start | bytes 2308
  71.3 8.2 %copy-start.77 = (f32[192]{0:T(256)}, f32[192]{0:T(256)S(1)}, u32[]{:S(2)}) copy-start(f32[192]{0:T(256)S(1)} %fusion.82) | copy-start | bytes 2308
  72.6 6.5 %copy-start.47 = (f32[192,3072]{1,0:T(8,128)}, f32[192,3072]{1,0:T(8,128)S(1)}, u32[]{:S(2)}) copy-start(f32[192,3072]{1,0:T(8,128)S(1)} %fusion.47) | copy-start | bytes 7077892
  72.6 6.5 %copy-start.61 = (bf16[768,64]{0,1:T(8,128)(2,1)S(1)}, bf16[768,64]{0,1:T(8,128)(2,1)}, u32[]{:S(2)}) copy-start(bf16[768,64]{0,1:T(8,128)(2,1)} %param.35) | copy-start | bytes 294916
  72.6 6.5 %copy-start.93 = (f32[64]{0:T(128)S(1)}, f32[64]{0:T(128)}, u32[]{:S(2)}) copy-start(f32[64]{0:T(128)} %param.36) | copy-start | bytes 772
  72.6 6.9 %copy-start.94 = (bf16[64,768]{1,0:T(8,128)(2,1)S(1)}, bf16[64,768]{1,0:T(8,128)(2,1)}, u32[]{:S(2)}) copy-start(bf16[64,768]{1,0:T(8,128)(2,1)} %param.37) | copy-start | bytes 294916
  72.6 6.9 %copy-start.98 = (f32[768]{0:T(1024)S(1)}, f32[768]{0:T(1024)}, u32[]{:S(2)}) copy-start(f32[768]{0:T(1024)} %param.38) | copy-start | bytes 9220
  91.7 11.1 %copy-start.87 = (f32[192]{0:T(256)S(1)}, f32[192]{0:T(256)}, u32[]{:S(2)}) copy-start(f32[192]{0:T(256)} %copy-done.86) | copy-start | bytes 2308
  91.7 11.1 %copy-start.24 = (f32[192,1,768]{2,0,1:T(8,128)S(1)}, f32[192,1,768]{2,0,1:T(8,128)}, u32[]{:S(2)}) copy-start(f32[192,1,768]{2,0,1:T(8,128)} %copy-done.23) | copy-start | bytes 1769476
  91.7 11.1 %copy-start.69 = (f32[768]{0:T(1024)S(1)}, f32[768]{0:T(1024)}, u32[]{:S(2)}) copy-start(f32[768]{0:T(1024)} %param.33) | copy-start | bytes 9220
  91.7 11.1 %copy-start.76 = (f32[192]{0:T(256)S(1)}, f32[192]{0:T(256)}, u32[]{:S(2)}) copy-start(f32[192]{0:T(256)} %copy-done.75) | copy-start | bytes 2308
  91.7 11.1 %copy-start.78 = (f32[192]{0:T(256)S(1)}, f32[192]{0:T(256)}, u32[]{:S(2)}) copy-start(f32[192]{0:T(256)} %copy-done.77) | copy-start | bytes 2308
  126.3 65.1 %reduce-scatter.7.cloned.1.call-start = ((), (), s32[]{:S(2)}) async-start(), calls=%async_computation.4 | async-start | bytes 1474560 | tf_op jit(solution)/shard_map/reshape.208
  139.7 176.2 %all-reduce.4.cloned.1.call-start = ((), (), s32[]{:S(2)}) async-start(), calls=%async_computation.6 | async-start | bytes 1572864 | tf_op jit(solution)/shard_map/psum | solution.py:250
  148.1 40.8 %copy-start.28 = (bf16[768,768]{1,0:T(8,128)(2,1)S(1)}, bf16[768,768]{1,0:T(8,128)(2,1)}, u32[]{:S(2)}) copy-start(bf16[768,768]{1,0:T(8,128)(2,1)} %param.25) | copy-start | bytes 3538948
  148.3 43.0 %copy-start.29 = (bf16[768,768]{1,0:T(8,128)(2,1)S(1)}, bf16[768,768]{1,0:T(8,128)(2,1)}, u32[]{:S(2)}) copy-start(bf16[768,768]{1,0:T(8,128)(2,1)} %param.24) | copy-start | bytes 3538948
  (84 other events, 180.2 us)
Sparse Core Ops, SparseCore 0:
  10.2 19.9 all-gather.6
  32.3 17.4 all-gather.4
  126.4 25.3 reduce-scatter.8
  154.4 25.7 reduce-scatter.6
  186.9 128.9 all-reduce.3
where the time goes:
time: 331 us; the launch traced here: 329 us
  waiting for transfers between devices  154 us (47%)
  matrix products  72.2 us (22%)
  blocking collectives  39.2 us (12%)
  local copies, waits for them, and re-layouts  35.6 us (11%)
  between operations  15.1 us (5%)
  other arithmetic  12.5 us (4%)
    psum x1, waiting for transfers between devices, body(): lax.psum((grads_one[0], grads_one[1], grads_one[2], grads_one[3], grad_ga...  122 us
    psum x1, blocking collectives, body(): lax.psum((grads_one[0], grads_one[1], grads_one[2], grads_one[3], grad_ga...  39.2 us
    dot_general x8, matrix products, project_back(): jnp.einsum('sbn,kn->sbk', incoming, weight, preferred_element_type=jnp.fl...  28.8 us
    unnamed x212, local copies, waits for them, and re-layouts  20.6 us
    all_gather x1, waiting for transfers between devices, body(): lax.all_gather(value_b, 'blk', axis=0, tiled=True)  17.4 us
    dot_general x10, matrix products, project(): jnp.einsum('sbk,kn->sbn', left, weight, preferred_element_type=jnp.float32)  15.1 us
    all_gather x1, waiting for transfers between devices, body(): lax.all_gather(key_b, 'blk', axis=0, tiled=True)  14.6 us
  transfers between devices with their start and end apart: 5, of which 3 were waited for; matrix products, arithmetic and copies ran while one was open for 10% of the time, Pallas kernels for 0%

commit v1 on v0

v1 whole, which is shorter than its diff:
```python
import functools

import jax
import jax.numpy as jnp
from jax import lax
from jax.experimental import pallas as pl
from jax.experimental.pallas import tpu as pltpu
from jax.sharding import PartitionSpec as P

HEAD = 64
GROUP = 4
LONG_AT = 128
LONG = 512
ROWS_A = 64
ROWS_B = 128
NEG = -1e30
F32 = jnp.float32
BF16 = jnp.bfloat16

VMEM = pl.BlockSpec(memory_space=pltpu.VMEM)
SMEM = pl.BlockSpec(memory_space=pltpu.SMEM)
ANY = pl.BlockSpec(memory_space=pl.ANY)


def nn(left, right):
    return lax.dot_general(left, right, (((1,), (0,)), ((), ())), preferred_element_type=F32)


def nt(left, right):
    return lax.dot_general(left, right, (((1,), (1,)), ((), ())), preferred_element_type=F32)


def tn(left, right):
    return lax.dot_general(left, right, (((0,), (0,)), ((), ())), preferred_element_type=F32)


def gelu_both(values):
    size = jnp.abs(values) * 0.7071067811865476
    inv = 1.0 / (1.0 + 0.3275911 * size)
    bell = jnp.exp(-size * size)
    poly = inv * (
        0.254829592
        + inv * (-0.284496736 + inv * (1.421413741 + inv * (-1.453152027 + inv * 1.061405429)))
    )
    tail = 0.5 * poly * bell
    phi = jnp.where(values >= 0, 1.0 - tail, tail)
    return values * phi, phi + values * bell * 0.3989422804014327


def normed(values):
    centre = jnp.mean(values, axis=-1, keepdims=True)
    centred = values - centre
    spread = jnp.mean(centred * centred, axis=-1, keepdims=True)
    scale = lax.rsqrt(spread + 1e-06)
    return centred * scale, scale


def norm_back(incoming, gain, normal, scale):
    scaled = incoming * gain
    first = jnp.mean(scaled, axis=-1, keepdims=True)
    second = jnp.mean(scaled * normal, axis=-1, keepdims=True)
    return scale * (scaled - first - normal * second)


def row_of(ref):
    return ref[...].reshape(1, ref.shape[0])


def own_rows(block):
    return (
        pl.multiple_of(jnp.where(block == 0, 128, 0), 64),
        pl.multiple_of(jnp.where(block == 0, 0, 64), 64),
    )


def partner_offset(block):
    return pl.multiple_of(jnp.where(block == 0, 0, jnp.where(block == 3, 256, 128)), 128)


def bounds(len_ref, valid_ref, places):
    low = jnp.zeros(places.shape, jnp.int32)
    high = jnp.zeros(places.shape, jnp.int32)
    start = jnp.int32(0)
    for slot in range(len_ref.shape[1]):
        end = start + len_ref[0, slot]
        inside = (places >= start) & (places < end)
        low = jnp.where(inside, start, low)
        high = jnp.where(inside, start + valid_ref[0, slot], high)
        start = end
    return low, high


def bias_of(len_ref, valid_ref, query_at, key_at, rows):
    places = query_at + lax.broadcasted_iota(jnp.int32, (rows, 1), 0)
    low, high = bounds(len_ref, valid_ref, places)
    keys = key_at + lax.broadcasted_iota(jnp.int32, (rows, LONG), 1)
    return jnp.where((keys >= low) & (keys < high), 0.0, NEG)


def bias_back_of(len_ref, valid_ref, key_at, query_at, rows):
    places = query_at + lax.broadcasted_iota(jnp.int32, (1, LONG), 1)
    low, high = bounds(len_ref, valid_ref, places)
    keys = key_at + lax.broadcasted_iota(jnp.int32, (rows, LONG), 0)
    return jnp.where((keys >= low) & (keys < high), 0.0, NEG)


def spread_heads(part):
    lane = lax.broadcasted_iota(jnp.int32, part.shape, 1) // HEAD
    return jnp.concatenate(
        [jnp.where(lane == head, part, jnp.zeros_like(part)) for head in range(GROUP)], axis=0
    )


def join_heads(stacked):
    rows = stacked.shape[0] // GROUP
    lane = lax.broadcasted_iota(jnp.int32, (rows, stacked.shape[1]), 1) // HEAD
    out = stacked[:rows]
    for head in range(1, GROUP):
        out = jnp.where(lane == head, stacked[head * rows : (head + 1) * rows], out)
    return out


def four(array):
    return jnp.concatenate([array] * GROUP, axis=0)


def project_kernel(block_ref, own_ref, mate_ref, wq_ref, wk_ref, wv_ref, q_ref, k_ref, v_ref):
    core = block_ref[0] % 2
    rows = own_ref.shape[0]
    own = own_ref[...]
    mate = mate_ref[...]
    q_ref[...] = (nn(own, wq_ref[...]) * 0.125).astype(BF16)
    mine = pl.multiple_of(core * rows, rows)
    other = pl.multiple_of((1 - core) * rows, rows)
    both = jnp.concatenate([own, mate], axis=0)
    keys = nn(both, wk_ref[...]).astype(BF16)
    values = nn(both, wv_ref[...]).astype(BF16)
    k_ref[pl.ds(mine, rows), :] = keys[:rows]
    k_ref[pl.ds(other, rows), :] = keys[rows:]
    v_ref[pl.ds(mine, rows), :] = values[:rows]
    v_ref[pl.ds(other, rows), :] = values[rows:]


def main_kernel(
    block_ref,
    len_ref,
    valid_ref,
    own_ref,
    far_ref,
    far_mate_ref,
    q_ref,
    kpair_ref,
    vpair_ref,
    cot_ref,
    down1_ref,
    dbias1_ref,
    up1_ref,
    ubias1_ref,
    gain1_ref,
    shift1_ref,
    down2_ref,
    dbias2_ref,
    up2_ref,
    ubias2_ref,
    gain2_ref,
    shift2_ref,
    wk_hbm,
    wv_hbm,
    wout_hbm,
    winner_hbm,
    wouter_hbm,
    mixed_ref,
    kbuf,
    vbuf,
    lse_ref,
    du1_ref,
    pack_ref,
    keep_ref,
    send_ref,
    wk_ref,
    wv_ref,
    wout_ref,
    winner_ref,
    wouter_ref,
    slope_ref,
    sems,
):
    copies = []
    for index, (source, target) in enumerate(
        (
            (wk_hbm, wk_ref),
            (wv_hbm, wv_ref),
            (wout_hbm, wout_ref),
            (winner_hbm, winner_ref),
            (wouter_hbm, wouter_ref),
        )
    ):
        copy = pltpu.make_async_copy(source, target, sems.at[index])
        copy.start()
        copies.append(copy)
    block = block_ref[0]
    core = block % 2
    chip = block // 2
    rows, width = own_ref.shape
    at_a, at_b = own_rows(block)
    meet_b = partner_offset(block)
    first = block * rows

    def mine(ref):
        return jnp.concatenate([ref[pl.ds(at_a, ROWS_A), :], ref[pl.ds(at_b, ROWS_B), :]], axis=0)

    def put(ref, value):
        ref[pl.ds(at_a, ROWS_A), :] = value[:ROWS_A]
        ref[pl.ds(at_b, ROWS_B), :] = value[ROWS_A:]

    def natural(value):
        rolled = jnp.concatenate([value[:, ROWS_A:], value[:, :ROWS_A]], axis=1)
        return jnp.where(block == 0, rolled, value)

    near = pl.multiple_of(chip * 2 * rows, 2 * rows)
    kbuf[pl.ds(near, 2 * rows), :] = kpair_ref[...]
    vbuf[pl.ds(near, 2 * rows), :] = vpair_ref[...]
    far_first = pl.multiple_of((1 - chip) * 2 * rows + core * rows, rows)
    far_second = pl.multiple_of((1 - chip) * 2 * rows + (1 - core) * rows, rows)
    both = jnp.concatenate([far_ref[...], far_mate_ref[...]], axis=0)
    copies[0].wait()
    keys = nn(both, wk_ref[...]).astype(BF16)
    kbuf[pl.ds(far_first, rows), :] = keys[:rows]
    kbuf[pl.ds(far_second, rows), :] = keys[rows:]
    copies[1].wait()
    values = nn(both, wv_ref[...]).astype(BF16)
    vbuf[pl.ds(far_first, rows), :] = values[:rows]
    vbuf[pl.ds(far_second, rows), :] = values[rows:]

    bias_a = four(bias_of(len_ref, valid_ref, first + at_a, LONG_AT, ROWS_A))
    bias_b = four(bias_of(len_ref, valid_ref, first + at_b, meet_b, ROWS_B))
    lane = lax.broadcasted_iota(jnp.int32, (1, 128), 1)
    attended_parts = []
    lse_parts = []
    for at, count, meet, bias in (
        (at_a, ROWS_A, LONG_AT, bias_a),
        (at_b, ROWS_B, meet_b, bias_b),
    ):
        pieces = []
        lse = jnp.zeros((count, 128), F32)
        for group in range(width // (GROUP * HEAD)):
            columns = slice(group * GROUP * HEAD, (group + 1) * GROUP * HEAD)
            queries = spread_heads(q_ref[pl.ds(at, count), columns])
            scores = nt(queries, kbuf[pl.ds(meet, LONG), columns]) + bias
            top = jnp.max(scores, axis=-1, keepdims=True)
            weights = jnp.exp(scores - top)
            total = jnp.sum(weights, axis=-1, keepdims=True)
            mixed_values = nn(weights.astype(BF16), vbuf[pl.ds(meet, LONG), columns])
            pieces.append(join_heads(mixed_values * (1.0 / total)))
            log_total = top + jnp.log(total)
            for head in range(GROUP):
                lse = jnp.where(
                    lane == group * GROUP + head, log_total[head * count : (head + 1) * count], lse
                )
        attended_parts.append(jnp.concatenate(pieces, axis=1))
        lse_parts.append(lse)
    attended_f = jnp.concatenate(attended_parts, axis=0)
    lse_own = jnp.concatenate(lse_parts, axis=0)
    put(lse_ref, lse_own)
    attended = attended_f.astype(BF16)
    copies[2].wait()
    branch = nn(attended, wout_ref[...]).astype(BF16)

    pre1 = nt(branch, down1_ref[...]) + row_of(dbias1_ref)
    inner1_f, slope1 = gelu_both(pre1)
    inner1 = inner1_f.astype(BF16)
    summed = (
        mine(own_ref).astype(F32) + branch.astype(F32) + nn(inner1, up1_ref[...]) + row_of(ubias1_ref)
    )
    normal1, scale1 = normed(summed)
    gain1 = row_of(gain1_ref)
    mid = (normal1 * gain1 + row_of(shift1_ref)).astype(BF16)

    copies[3].wait()
    copies[4].wait()
    hidden_units = winner_ref.shape[1]
    chunk = 512
    ffn_f = jnp.zeros((rows, width), F32)
    for at in range(0, hidden_units, chunk):
        hidden_f, slope = gelu_both(nn(mid, winner_ref[:, at : at + chunk]))
        slope_ref[:, at : at + chunk] = slope
        ffn_f = ffn_f + nn(hidden_f.astype(BF16), wouter_ref[at : at + chunk, :])
    ffn = ffn_f.astype(BF16)

    pre2 = nt(ffn, down2_ref[...]) + row_of(dbias2_ref)
    inner2_f, slope2 = gelu_both(pre2)
    inner2 = inner2_f.astype(BF16)
    summed = mid.astype(F32) + ffn.astype(F32) + nn(inner2, up2_ref[...]) + row_of(ubias2_ref)
    normal2, scale2 = normed(summed)
    gain2 = row_of(gain2_ref)
    put(mixed_ref, (normal2 * gain2 + row_of(shift2_ref)).astype(BF16))

    cot = mine(cot_ref).astype(F32)
    grad_gain2 = jnp.sum(cot * normal2, axis=0, keepdims=True)
    grad_shift2 = jnp.sum(cot, axis=0, keepdims=True)
    du2 = norm_back(cot, gain2, normal2, scale2)

    def adapter_back(source, down, up, inner, slope, incoming):
        out_grad = incoming.astype(BF16)
        grad_up = tn(inner, out_grad)
        grad_ubias = jnp.sum(out_grad.astype(F32), axis=0, keepdims=True)
        grad_pre = (nt(out_grad, up) * slope).astype(BF16)
        grad_down = tn(grad_pre, source)
        grad_dbias = jnp.sum(grad_pre.astype(F32), axis=0, keepdims=True)
        return nn(grad_pre, down), grad_down, grad_dbias, grad_up, grad_ubias

    back2, grad_down2, grad_dbias2, grad_up2, grad_ubias2 = adapter_back(
        ffn, down2_ref[...], up2_ref[...], inner2, slope2, du2
    )
    dffn = (du2 + back2).astype(BF16)
    dmid = du2
    for at in range(0, hidden_units, chunk):
        dhidden = (nt(dffn, wouter_ref[at : at + chunk, :]) * slope_ref[:, at : at + chunk]).astype(
            BF16
        )
        dmid = dmid + nt(dhidden, winner_ref[:, at : at + chunk])

    grad_gain1 = jnp.sum(dmid * normal1, axis=0, keepdims=True)
    grad_shift1 = jnp.sum(dmid, axis=0, keepdims=True)
    du1 = norm_back(dmid, gain1, normal1, scale1)
    back1, grad_down1, grad_dbias1, grad_up1, grad_ubias1 = adapter_back(
        branch, down1_ref[...], up1_ref[...], inner1, slope1, du1
    )
    put(du1_ref, du1)

    blank = jnp.zeros((1, width), F32)
    both_dbias = jnp.concatenate(
        [grad_dbias1, grad_dbias2, jnp.zeros((1, width - 2 * grad_dbias1.shape[1]), F32)], axis=1
    )
    quarters = (
        (grad_up1, grad_ubias1, both_dbias),
        (grad_down1, grad_gain1, grad_shift1),
        (grad_up2, grad_ubias2, blank),
        (grad_down2, grad_gain2, grad_shift2),
    )
    for index, (matrix, one, two) in enumerate(quarters):
        small = jnp.concatenate([one, two, jnp.zeros((14, width), F32)], axis=0)
        whole = jnp.concatenate([matrix, small], axis=0).astype(BF16)
        place = jnp.where(chip == index // 2, 0, 1)

        @pl.when(core == index % 2)
        def _(place=place, whole=whole):
            keep_ref[place] = whole

        @pl.when(core != index % 2)
        def _(place=place, whole=whole):
            send_ref[place] = whole

    dbranch = (du1 + back1).astype(BF16)
    dattended = nt(dbranch, wout_ref[...]).astype(BF16)
    pack_ref[pl.ds(at_a, ROWS_A), :] = dattended[:ROWS_A]
    pack_ref[pl.ds(at_b, ROWS_B), :] = dattended[ROWS_A:]
    product = dattended.astype(F32) * attended_f
    product_hi = product.astype(BF16)
    product_lo = (product - product_hi.astype(F32)).astype(BF16)
    head_of = lax.broadcasted_iota(jnp.int32, (16, width), 1) // HEAD
    picks = (head_of == lax.broadcasted_iota(jnp.int32, (16, width), 0)).astype(BF16)
    delta = natural(nt(picks, product_hi) + nt(picks, product_lo))
    lse_rows = natural(
        jnp.transpose(jnp.concatenate([lse_own, jnp.zeros((256 - rows, 128), F32)], axis=0))[
            :16, :rows
        ]
    )

    def pieces_of(value, count):
        out = []
        for _ in range(count):
            piece = value.astype(BF16)
            value = value - piece.astype(F32)
            out.append(jnp.concatenate([piece, jnp.zeros((16, 256 - rows), BF16)], axis=1))
        return out

    pack_ref[rows : rows + 16, :] = jnp.concatenate(pieces_of(lse_rows, 3), axis=1)
    pack_ref[rows + 16 : rows + 32, :] = jnp.concatenate(
        pieces_of(delta, 2) + [jnp.zeros((16, 256), BF16)], axis=1
    )


def query_back_kernel(
    block_ref,
    len_ref,
    valid_ref,
    own_ref,
    mate_ref,
    far_ref,
    far_mate_ref,
    q_ref,
    kbuf,
    vbuf,
    lse_ref,
    pack_ref,
    du1_ref,
    wq_ref,
    qbuf,
    part_ref,
):
    block = block_ref[0]
    rows, width = own_ref.shape
    at_a, at_b = own_rows(block)
    meet_b = partner_offset(block)
    first = block * rows
    wq = wq_ref[...]
    tokens = jnp.concatenate(
        [mate_ref[...], far_ref[...], far_mate_ref[...]], axis=0
    )
    queries_all = (nn(tokens, wq) * 0.125).astype(BF16)
    qbuf[pl.ds(pl.multiple_of(block * rows, rows), rows), :] = q_ref[...]
    for index in range(3):
        spot = pl.multiple_of((block ^ (index + 1)) * rows, rows)
        qbuf[pl.ds(spot, rows), :] = queries_all[index * rows : (index + 1) * rows]
    bias_a = four(bias_of(len_ref, valid_ref, first + at_a, LONG_AT, ROWS_A))
    bias_b = four(bias_of(len_ref, valid_ref, first + at_b, meet_b, ROWS_B))
    lane = lax.broadcasted_iota(jnp.int32, (1, 128), 1)
    for at, count, meet, bias in (
        (at_a, ROWS_A, LONG_AT, bias_a),
        (at_b, ROWS_B, meet_b, bias_b),
    ):
        pieces = []
        lse = lse_ref[pl.ds(at, count), :]
        for group in range(width // (GROUP * HEAD)):
            columns = slice(group * GROUP * HEAD, (group + 1) * GROUP * HEAD)
            log_total = jnp.concatenate(
                [
                    jnp.sum(
                        jnp.where(lane == group * GROUP + head, lse, 0.0), axis=-1, keepdims=True
                    )
                    for head in range(GROUP)
                ],
                axis=0,
            )
            keys = kbuf[pl.ds(meet, LONG), columns]
            scores = nt(spread_heads(q_ref[pl.ds(at, count), columns]), keys) + bias
            probs = jnp.exp(scores - log_total)
            dprobs = nt(
                spread_heads(pack_ref[pl.ds(at, count), columns]), vbuf[pl.ds(meet, LONG), columns]
            )
            delta = jnp.sum(probs * dprobs, axis=-1, keepdims=True)
            dscores = (probs * (dprobs - delta)).astype(BF16)
            pieces.append(join_heads(nn(dscores, keys)))
        dquery = jnp.concatenate(pieces, axis=1).astype(BF16)
        part_ref[pl.ds(at, count), :] = du1_ref[pl.ds(at, count), :] + nt(dquery, wq) * 0.125


def key_back_kernel(
    block_ref,
    len_ref,
    valid_ref,
    own_ref,
    mate_ref,
    far_ref,
    far_mate_ref,
    qbuf,
    kbuf,
    vbuf,
    part_ref,
    wk_ref,
    wv_ref,
    out_ref,
    abuf,
    lse_ref,
    delta_ref,
):
    block = block_ref[0]
    rows, width = out_ref.shape
    at_a, at_b = own_rows(block)
    meet_b = partner_offset(block)
    first = block * rows
    for index, ref in enumerate((own_ref, mate_ref, far_ref, far_mate_ref)):
        source = block ^ index
        abuf[pl.ds(pl.multiple_of(source * rows, rows), rows), :] = ref[:rows, :]
        lse = ref[rows : rows + 16, :].astype(F32)
        delta = ref[rows + 16 : rows + 32, :].astype(F32)
        lse_ref[source] = lse[:, :256] + (lse[:, 256:512] + lse[:, 512:])
        delta_ref[source] = delta[:, :256] + delta[:, 256:512]
    lse_all = jnp.concatenate([lse_ref[index][:, :rows] for index in range(4)], axis=1)
    delta_all = jnp.concatenate([delta_ref[index][:, :rows] for index in range(4)], axis=1)
    bias_a = four(bias_back_of(len_ref, valid_ref, first + at_a, LONG_AT, ROWS_A))
    bias_b = four(bias_back_of(len_ref, valid_ref, first + at_b, meet_b, ROWS_B))

    def window(stat, meet):
        if isinstance(meet, int):
            return stat[:, meet : meet + LONG]
        out = stat[:, :LONG]
        for start in (128, 256):
            out = jnp.where(meet == start, stat[:, start : start + LONG], out)
        return out

    for at, count, meet, bias in (
        (at_a, ROWS_A, LONG_AT, bias_a),
        (at_b, ROWS_B, meet_b, bias_b),
    ):
        lse_here = window(lse_all, meet)
        delta_here = window(delta_all, meet)
        dkeys = []
        dvalues = []
        for group in range(width // (GROUP * HEAD)):
            columns = slice(group * GROUP * HEAD, (group + 1) * GROUP * HEAD)

            def per_head(stat):
                return jnp.concatenate(
                    [
                        jnp.broadcast_to(
                            stat[group * GROUP + head : group * GROUP + head + 1], (count, LONG)
                        )
                        for head in range(GROUP)
                    ],
                    axis=0,
                )

            queries = qbuf[pl.ds(meet, LONG), columns]
            grads = abuf[pl.ds(meet, LONG), columns]
            own_at = pl.multiple_of(first + at, 64)
            scores = nt(spread_heads(kbuf[pl.ds(own_at, count), columns]), queries) + bias
            probs = jnp.exp(scores - per_head(lse_here))
            dprobs = nt(spread_heads(vbuf[pl.ds(own_at, count), columns]), grads)
            dscores = (probs * (dprobs - per_head(delta_here))).astype(BF16)
            dkeys.append(join_heads(nn(dscores, queries)))
            dvalues.append(join_heads(nn(probs.astype(BF16), grads)))
        dkey = jnp.concatenate(dkeys, axis=1).astype(BF16)
        dvalue = jnp.concatenate(dvalues, axis=1).astype(BF16)
        out_ref[pl.ds(at, count), :] = (
            part_ref[pl.ds(at, count), :] + nt(dkey, wk_ref[...]) + nt(dvalue, wv_ref[...])
        ).astype(BF16)


def params(megabytes):
    return pltpu.CompilerParams(vmem_limit_bytes=megabytes << 20)


def cost(gigaflop, megabytes):
    return pl.CostEstimate(
        flops=int(gigaflop * 1e9), bytes_accessed=int(megabytes * 1e6), transcendentals=0
    )


def shape(dims, dtype):
    return jax.ShapeDtypeStruct(dims, dtype)


def body(
    dp_size,
    tokens,
    w_query,
    w_key,
    w_value,
    w_out,
    w_inner,
    w_outer,
    down_one,
    dbias_one,
    up_one,
    ubias_one,
    gain_one,
    shift_one,
    down_two,
    dbias_two,
    up_two,
    ubias_two,
    gain_two,
    shift_two,
    seg_len,
    seg_valid,
    cotangent,
):
    rows, _, width = tokens.shape
    adapt = up_one.shape[0]
    hidden = w_inner.shape[1]
    block = lax.axis_index("blk")
    core, chip = block % 2, block // 2
    block_arr = block.reshape(1).astype(jnp.int32)
    own = tokens.reshape(rows, width)
    cot = cotangent.reshape(rows, width)

    def swap(array, mask):
        return lax.ppermute(array, "blk", [(i, i ^ mask) for i in range(4)])

    def swap_all(array, mask):
        return lax.ppermute(
            array, ("dp", "blk"), [(i, i ^ mask) for i in range(4 * dp_size)]
        )

    far = swap(own, 2)
    mate = swap(own, 1)
    far_mate = swap(far, 1)

    q, kpair, vpair = pl.pallas_call(
        project_kernel,
        in_specs=[SMEM] + [VMEM] * 5,
        out_specs=[VMEM] * 3,
        out_shape=[shape((rows, width), BF16)] + [shape((2 * rows, width), BF16)] * 2,
        compiler_params=params(24),
        cost_estimate=cost(1.2, 5.0),
        name="project",
    )(block_arr, own, mate, w_query, w_key, w_value)

    pack_rows = rows + 32
    part_rows = adapt + 16
    mixed, kbuf, vbuf, lse, du1, pack, keep, send = pl.pallas_call(
        main_kernel,
        in_specs=[SMEM] * 3 + [VMEM] * 19 + [ANY] * 5,
        out_specs=[VMEM] * 8,
        out_shape=[
            shape((rows, width), BF16),
            shape((4 * rows, width), BF16),
            shape((4 * rows, width), BF16),
            shape((rows, 128), F32),
            shape((rows, width), F32),
            shape((pack_rows, width), BF16),
            shape((2, part_rows, width), BF16),
            shape((2, part_rows, width), BF16),
        ],
        scratch_shapes=[
            pltpu.VMEM((width, width), BF16),
            pltpu.VMEM((width, width), BF16),
            pltpu.VMEM((width, width), BF16),
            pltpu.VMEM((width, hidden), BF16),
            pltpu.VMEM((hidden, width), BF16),
            pltpu.VMEM((rows, hidden), F32),
            pltpu.SemaphoreType.DMA((5,)),
        ],
        compiler_params=params(48),
        cost_estimate=cost(8.0, 20.0),
        name="layer",
    )(
        block_arr,
        seg_len,
        seg_valid,
        own,
        far,
        far_mate,
        q,
        kpair,
        vpair,
        cot,
        down_one.T,
        dbias_one,
        up_one,
        ubias_one,
        gain_one,
        shift_one,
        down_two.T,
        dbias_two,
        up_two,
        ubias_two,
        gain_two,
        shift_two,
        w_key,
        w_value,
        w_out,
        w_inner,
        w_outer,
    )

    pack_far = swap(pack, 2)
    pack_mate = swap(pack, 1)
    pack_far_mate = swap(pack_far, 1)

    def add(left, right):
        return (left.astype(F32) + right.astype(F32)).astype(BF16)

    total = add(keep, swap_all(send, 1))
    total = add(total[0], swap_all(total[1], 2))
    mask = 4
    while mask < 4 * dp_size:
        total = add(total, swap_all(total, mask))
        mask *= 2
    half = jnp.stack([total, swap_all(total, 2)])
    other_half = swap_all(half, 1)

    qbuf, part = pl.pallas_call(
        query_back_kernel,
        in_specs=[SMEM] * 3 + [VMEM] * 11,
        out_specs=[VMEM] * 2,
        out_shape=[shape((4 * rows, width), BF16), shape((rows, width), F32)],
        compiler_params=params(40),
        cost_estimate=cost(2.0, 6.0),
        name="query_back",
    )(
        block_arr,
        seg_len,
        seg_valid,
        own,
        mate,
        far,
        far_mate,
        q,
        kbuf,
        vbuf,
        lse,
        pack,
        du1,
        w_query,
    )
    input_grad = pl.pallas_call(
        key_back_kernel,
        in_specs=[SMEM] * 3 + [VMEM] * 10,
        out_specs=VMEM,
        out_shape=shape((rows, width), BF16),
        scratch_shapes=[
            pltpu.VMEM((4 * rows, width), BF16),
            pltpu.VMEM((4, 16, 256), F32),
            pltpu.VMEM((4, 16, 256), F32),
        ],
        compiler_params=params(40),
        cost_estimate=cost(2.5, 6.0),
        name="key_back",
    )(
        block_arr,
        seg_len,
        seg_valid,
        pack,
        pack_mate,
        pack_far,
        pack_far_mate,
        qbuf,
        kbuf,
        vbuf,
        part,
        w_key,
        w_value,
    )

    def quarter(index):
        same = jnp.where(chip == index // 2, half[0], half[1])
        flipped = jnp.where(chip == index // 2, other_half[0], other_half[1])
        return jnp.where(core == index % 2, same, flipped).astype(F32)

    up1, down1, up2, down2 = (quarter(index) for index in range(4))
    return (
        mixed.reshape(tokens.shape),
        input_grad.reshape(tokens.shape),
        down1[:adapt].T,
        up1[adapt + 1, :adapt],
        up1[:adapt],
        up1[adapt],
        down1[adapt],
        down1[adapt + 1],
        down2[:adapt].T,
        up1[adapt + 1, adapt : 2 * adapt],
        up2[:adapt],
        up2[adapt],
        down2[adapt],
        down2[adapt + 1],
    )


def solution(mesh):
    in_specs = (
        (P("blk", "dp", None),) + (P(),) * 18 + (P("dp", None),) * 2 + (P("blk", "dp", None),)
    )
    out_specs = (P("blk", "dp", None),) * 2 + (P(),) * 12
    return jax.shard_map(
        functools.partial(body, mesh.shape["dp"]),
        mesh=mesh,
        in_specs=in_specs,
        out_specs=out_specs,
        check_vma=False,
    )
```

time: 331 us -> 88.7 us (0.27)
  waiting for transfers between devices: 154 us -> 16.6 us
  matrix products: 72.2 us -> 0 us
  blocking collectives: 39.2 us -> 0 us
  Pallas kernels: 0 us -> 29.9 us
  starting transfers between devices: 0.21 us -> 23.4 us
  local copies, waits for them, and re-layouts: 35.6 us -> 14.4 us
  between operations: 15.1 us -> 1.06 us
  other arithmetic: 12.5 us -> 2.87 us
    psum x1 -> x0, waiting for transfers between devices: 122 us -> none  [body(): lax.psum((grads_one[0], grads_one[1], grads_one[2], grads_one[3], grad_ga...]
    dot_general x46 -> x0, matrix products: 72.2 us -> none  [the longest x8 28.8 us: project_back(): jnp.einsum('sbn,kn->sbk', incoming, weight, preferred_element_type=jnp.fl...]
    psum x1 -> x0, blocking collectives: 39.2 us -> none  [body(): lax.psum((grads_one[0], grads_one[1], grads_one[2], grads_one[3], grad_ga...]
    all_gather x2 -> x0, waiting for transfers between devices: 32 us -> none  [the longest x1 17.4 us: body(): lax.all_gather(value_b, 'blk', axis=0, tiled=True)]
    pallas_call x0 -> x4, Pallas kernels: none -> 29.9 us  [the longest x1 17.2 us: body(): pl.pallas_call(main_kernel, in_specs=[SMEM] * 3 + [VMEM] * 19 + [ANY] * 5...]
    ppermute x0 -> x13, starting transfers between devices: none -> 23.4 us  [the longest x6 12.2 us: swap(): return lax.ppermute(array, 'blk', [(i, i ^ mask) for i in range(4)])]
    ppermute x0 -> x13, waiting for transfers between devices: none -> 16.6 us  [the longest x7 10.6 us: swap_all(): lax.ppermute(array, ('dp', 'blk'), [(i, i ^ mask) for i in range(4 * dp_s...]
    unnamed x212 -> x64, local copies, waits for them, and re-layouts: 20.6 us -> 10.4 us
  transfers between devices with their start and end apart: 5 -> 13, of which waited for: 3 -> 6; matrix products, arithmetic and copies ran while one was open for 10% -> 2% of each run, Pallas kernels for 0% -> 14%
where the time goes in v1:
time: 88.7 us; the launch traced here: 88.2 us
  Pallas kernels  29.9 us (34%)
  starting transfers between devices  23.4 us (26%)
  waiting for transfers between devices  16.6 us (19%)
  local copies, waits for them, and re-layouts  14.4 us (16%)
  other arithmetic  2.87 us (3%)
  between operations  1.06 us (1%)
    pallas_call x1, Pallas kernels, body(): pl.pallas_call(main_kernel, in_specs=[SMEM] * 3 + [VMEM] * 19 + [ANY] * 5...  17.2 us
    ppermute x6, starting transfers between devices, swap(): return lax.ppermute(array, 'blk', [(i, i ^ mask) for i in range(4)])  12.2 us
    ppermute x7, starting transfers between devices, swap_all(): lax.ppermute(array, ('dp', 'blk'), [(i, i ^ mask) for i in range(4 * dp_s...  11.2 us
    ppermute x7, waiting for transfers between devices, swap_all(): lax.ppermute(array, ('dp', 'blk'), [(i, i ^ mask) for i in range(4 * dp_s...  10.6 us
    unnamed x64, local copies, waits for them, and re-layouts  10.4 us
    ppermute x6, waiting for transfers between devices, swap(): return lax.ppermute(array, 'blk', [(i, i ^ mask) for i in range(4)])  6 us
    pallas_call x1, Pallas kernels, body(): pl.pallas_call(key_back_kernel, in_specs=[SMEM] * 3 + [VMEM] * 10, out_sp...  5.8 us
    pallas_call x1, Pallas kernels, body(): pl.pallas_call(query_back_kernel, in_specs=[SMEM] * 3 + [VMEM] * 11, out_...  5.52 us
  transfers between devices with their start and end apart: 13, of which 6 were waited for; matrix products, arithmetic and copies ran while one was open for 2% of the time, Pallas kernels for 14%

profile of v1, /device:TPU:1, one launch (start us, length us, event | category | flops | bytes accessed | tf_op | source)
XLA Modules:
  0.0 88.2 jit_solution(16852703621391397735)
XLA Ops:
  0.6 2.1 %collective-permute-start = (bf16[192,768]{1,0:T(8,128)(2,1)}, bf16[192,768]{1,0:T(8,128)(2,1)S(1)}, u32[]{:S(2)}, u32[]{:S(2)}) collective-permute-start(bf16[192,768]{1,0:T(8,128)(2,1)} %bitcast.39), channel_id=1, source_target_pairs={{0,2},{1,3},{2,0},{3,1},{4,6},{5,7},{6,4},{7,5},{8,10},{9,11},{10,... | collective-permute-start | bytes 884744 | tf_op jit(solution)/shard_map/ppermute | solution.py:580
  3.7 6.0 %collective-permute-done.far_ref = bf16[192,768]{1,0:T(8,128)(2,1)S(1)} collective-permute-done((bf16[192,768]{1,0:T(8,128)(2,1)}, bf16[192,768]{1,0:T(8,128)(2,1)S(1)}, u32[]{:S(2)}, u32[]{:S(2)}) %collective-permute-start) | collective-permute-done | bytes 294944 | tf_op jit(solution)/shard_map/ppermute | solution.py:580
  9.7 1.2 %collective-permute-start.1 = (bf16[192,768]{1,0:T(8,128)(2,1)S(1)}, bf16[192,768]{1,0:T(8,128)(2,1)S(1)}, u32[]{:S(2)}, u32[]{:S(2)}) collective-permute-start(bf16[192,768]{1,0:T(8,128)(2,1)S(1)} %collective-permute-done.far_ref), channel_id=1, source_target_pairs={{0,1},{1,0},{2,3},{3,2},{4,5},{5,4},{6,7},{7,6},{8,9},{9,8},{10,11... | collective-permute-start | bytes 884744 | tf_op jit(solution)/shard_map/ppermute | solution.py:580
  10.9 1.3 %copy-done = bf16[768,768]{1,0:T(8,128)(2,1)S(1)} copy-done((bf16[768,768]{1,0:T(8,128)(2,1)S(1)}, bf16[768,768]{1,0:T(8,128)(2,1)}, u32[]{:S(2)}) %copy-start) | copy-done | bytes 1179672
  12.2 1.3 %copy-done.2 = bf16[768,768]{1,0:T(8,128)(2,1)S(1)} copy-done((bf16[768,768]{1,0:T(8,128)(2,1)S(1)}, bf16[768,768]{1,0:T(8,128)(2,1)}, u32[]{:S(2)}) %copy-start.2) | copy-done | bytes 1179672
  13.5 1.3 %copy-done.4 = bf16[768,768]{1,0:T(8,128)(2,1)S(1)} copy-done((bf16[768,768]{1,0:T(8,128)(2,1)S(1)}, bf16[768,768]{1,0:T(8,128)(2,1)}, u32[]{:S(2)}) %copy-start.4) | copy-done | bytes 1179672
  15.9 1.3 %project.1 = (bf16[192,768]{1,0:T(8,128)(2,1)S(1)}, bf16[384,768]{1,0:T(8,128)(2,1)S(1)}, bf16[384,768]{1,0:T(8,128)(2,1)S(1)}) custom-call(s32[1]{0:T(128)} %bitcast.block_ref, bf16[192,768]{1,0:T(8,128)(2,1)S(1)} %bitcast.41, bf16[192,768]{1,0:T(8,128)(2,1)S(1)} %collective-permute-done.2.mate_ref, bf16[768,768]{1,0:T(8,128)(2,1)S(1)} %copy-done, ...), custom_call_target="tpu_custom_call" | custom-call | flops 1200000000 | bytes 5000000 | tf_op jit(solution)/shard_map/project/pallas_call | solution.py:591
  17.4 17.2 %layer.1 = (bf16[192,768]{1,0:T(8,128)(2,1)}, bf16[768,768]{1,0:T(8,128)(2,1)S(1)}, bf16[768,768]{1,0:T(8,128)(2,1)}, f32[192,128]{1,0:T(8,128)S(1)}, f32[192,76...) custom-call(s32[1]{0:T(128)} %bitcast.block_ref, ...), custom_call_target="tpu_custom_call" | custom-call | flops 8000000000 | bytes 20000000 | tf_op jit(solution)/shard_map/layer/pallas_call | solution.py:603
  34.7 1.5 %collective-permute-done.6 = bf16[2,80,768]{2,1,0:T(8,128)(2,1)S(1)} collective-permute-done((bf16[2,80,768]{2,1,0:T(8,128)(2,1)S(1)}, bf16[2,80,768]{2,1,0:T(8,128)(2,1)S(1)}, u32[]{:S(2)}, u32[]{:S(2)}) %collective-permute-start.6) | collective-permute-done | bytes 245792 | tf_op jit(solution)/shard_map/ppermute | solution.py:583
  36.3 1.5 %collective-permute-start.7 = (bf16[80,768]{1,0:T(8,128)(2,1)S(1)}, bf16[80,768]{1,0:T(8,128)(2,1)S(1)}, u32[]{:S(2)}, u32[]{:S(2)}) collective-permute-start(bf16[80,768]{1,0:T(8,128)(2,1)S(1)} %slice_bitcast_fusion.2), channel_id=1, source_target_pairs={{0,2},{1,3},{2,0},{3,1},{4,6},{5,7},{6,4},{7,5},{8,10},{9,11},{10,... | collective-permute-start | bytes 368648 | tf_op jit(solution)/shard_map/ppermute | solution.py:583
  37.9 3.3 %collective-permute-done.7 = bf16[80,768]{1,0:T(8,128)(2,1)S(1)} collective-permute-done((bf16[80,768]{1,0:T(8,128)(2,1)S(1)}, bf16[80,768]{1,0:T(8,128)(2,1)S(1)}, u32[]{:S(2)}, u32[]{:S(2)}) %collective-permute-start.7) | collective-permute-done | bytes 122912 | tf_op jit(solution)/shard_map/ppermute | solution.py:583
  41.2 1.5 %collective-permute-start.8 = (bf16[80,768]{1,0:T(8,128)(2,1)S(1)}, bf16[80,768]{1,0:T(8,128)(2,1)S(1)}, u32[]{:S(2)}, u32[]{:S(2)}) collective-permute-start(bf16[80,768]{1,0:T(8,128)(2,1)S(1)} %fusion), channel_id=1, source_target_pairs={{0,4},{1,5},{2,6},{3,7},{4,0},{5,1},{6,2},{7,3},{8,12},{9,13},{10,... | collective-permute-start | bytes 368648 | tf_op jit(solution)/shard_map/ppermute | solution.py:583
  42.8 2.3 %collective-permute-done.8 = bf16[80,768]{1,0:T(8,128)(2,1)S(1)} collective-permute-done((bf16[80,768]{1,0:T(8,128)(2,1)S(1)}, bf16[80,768]{1,0:T(8,128)(2,1)S(1)}, u32[]{:S(2)}, u32[]{:S(2)}) %collective-permute-start.8) | collective-permute-done | bytes 122912 | tf_op jit(solution)/shard_map/ppermute | solution.py:583
  45.1 1.6 %collective-permute-start.9 = (bf16[80,768]{1,0:T(8,128)(2,1)S(1)}, bf16[80,768]{1,0:T(8,128)(2,1)S(1)}, u32[]{:S(2)}, u32[]{:S(2)}) collective-permute-start(bf16[80,768]{1,0:T(8,128)(2,1)S(1)} %add_convert_fusion.3), channel_id=1, source_target_pairs={{0,8},{1,9},{2,10},{3,11},{4,12},{5,13},{6,14},{7,15},{8,0},{9,1},... | collective-permute-start | bytes 368648 | tf_op jit(solution)/shard_map/ppermute | solution.py:583
  46.7 2.3 %collective-permute-done.9 = bf16[80,768]{1,0:T(8,128)(2,1)S(1)} collective-permute-done((bf16[80,768]{1,0:T(8,128)(2,1)S(1)}, bf16[80,768]{1,0:T(8,128)(2,1)S(1)}, u32[]{:S(2)}, u32[]{:S(2)}) %collective-permute-start.9) | collective-permute-done | bytes 122912 | tf_op jit(solution)/shard_map/ppermute | solution.py:583
  49.0 2.5 %collective-permute-start.10 = (bf16[80,768]{1,0:T(8,128)(2,1)S(1)}, bf16[80,768]{1,0:T(8,128)(2,1)S(1)}, u32[]{:S(2)}, u32[]{:S(2)}) collective-permute-start(bf16[80,768]{1,0:T(8,128)(2,1)S(1)} %add_convert_fusion.2), channel_id=1, source_target_pairs={{0,16},{1,17},{2,18},{3,19},{4,20},{5,21},{6,22},{7,23},{8,24},{9,... | collective-permute-start | bytes 368648 | tf_op jit(solution)/shard_map/ppermute | solution.py:583
  54.6 2.4 %collective-permute-start.11 = (bf16[80,768]{1,0:T(8,128)(2,1)}, bf16[80,768]{1,0:T(8,128)(2,1)}, u32[]{:S(2)}, u32[]{:S(2)}) collective-permute-start(bf16[80,768]{1,0:T(8,128)(2,1)} %add_convert_fusion.1), channel_id=1, source_target_pairs={{0,2},{1,3},{2,0},{3,1},{4,6},{5,7},{6,4},{7,5},{8,10},{9,11},{10,... | collective-permute-start | bytes 368648 | tf_op jit(solution)/shard_map/ppermute | solution.py:583
  57.0 4.7 %collective-permute-start.3 = (bf16[224,768]{1,0:T(8,128)(2,1)S(1)}, bf16[224,768]{1,0:T(8,128)(2,1)S(1)}, u32[]{:S(2)}, u32[]{:S(2)}) collective-permute-start(bf16[224,768]{1,0:T(8,128)(2,1)S(1)} %get-tuple-element.31.pack_ref.own_ref), channel_id=1, source_target_pairs={{0,1},{1,0},{2,3},{3,2},{4,5},{5,4},{6,7},{7,6},{8,9},{9,8},{10,11... | collective-permute-start | bytes 1032200 | tf_op jit(solution)/shard_map/ppermute | solution.py:580
  61.7 2.0 %collective-permute-start.5 = (bf16[224,768]{1,0:T(8,128)(2,1)S(1)}, bf16[224,768]{1,0:T(8,128)(2,1)S(1)}, u32[]{:S(2)}, u32[]{:S(2)}) collective-permute-start(bf16[224,768]{1,0:T(8,128)(2,1)S(1)} %collective-permute-done.4.far_ref), channel_id=1, source_target_pairs={{0,1},{1,0},{2,3},{3,2},{4,5},{5,4},{6,7},{7,6},{8,9},{9,8},{10,11... | collective-permute-start | bytes 1032200 | tf_op jit(solution)/shard_map/ppermute | solution.py:580
  64.8 1.6 %collective-permute-start.12 = (bf16[2,80,768]{2,1,0:T(8,128)(2,1)S(1)}, bf16[2,80,768]{2,1,0:T(8,128)(2,1)S(1)}, u32[]{:S(2)}, u32[]{:S(2)}) collective-permute-start(bf16[2,80,768]{2,1,0:T(8,128)(2,1)S(1)} %pad_maximum_fusion), channel_id=1, source_target_pairs={{0,1},{1,0},{2,3},{3,2},{4,5},{5,4},{6,7},{7,6},{8,9},{9,8},{10,11... | collective-permute-start | bytes 737288 | tf_op jit(solution)/shard_map/ppermute | solution.py:583
  68.2 1.3 %copy-done.28 = bf16[768,768]{1,0:T(8,128)(2,1)S(1)} copy-done((bf16[768,768]{1,0:T(8,128)(2,1)S(1)}, bf16[768,768]{1,0:T(8,128)(2,1)}, u32[]{:S(2)}) %copy-start.28) | copy-done | bytes 1179672
  69.5 1.3 %copy-done.29 = bf16[768,768]{1,0:T(8,128)(2,1)S(1)} copy-done((bf16[768,768]{1,0:T(8,128)(2,1)S(1)}, bf16[768,768]{1,0:T(8,128)(2,1)}, u32[]{:S(2)}) %copy-start.29) | copy-done | bytes 1179672
  71.8 5.5 %query_back.1 = (bf16[768,768]{1,0:T(8,128)(2,1)S(1)}, f32[192,768]{1,0:T(8,128)S(1)}) custom-call(s32[1]{0:T(128)} %bitcast.block_ref, s32[1,6]{1,0:T(1,128)S(1)} %copy-done.23, s32[1,6]{1,0:T(1,128)S(1)} %copy-done.24, bf16[192,768]{1,0:T(8,128)(2,1)S(1)} %bitcast.43, bf16[192,768]{1,0:T(8,128)(2,1)S(1)} %collective-permute-done.2.mate_ref, ...), custom_call_target="tpu_custom_call" | custom-call | flops 2000000000 | bytes 6000000 | tf_op jit(solution)/shard_map/query_back/pallas_call | solution.py:675
  77.4 5.8 %key_back.1 = bf16[192,768]{1,0:T(8,128)(2,1)} custom-call(s32[1]{0:T(128)} %bitcast.block_ref, s32[1,6]{1,0:T(1,128)S(1)} %copy-done.23, s32[1,6]{1,0:T(1,128)S(1)} %copy-done.24, bf16[224,768]{1,0:T(8,128)(2,1)S(1)} %get-tuple-element.31.pack_ref.own_ref, bf16[224,768]{1,0:T(8,128)(2,1)S(1)} %collective-permute-done.3.mate_ref, ...), custom_call_target="tpu_custom_call" | custom-call | flops 2500000000 | bytes 6000000 | tf_op jit(solution)/shard_map/key_back/pallas_call | solution.py:699
  (84 shorter events, 14.4 us)
Async XLA Ops:
  0.6 9.1 %collective-permute-start = (bf16[192,768]{1,0:T(8,128)(2,1)}, bf16[192,768]{1,0:T(8,128)(2,1)S(1)}, u32[]{:S(2)}, u32[]{:S(2)}) collective-permute-start(bf16[192,768]{1,0:T(8,128)(2,1)} %bitcast.39), channel_id=1, source_target_pairs={{0,2},{1,3},{2,0},{3,1},{4,6},{5,7},{6,4},{7,5},{8,10},{9,11},{10,... | collective-permute-start | bytes 884744 | tf_op jit(solution)/shard_map/ppermute | solution.py:580
  2.8 8.2 %collective-permute-start.2 = (bf16[192,768]{1,0:T(8,128)(2,1)}, bf16[192,768]{1,0:T(8,128)(2,1)S(1)}, u32[]{:S(2)}, u32[]{:S(2)}) collective-permute-start(bf16[192,768]{1,0:T(8,128)(2,1)} %bitcast.40), channel_id=1, source_target_pairs={{0,1},{1,0},{2,3},{3,2},{4,5},{5,4},{6,7},{7,6},{8,9},{9,8},{10,11... | collective-permute-start | bytes 884744 | tf_op jit(solution)/shard_map/ppermute | solution.py:580
  9.7 7.5 %collective-permute-start.1 = (bf16[192,768]{1,0:T(8,128)(2,1)S(1)}, bf16[192,768]{1,0:T(8,128)(2,1)S(1)}, u32[]{:S(2)}, u32[]{:S(2)}) collective-permute-start(bf16[192,768]{1,0:T(8,128)(2,1)S(1)} %collective-permute-done.far_ref), channel_id=1, source_target_pairs={{0,1},{1,0},{2,3},{3,2},{4,5},{5,4},{6,7},{7,6},{8,9},{9,8},{10,11... | collective-permute-start | bytes 884744 | tf_op jit(solution)/shard_map/ppermute | solution.py:580
  15.7 1.6 %copy-start.13 = (bf16[768,64]{0,1:T(8,128)(2,1)S(1)}, bf16[768,64]{0,1:T(8,128)(2,1)}, u32[]{:S(2)}) copy-start(bf16[768,64]{0,1:T(8,128)(2,1)} %param.35) | copy-start | bytes 294916
  15.7 1.6 %copy-start.14 = (bf16[64,768]{1,0:T(8,128)(2,1)S(1)}, bf16[64,768]{1,0:T(8,128)(2,1)}, u32[]{:S(2)}) copy-start(bf16[64,768]{1,0:T(8,128)(2,1)} %up2_ref.1) | copy-start | bytes 294916
  15.7 1.6 %copy-start.15 = (f32[768]{0:T(1024)S(1)}, f32[768]{0:T(1024)}, u32[]{:S(2)}) copy-start(f32[768]{0:T(1024)} %ubias1_ref.1) | copy-start | bytes 9220
  15.7 1.6 %copy-start.16 = (f32[768]{0:T(1024)S(1)}, f32[768]{0:T(1024)}, u32[]{:S(2)}) copy-start(f32[768]{0:T(1024)} %gain1_ref.1) | copy-start | bytes 9220
  17.2 17.4 %copy-start.25 = (bf16[192,768]{1,0:T(8,128)(2,1)}, bf16[192,768]{1,0:T(8,128)(2,1)S(1)}, u32[]{:S(2)}) copy-start(bf16[192,768]{1,0:T(8,128)(2,1)S(1)} %get-tuple-element.27.q_ref) | copy-start | bytes 884740
  17.2 17.4 %copy-start.9 = (bf16[192,768]{1,0:T(8,128)(2,1)}, bf16[192,768]{1,0:T(8,128)(2,1)S(1)}, u32[]{:S(2)}) copy-start(bf16[192,768]{1,0:T(8,128)(2,1)S(1)} %collective-permute-done.1.far_mate_ref) | copy-start | bytes 884740
  34.6 20.0 %copy-start.27 = (bf16[768,768]{1,0:T(8,128)(2,1)}, bf16[768,768]{1,0:T(8,128)(2,1)S(1)}, u32[]{:S(2)}) copy-start(bf16[768,768]{1,0:T(8,128)(2,1)S(1)} %get-tuple-element.32.kbuf) | copy-start | bytes 3538948
  34.7 20.0 %copy-start.30 = (f32[192,768]{1,0:T(8,128)}, f32[192,768]{1,0:T(8,128)S(1)}, u32[]{:S(2)}) copy-start(f32[192,768]{1,0:T(8,128)S(1)} %get-tuple-element.35.du1_ref) | copy-start | bytes 1769476
  34.7 1.6 %collective-permute-start.6 = (bf16[2,80,768]{2,1,0:T(8,128)(2,1)S(1)}, bf16[2,80,768]{2,1,0:T(8,128)(2,1)S(1)}, u32[]{:S(2)}, u32[]{:S(2)}) collective-permute-start(bf16[2,80,768]{2,1,0:T(8,128)(2,1)S(1)} %get-tuple-element.39), channel_id=1, source_target_pairs={{0,1},{1,0},{2,3},{3,2},{4,5},{5,4},{6,7},{7,6},{8,9},{9,8},{10,11... | collective-permute-start | bytes 737288 | tf_op jit(solution)/shard_map/ppermute | solution.py:583
  36.3 30.0 %copy-start.1 = (bf16[768,768]{1,0:T(8,128)(2,1)S(1)}, bf16[768,768]{1,0:T(8,128)(2,1)}, u32[]{:S(2)}) copy-start(bf16[768,768]{1,0:T(8,128)(2,1)} %wq_ref.3) | copy-start | bytes 3538948
  36.3 4.8 %collective-permute-start.7 = (bf16[80,768]{1,0:T(8,128)(2,1)S(1)}, bf16[80,768]{1,0:T(8,128)(2,1)S(1)}, u32[]{:S(2)}, u32[]{:S(2)}) collective-permute-start(bf16[80,768]{1,0:T(8,128)(2,1)S(1)} %slice_bitcast_fusion.2), channel_id=1, source_target_pairs={{0,2},{1,3},{2,0},{3,1},{4,6},{5,7},{6,4},{7,5},{8,10},{9,11},{10,... | collective-permute-start | bytes 368648 | tf_op jit(solution)/shard_map/ppermute | solution.py:583
  41.2 3.8 %collective-permute-start.8 = (bf16[80,768]{1,0:T(8,128)(2,1)S(1)}, bf16[80,768]{1,0:T(8,128)(2,1)S(1)}, u32[]{:S(2)}, u32[]{:S(2)}) collective-permute-start(bf16[80,768]{1,0:T(8,128)(2,1)S(1)} %fusion), channel_id=1, source_target_pairs={{0,4},{1,5},{2,6},{3,7},{4,0},{5,1},{6,2},{7,3},{8,12},{9,13},{10,... | collective-permute-start | bytes 368648 | tf_op jit(solution)/shard_map/ppermute | solution.py:583
  45.1 3.9 %collective-permute-start.9 = (bf16[80,768]{1,0:T(8,128)(2,1)S(1)}, bf16[80,768]{1,0:T(8,128)(2,1)S(1)}, u32[]{:S(2)}, u32[]{:S(2)}) collective-permute-start(bf16[80,768]{1,0:T(8,128)(2,1)S(1)} %add_convert_fusion.3), channel_id=1, source_target_pairs={{0,8},{1,9},{2,10},{3,11},{4,12},{5,13},{6,14},{7,15},{8,0},{9,1},... | collective-permute-start | bytes 368648 | tf_op jit(solution)/shard_map/ppermute | solution.py:583
  49.0 5.0 %collective-permute-start.10 = (bf16[80,768]{1,0:T(8,128)(2,1)S(1)}, bf16[80,768]{1,0:T(8,128)(2,1)S(1)}, u32[]{:S(2)}, u32[]{:S(2)}) collective-permute-start(bf16[80,768]{1,0:T(8,128)(2,1)S(1)} %add_convert_fusion.2), channel_id=1, source_target_pairs={{0,16},{1,17},{2,18},{3,19},{4,20},{5,21},{6,22},{7,23},{8,24},{9,... | collective-permute-start | bytes 368648 | tf_op jit(solution)/shard_map/ppermute | solution.py:583
  51.5 10.2 %collective-permute-start.4 = (bf16[224,768]{1,0:T(8,128)(2,1)S(1)}, bf16[224,768]{1,0:T(8,128)(2,1)S(1)}, u32[]{:S(2)}, u32[]{:S(2)}) collective-permute-start(bf16[224,768]{1,0:T(8,128)(2,1)S(1)} %get-tuple-element.31.pack_ref.own_ref), channel_id=1, source_target_pairs={{0,2},{1,3},{2,0},{3,1},{4,6},{5,7},{6,4},{7,5},{8,10},{9,11},{10,... | collective-permute-start | bytes 1032200 | tf_op jit(solution)/shard_map/ppermute | solution.py:580
  54.6 9.1 %collective-permute-start.11 = (bf16[80,768]{1,0:T(8,128)(2,1)}, bf16[80,768]{1,0:T(8,128)(2,1)}, u32[]{:S(2)}, u32[]{:S(2)}) collective-permute-start(bf16[80,768]{1,0:T(8,128)(2,1)} %add_convert_fusion.1), channel_id=1, source_target_pairs={{0,2},{1,3},{2,0},{3,1},{4,6},{5,7},{6,4},{7,5},{8,10},{9,11},{10,... | collective-permute-start | bytes 368648 | tf_op jit(solution)/shard_map/ppermute | solution.py:583
  57.0 20.3 %collective-permute-start.3 = (bf16[224,768]{1,0:T(8,128)(2,1)S(1)}, bf16[224,768]{1,0:T(8,128)(2,1)S(1)}, u32[]{:S(2)}, u32[]{:S(2)}) collective-permute-start(bf16[224,768]{1,0:T(8,128)(2,1)S(1)} %get-tuple-element.31.pack_ref.own_ref), channel_id=1, source_target_pairs={{0,1},{1,0},{2,3},{3,2},{4,5},{5,4},{6,7},{7,6},{8,9},{9,8},{10,11... | collective-permute-start | bytes 1032200 | tf_op jit(solution)/shard_map/ppermute | solution.py:580
  61.7 15.7 %collective-permute-start.5 = (bf16[224,768]{1,0:T(8,128)(2,1)S(1)}, bf16[224,768]{1,0:T(8,128)(2,1)S(1)}, u32[]{:S(2)}, u32[]{:S(2)}) collective-permute-start(bf16[224,768]{1,0:T(8,128)(2,1)S(1)} %collective-permute-done.4.far_ref), channel_id=1, source_target_pairs={{0,1},{1,0},{2,3},{3,2},{4,5},{5,4},{6,7},{7,6},{8,9},{9,8},{10,11... | collective-permute-start | bytes 1032200 | tf_op jit(solution)/shard_map/ppermute | solution.py:580
  64.8 18.5 %collective-permute-start.12 = (bf16[2,80,768]{2,1,0:T(8,128)(2,1)S(1)}, bf16[2,80,768]{2,1,0:T(8,128)(2,1)S(1)}, u32[]{:S(2)}, u32[]{:S(2)}) collective-permute-start(bf16[2,80,768]{2,1,0:T(8,128)(2,1)S(1)} %pad_maximum_fusion), channel_id=1, source_target_pairs={{0,1},{1,0},{2,3},{3,2},{4,5},{5,4},{6,7},{7,6},{8,9},{9,8},{10,11... | collective-permute-start | bytes 737288 | tf_op jit(solution)/shard_map/ppermute | solution.py:583
  71.8 5.6 %copy-start.3 = (bf16[768,768]{1,0:T(8,128)(2,1)S(1)}, bf16[768,768]{1,0:T(8,128)(2,1)}, u32[]{:S(2)}) copy-start(bf16[768,768]{1,0:T(8,128)(2,1)} %wk_ref.3) | copy-start | bytes 3538948
  71.8 5.6 %copy-start.5 = (bf16[768,768]{1,0:T(8,128)(2,1)S(1)}, bf16[768,768]{1,0:T(8,128)(2,1)}, u32[]{:S(2)}) copy-start(bf16[768,768]{1,0:T(8,128)(2,1)} %wv_ref.3) | copy-start | bytes 3538948
  (21 other events, 28.9 us)

commit v2 on v1

v2 whole, which is shorter than its diff:
```python
import functools

import jax
import jax.numpy as jnp
from jax import lax
from jax.experimental import pallas as pl
from jax.experimental.pallas import tpu as pltpu
from jax.sharding import PartitionSpec as P

HEAD = 64
GROUP = 4
LONG_AT = 128
LONG = 512
ROWS_A = 64
SHARE = 128
CHUNK = 512
SMALL = 8
ROWS_B = 128
NEG = -1e30
F32 = jnp.float32
BF16 = jnp.bfloat16

VMEM = pl.BlockSpec(memory_space=pltpu.VMEM)
SMEM = pl.BlockSpec(memory_space=pltpu.SMEM)
HBM = pl.BlockSpec(memory_space=pltpu.HBM)


def nn(left, right):
    return lax.dot_general(left, right, (((1,), (0,)), ((), ())), preferred_element_type=F32)


def nt(left, right):
    return lax.dot_general(left, right, (((1,), (1,)), ((), ())), preferred_element_type=F32)


def tn(left, right):
    return lax.dot_general(left, right, (((0,), (0,)), ((), ())), preferred_element_type=F32)


def gelu_both(values):
    size = jnp.abs(values) * 0.7071067811865476
    inv = 1.0 / (1.0 + 0.3275911 * size)
    bell = jnp.exp(-size * size)
    poly = inv * (
        0.254829592
        + inv * (-0.284496736 + inv * (1.421413741 + inv * (-1.453152027 + inv * 1.061405429)))
    )
    tail = 0.5 * poly * bell
    phi = jnp.where(values >= 0, 1.0 - tail, tail)
    return values * phi, phi + values * bell * 0.3989422804014327


def normed(values):
    centre = jnp.mean(values, axis=-1, keepdims=True)
    centred = values - centre
    spread = jnp.mean(centred * centred, axis=-1, keepdims=True)
    scale = lax.rsqrt(spread + 1e-06)
    return centred * scale, scale


def norm_back(incoming, gain, normal, scale):
    scaled = incoming * gain
    first = jnp.mean(scaled, axis=-1, keepdims=True)
    second = jnp.mean(scaled * normal, axis=-1, keepdims=True)
    return scale * (scaled - first - normal * second)


def row_of(ref):
    return ref[...].reshape(1, ref.shape[0])


def own_rows(block):
    return (
        pl.multiple_of(jnp.where(block == 0, 128, 0), 64),
        pl.multiple_of(jnp.where(block == 0, 0, 64), 64),
    )


def far_place(chip):
    return pl.multiple_of(LONG_AT + 2 * SHARE * (1 - chip), 128)


def far_tokens(core, far_ref, far_mate_ref):
    far, far_mate = far_ref[...], far_mate_ref[...]
    first = core == 0
    return jnp.concatenate(
        [jnp.where(first, far, far_mate), jnp.where(first, far_mate, far)], axis=0
    )


def partner_offset(block):
    return pl.multiple_of(jnp.where(block == 0, 0, jnp.where(block == 3, 256, 128)), 128)


def bounds(len_ref, valid_ref, places):
    low = jnp.zeros(places.shape, jnp.int32)
    high = jnp.zeros(places.shape, jnp.int32)
    start = jnp.int32(0)
    for slot in range(len_ref.shape[1]):
        end = start + len_ref[0, slot]
        inside = (places >= start) & (places < end)
        low = jnp.where(inside, start, low)
        high = jnp.where(inside, start + valid_ref[0, slot], high)
        start = end
    return low, high


def bias_of(len_ref, valid_ref, query_at, key_at, rows):
    places = query_at + lax.broadcasted_iota(jnp.int32, (rows, 1), 0)
    low, high = bounds(len_ref, valid_ref, places)
    keys = key_at + lax.broadcasted_iota(jnp.int32, (rows, LONG), 1)
    return jnp.where((keys >= low) & (keys < high), 0.0, NEG)


def bias_back_of(len_ref, valid_ref, key_at, query_at, rows):
    places = query_at + lax.broadcasted_iota(jnp.int32, (1, LONG), 1)
    low, high = bounds(len_ref, valid_ref, places)
    keys = key_at + lax.broadcasted_iota(jnp.int32, (rows, LONG), 0)
    return jnp.where((keys >= low) & (keys < high), 0.0, NEG)


def spread_heads(part):
    lane = lax.broadcasted_iota(jnp.int32, part.shape, 1) // HEAD
    return jnp.concatenate(
        [jnp.where(lane == head, part, jnp.zeros_like(part)) for head in range(GROUP)], axis=0
    )


def join_heads(stacked):
    rows = stacked.shape[0] // GROUP
    lane = lax.broadcasted_iota(jnp.int32, (rows, stacked.shape[1]), 1) // HEAD
    out = stacked[:rows]
    for head in range(1, GROUP):
        out = jnp.where(lane == head, stacked[head * rows : (head + 1) * rows], out)
    return out


def masked(scores, bias):
    split = scores.reshape((GROUP,) + bias.shape)
    return (split + bias).reshape(scores.shape)


def less_rows(stacked, rows):
    count = stacked.shape[0] // GROUP
    return jnp.concatenate(
        [stacked[head * count : (head + 1) * count] - rows[head : head + 1] for head in range(GROUP)],
        axis=0,
    )


def project_kernel(
    len_ref,
    valid_ref,
    own_hbm,
    mate_ref,
    wq_hbm,
    wk_hbm,
    wv_hbm,
    wout_hbm,
    winner_hbm,
    q_ref,
    k_ref,
    v_ref,
    bias_a_ref,
    bias_b_ref,
    back_a_ref,
    back_b_ref,
    wq_ref,
    wk_ref,
    wv_ref,
    wout_ref,
    winner_ref,
    own_ref,
    sems,
):
    moves = (
        (own_hbm, own_ref),
        (wq_hbm, wq_ref),
        (wk_hbm, wk_ref),
        (wv_hbm, wv_ref),
        (wout_hbm, wout_ref),
        (winner_hbm, winner_ref),
    )
    copies = [
        pltpu.make_async_copy(source, target, sems.at[index])
        for index, (source, target) in enumerate(moves)
    ]
    for copy in copies:
        copy.start()
    block = lax.axis_index("blk")
    core = block % 2
    rows = own_ref.shape[0]
    first = block * rows
    at_a, at_b = own_rows(block)
    meet_b = partner_offset(block)
    bias_a_ref[...] = bias_of(len_ref, valid_ref, first + at_a, LONG_AT, ROWS_A)
    bias_b_ref[...] = bias_of(len_ref, valid_ref, first + at_b, meet_b, ROWS_B)
    back_a_ref[...] = bias_back_of(len_ref, valid_ref, first + at_a, LONG_AT, ROWS_A)
    back_b_ref[...] = bias_back_of(len_ref, valid_ref, first + at_b, meet_b, ROWS_B)
    mine = pl.multiple_of(core * rows, rows)
    other = pl.multiple_of((1 - core) * rows, rows)
    copies[0].wait()
    both = jnp.concatenate([own_ref[...], mate_ref[...]], axis=0)
    for copy, weight, out, scale in (
        (copies[1], wq_ref, q_ref, 0.125),
        (copies[2], wk_ref, k_ref, 1.0),
        (copies[3], wv_ref, v_ref, 1.0),
    ):
        copy.wait()
        product = (nn(both, weight[...]) * scale).astype(BF16)
        out[pl.ds(mine, rows), :] = product[:rows]
        out[pl.ds(other, rows), :] = product[rows:]
    copies[4].wait()
    copies[5].wait()


def main_kernel(
    own_ref,
    far_ref,
    far_mate_ref,
    q_ref,
    kpair_ref,
    vpair_ref,
    bias_a_ref,
    bias_b_ref,
    cot_ref,
    down1_ref,
    dbias1_ref,
    up1_ref,
    ubias1_ref,
    gain1_ref,
    shift1_ref,
    down2_ref,
    dbias2_ref,
    up2_ref,
    ubias2_ref,
    gain2_ref,
    shift2_ref,
    wk_ref,
    wv_ref,
    wout_ref,
    winner_ref,
    wouter_hbm,
    mixed_hbm,
    kbuf,
    vbuf,
    lse_ref,
    du1_ref,
    pack_ref,
    keep_ref,
    send_ref,
    wouter_ref,
    slope_ref,
    mixed_ref,
    sems,
):
    hidden_units = winner_ref.shape[1]
    outer_copies = []
    for index in range(hidden_units // CHUNK):
        part = pl.ds(index * CHUNK, CHUNK)
        copy = pltpu.make_async_copy(wouter_hbm.at[part], wouter_ref.at[part], sems.at[1 + index])
        copy.start()
        outer_copies.append(copy)
    mixed_copy = pltpu.make_async_copy(mixed_ref, mixed_hbm, sems.at[0])
    block = lax.axis_index("blk")
    core = block % 2
    chip = block // 2
    rows, width = own_ref.shape
    at_a, at_b = own_rows(block)
    meet_b = partner_offset(block)

    def mine(ref):
        return jnp.concatenate([ref[pl.ds(at_a, ROWS_A), :], ref[pl.ds(at_b, ROWS_B), :]], axis=0)

    def put(ref, value):
        ref[pl.ds(at_a, ROWS_A), :] = value[:ROWS_A]
        ref[pl.ds(at_b, ROWS_B), :] = value[ROWS_A:]

    def natural(value):
        rolled = jnp.concatenate([value[:, ROWS_A:], value[:, :ROWS_A]], axis=1)
        return jnp.where(block == 0, rolled, value)

    near = pl.multiple_of(chip * 2 * rows, 2 * rows)
    kbuf[pl.ds(near, 2 * rows), :] = kpair_ref[...]
    vbuf[pl.ds(near, 2 * rows), :] = vpair_ref[...]
    far = far_tokens(core, far_ref, far_mate_ref)
    kbuf[pl.ds(far_place(chip), 2 * SHARE), :] = nn(far, wk_ref[...]).astype(BF16)
    vbuf[pl.ds(far_place(chip), 2 * SHARE), :] = nn(far, wv_ref[...]).astype(BF16)

    lane = lax.broadcasted_iota(jnp.int32, (1, 128), 1)
    attended_parts = []
    lse_parts = []
    for at, count, meet, bias_ref in (
        (at_a, ROWS_A, LONG_AT, bias_a_ref),
        (at_b, ROWS_B, meet_b, bias_b_ref),
    ):
        pieces = []
        lse = jnp.zeros((count, 128), F32)
        for group in range(width // (GROUP * HEAD)):
            columns = slice(group * GROUP * HEAD, (group + 1) * GROUP * HEAD)
            queries = spread_heads(q_ref[pl.ds(core * rows + at, count), columns])
            scores = masked(nt(queries, kbuf[pl.ds(meet, LONG), columns]), bias_ref[...])
            top = jnp.max(scores, axis=-1, keepdims=True)
            weights = jnp.exp(scores - top)
            total = jnp.sum(weights, axis=-1, keepdims=True)
            mixed_values = nn(weights.astype(BF16), vbuf[pl.ds(meet, LONG), columns])
            pieces.append(join_heads(mixed_values * (1.0 / total)))
            log_total = top + jnp.log(total)
            for head in range(GROUP):
                lse = jnp.where(
                    lane == group * GROUP + head, log_total[head * count : (head + 1) * count], lse
                )
        attended_parts.append(jnp.concatenate(pieces, axis=1))
        lse_parts.append(lse)
    attended_f = jnp.concatenate(attended_parts, axis=0)
    lse_own = jnp.concatenate(lse_parts, axis=0)
    put(lse_ref, lse_own)
    attended = attended_f.astype(BF16)
    branch = nn(attended, wout_ref[...]).astype(BF16)

    pre1 = nt(branch, down1_ref[...]) + row_of(dbias1_ref)
    inner1_f, slope1 = gelu_both(pre1)
    inner1 = inner1_f.astype(BF16)
    summed = (
        mine(own_ref).astype(F32) + branch.astype(F32) + nn(inner1, up1_ref[...]) + row_of(ubias1_ref)
    )
    normal1, scale1 = normed(summed)
    gain1 = row_of(gain1_ref)
    mid = (normal1 * gain1 + row_of(shift1_ref)).astype(BF16)

    ffn_f = jnp.zeros((rows, width), F32)
    for at in range(0, hidden_units, CHUNK):
        hidden_f, slope = gelu_both(nn(mid, winner_ref[:, at : at + CHUNK]))
        slope_ref[:, at : at + CHUNK] = slope
        outer_copies[at // CHUNK].wait()
        ffn_f = ffn_f + nn(hidden_f.astype(BF16), wouter_ref[at : at + CHUNK, :])
    ffn = ffn_f.astype(BF16)

    pre2 = nt(ffn, down2_ref[...]) + row_of(dbias2_ref)
    inner2_f, slope2 = gelu_both(pre2)
    inner2 = inner2_f.astype(BF16)
    summed = mid.astype(F32) + ffn.astype(F32) + nn(inner2, up2_ref[...]) + row_of(ubias2_ref)
    normal2, scale2 = normed(summed)
    gain2 = row_of(gain2_ref)
    put(mixed_ref, (normal2 * gain2 + row_of(shift2_ref)).astype(BF16))
    mixed_copy.start()

    cot = mine(cot_ref).astype(F32)
    grad_gain2 = jnp.sum(cot * normal2, axis=0, keepdims=True)
    grad_shift2 = jnp.sum(cot, axis=0, keepdims=True)
    du2 = norm_back(cot, gain2, normal2, scale2)

    def adapter_back(source, down, up, inner, slope, incoming):
        out_grad = incoming.astype(BF16)
        grad_up = tn(inner, out_grad)
        grad_ubias = jnp.sum(out_grad.astype(F32), axis=0, keepdims=True)
        grad_pre = (nt(out_grad, up) * slope).astype(BF16)
        grad_down = tn(grad_pre, source)
        grad_dbias = jnp.sum(grad_pre.astype(F32), axis=0, keepdims=True)
        return nn(grad_pre, down), grad_down, grad_dbias, grad_up, grad_ubias

    back2, grad_down2, grad_dbias2, grad_up2, grad_ubias2 = adapter_back(
        ffn, down2_ref[...], up2_ref[...], inner2, slope2, du2
    )
    dffn = (du2 + back2).astype(BF16)
    dmid = du2
    for at in range(0, hidden_units, CHUNK):
        dhidden = (nt(dffn, wouter_ref[at : at + CHUNK, :]) * slope_ref[:, at : at + CHUNK]).astype(
            BF16
        )
        dmid = dmid + nt(dhidden, winner_ref[:, at : at + CHUNK])

    grad_gain1 = jnp.sum(dmid * normal1, axis=0, keepdims=True)
    grad_shift1 = jnp.sum(dmid, axis=0, keepdims=True)
    du1 = norm_back(dmid, gain1, normal1, scale1)
    back1, grad_down1, grad_dbias1, grad_up1, grad_ubias1 = adapter_back(
        branch, down1_ref[...], up1_ref[...], inner1, slope1, du1
    )
    put(du1_ref, du1)

    blank = jnp.zeros((1, width), F32)
    both_dbias = jnp.concatenate(
        [
            grad_dbias1,
            jnp.zeros((1, 128 - grad_dbias1.shape[1]), F32),
            grad_dbias2,
            jnp.zeros((1, width - 128 - grad_dbias2.shape[1]), F32),
        ],
        axis=1,
    )
    quarters = (
        (grad_up1, grad_ubias1, both_dbias),
        (grad_down1, grad_gain1, grad_shift1),
        (grad_up2, grad_ubias2, blank),
        (grad_down2, grad_gain2, grad_shift2),
    )
    for index, (matrix, one, two) in enumerate(quarters):
        small = jnp.concatenate([one, two, jnp.zeros((SMALL - 2, width), F32)], axis=0)
        whole = jnp.concatenate([matrix, small], axis=0).astype(BF16)
        place = jnp.where(chip == index // 2, 0, 1)

        @pl.when(core == index % 2)
        def _(place=place, whole=whole):
            keep_ref[place] = whole

        @pl.when(core != index % 2)
        def _(place=place, whole=whole):
            send_ref[place] = whole

    dbranch = (du1 + back1).astype(BF16)
    dattended = nt(dbranch, wout_ref[...]).astype(BF16)
    put(pack_ref, dattended)
    product = dattended.astype(F32) * attended_f
    product_hi = product.astype(BF16)
    product_lo = (product - product_hi.astype(F32)).astype(BF16)
    head_of = lax.broadcasted_iota(jnp.int32, (16, width), 1) // HEAD
    picks = (head_of == lax.broadcasted_iota(jnp.int32, (16, width), 0)).astype(BF16)
    delta = natural(nt(picks, product_hi) + nt(picks, product_lo))
    lse_rows = natural(
        jnp.transpose(jnp.concatenate([lse_own, jnp.zeros((256 - rows, 128), F32)], axis=0))[
            :16, :rows
        ]
    )

    def pieces_of(value, count):
        out = []
        for _ in range(count):
            piece = value.astype(BF16)
            value = value - piece.astype(F32)
            out.append(jnp.concatenate([piece, jnp.zeros((16, 256 - rows), BF16)], axis=1))
        return out

    pack_ref[rows : rows + 16, :] = jnp.concatenate(pieces_of(lse_rows, 3), axis=1)
    pack_ref[rows + 16 : rows + 32, :] = jnp.concatenate(
        pieces_of(delta, 2) + [jnp.zeros((16, 256), BF16)], axis=1
    )
    mixed_copy.wait()


def query_back_kernel(
    group,
    far_ref,
    far_mate_ref,
    q_ref,
    kbuf,
    vbuf,
    bias_a_ref,
    bias_b_ref,
    lse_ref,
    pack_ref,
    part_in_ref,
    wq_ref,
    qbuf,
    part_ref,
):
    block = lax.axis_index("blk")
    rows = q_ref.shape[0] // 2
    core, chip = block % 2, block // 2
    at_a, at_b = own_rows(block)
    meet_b = partner_offset(block)
    columns = slice(group * GROUP * HEAD, (group + 1) * GROUP * HEAD)
    wq = wq_ref[:, columns]
    queries_far = (nn(far_tokens(core, far_ref, far_mate_ref), wq) * 0.125).astype(BF16)
    qbuf[pl.ds(pl.multiple_of(chip * 2 * rows, rows), 2 * rows), :] = q_ref[:, columns]
    qbuf[pl.ds(far_place(chip), 2 * SHARE), :] = queries_far
    lane = lax.broadcasted_iota(jnp.int32, (1, 128), 1)
    for at, count, meet, bias_ref in (
        (at_a, ROWS_A, LONG_AT, bias_a_ref),
        (at_b, ROWS_B, meet_b, bias_b_ref),
    ):
        lse = lse_ref[pl.ds(at, count), :]
        log_total = jnp.concatenate(
            [
                jnp.sum(jnp.where(lane == group * GROUP + head, lse, 0.0), axis=-1, keepdims=True)
                for head in range(GROUP)
            ],
            axis=0,
        )
        keys = kbuf[pl.ds(meet, LONG), columns]
        scores = nt(spread_heads(q_ref[pl.ds(core * rows + at, count), columns]), keys)
        scores = masked(scores, bias_ref[...])
        probs = jnp.exp(scores - log_total)
        dprobs = nt(
            spread_heads(pack_ref[pl.ds(at, count), columns]), vbuf[pl.ds(meet, LONG), columns]
        )
        delta = jnp.sum(probs * dprobs, axis=-1, keepdims=True)
        dscores = (probs * (dprobs - delta)).astype(BF16)
        dquery = join_heads(nn(dscores, keys)).astype(BF16)
        part_ref[pl.ds(at, count), :] = part_in_ref[pl.ds(at, count), :] + nt(dquery, wq) * 0.125


def key_back_kernel(
    group,
    own_ref,
    mate_ref,
    far_ref,
    far_mate_ref,
    qbuf,
    kbuf,
    vbuf,
    back_a_ref,
    back_b_ref,
    part_ref,
    wk_ref,
    wv_ref,
    out_ref,
    abuf,
):
    block = lax.axis_index("blk")
    rows, width = out_ref.shape
    core, chip = block % 2, block // 2
    at_a, at_b = own_rows(block)
    meet_b = partner_offset(block)
    first = block * rows
    columns = slice(group * GROUP * HEAD, (group + 1) * GROUP * HEAD)
    abuf[pl.ds(pl.multiple_of(first, rows), rows), :] = own_ref[:rows, columns]
    abuf[pl.ds(pl.multiple_of((block ^ 1) * rows, rows), rows), :] = mate_ref[:rows, columns]
    far_at = far_place(chip)
    far_first = pl.multiple_of(far_at + SHARE * core, 128)
    far_second = pl.multiple_of(far_at + SHARE * (1 - core), 128)
    abuf[pl.ds(far_first, SHARE), :] = far_ref[:SHARE, columns]
    abuf[pl.ds(far_second, SHARE), :] = far_mate_ref[:SHARE, columns]
    stats = []
    for ref, at in ((own_ref, rows), (mate_ref, rows), (far_ref, SHARE), (far_mate_ref, SHARE)):
        lse = ref[at : at + 16, :].astype(F32)
        delta = ref[at + 16 : at + 32, :].astype(F32)
        stats.append(
            (
                (lse[:, :256] + (lse[:, 256:512] + lse[:, 512:]))[:, :rows],
                (delta[:, :256] + delta[:, 256:512])[:, :rows],
            )
        )

    def in_order(which):
        ordered = []
        for place in range(4):
            pick = stats[place][which]
            for index in range(4):
                pick = jnp.where(block ^ index == place, stats[index][which], pick)
            ordered.append(pick)
        return jnp.concatenate(ordered, axis=1)

    lse_all, delta_all = in_order(0), in_order(1)

    def window(stat, meet):
        stat = stat[group * GROUP : (group + 1) * GROUP]
        if isinstance(meet, int):
            return stat[:, meet : meet + LONG]
        here = stat[:, :LONG]
        for start in (128, 256):
            here = jnp.where(meet == start, stat[:, start : start + LONG], here)
        return here

    for at, count, meet, bias_ref in (
        (at_a, ROWS_A, LONG_AT, back_a_ref),
        (at_b, ROWS_B, meet_b, back_b_ref),
    ):
        queries = qbuf[pl.ds(meet, LONG), :]
        grads = abuf[pl.ds(meet, LONG), :]
        own_at = pl.multiple_of(first + at, 64)
        scores = nt(spread_heads(kbuf[pl.ds(own_at, count), columns]), queries)
        scores = masked(scores, bias_ref[...])
        probs = jnp.exp(less_rows(scores, window(lse_all, meet)))
        dprobs = nt(spread_heads(vbuf[pl.ds(own_at, count), columns]), grads)
        dscores = (probs * less_rows(dprobs, window(delta_all, meet))).astype(BF16)
        dkey = join_heads(nn(dscores, queries)).astype(BF16)
        dvalue = join_heads(nn(probs.astype(BF16), grads)).astype(BF16)
        out_ref[pl.ds(at, count), :] = (
            part_ref[pl.ds(at, count), :]
            + nt(dkey, wk_ref[:, columns])
            + nt(dvalue, wv_ref[:, columns])
        ).astype(out_ref.dtype)


def unpack_kernel(*refs):
    parts, outs = refs[:4], refs[4:]
    block = lax.axis_index("blk")
    core, chip = block % 2, block // 2
    adapt = outs[0].shape[0]
    matrices = (outs[2], outs[0], outs[8], outs[6])
    vectors = ((outs[3], None), (outs[4], outs[5]), (outs[9], None), (outs[10], outs[11]))
    for index in range(4):
        place = (core ^ (index % 2)) + 2 * (chip ^ (index // 2))
        for at, part in enumerate(parts):

            @pl.when(place == at)
            def _(index=index, part=part):
                matrices[index][...] = part[:adapt, :].astype(F32)
                small = part[adapt : adapt + SMALL, :].astype(F32)
                one, two = vectors[index]
                one[...] = small[0]
                if two is not None:
                    two[...] = small[1]
                if index == 0:
                    outs[1][...] = small[1, :adapt]
                    outs[7][...] = small[1, 128 : 128 + adapt]


def params(megabytes):
    return pltpu.CompilerParams(vmem_limit_bytes=megabytes << 20)


def cost(gigaflop, megabytes):
    return pl.CostEstimate(
        flops=int(gigaflop * 1e9), bytes_accessed=int(megabytes * 1e6), transcendentals=0
    )


def after(array, *others):
    return lax.optimization_barrier((array,) + others)[0]


def vmem(dims, dtype):
    return pltpu.VMEM(dims, dtype)


def in_hbm(array):
    return pltpu.with_memory_space_constraint(array, pltpu.HBM)


def shape(dims, dtype):
    return jax.ShapeDtypeStruct(dims, dtype)


def body(
    dp_size,
    tokens,
    w_query,
    w_key,
    w_value,
    w_out,
    w_inner,
    w_outer,
    down_one,
    dbias_one,
    up_one,
    ubias_one,
    gain_one,
    shift_one,
    down_two,
    dbias_two,
    up_two,
    ubias_two,
    gain_two,
    shift_two,
    seg_len,
    seg_valid,
    cotangent,
):
    rows, _, width = tokens.shape
    adapt = up_one.shape[0]
    hidden = w_inner.shape[1]
    block = lax.axis_index("blk")
    own = tokens.reshape(rows, width)
    cot = cotangent.reshape(rows, width)

    def swap(array, mask):
        return lax.ppermute(array, "blk", [(i, i ^ mask) for i in range(4)])

    def swap_all(array, mask):
        return lax.ppermute(
            array, ("dp", "blk"), [(i, i ^ mask) for i in range(4 * dp_size)]
        )

    mate = swap(own, 1)
    def near_share(own, mate):
        choices = (
            (own[128:192], own[64:128], own[:64], mate[128:192]),
            (mate[:64], own[128:192], own[64:128], own[:64]),
        )
        halves = []
        for options in choices:
            half = options[0]
            for index in range(1, 4):
                half = jnp.where(block == index, options[index], half)
            halves.append(half)
        return halves

    far = swap(jnp.concatenate(near_share(own, mate), axis=0), 2)
    mask_shapes = [vmem((count, LONG), F32) for count in (ROWS_A, ROWS_B)] * 2
    (
        q,
        kpair,
        vpair,
        bias_a,
        bias_b,
        back_a,
        back_b,
        wq_here,
        wk_here,
        wv_here,
        wout_here,
        winner_here,
    ) = pl.pallas_call(
        project_kernel,
        in_specs=[SMEM] * 2 + [HBM, VMEM] + [HBM] * 5,
        out_specs=[VMEM] * 12,
        out_shape=[vmem((2 * rows, width), BF16)] * 3
        + mask_shapes
        + [vmem((width, width), BF16)] * 4
        + [vmem((width, hidden), BF16)],
        scratch_shapes=[pltpu.VMEM((rows, width), BF16), pltpu.SemaphoreType.DMA((6,))],
        compiler_params=params(4),
        cost_estimate=cost(2.0, 12.0),
        name="project",
    )(
        in_hbm(seg_len),
        in_hbm(seg_valid),
        in_hbm(own),
        mate,
        in_hbm(w_query),
        in_hbm(w_key),
        in_hbm(w_value),
        in_hbm(w_out),
        in_hbm(w_inner),
    )
    far_mate = swap(after(far, q), 1)

    part_rows = adapt + SMALL
    mixed, kbuf, vbuf, lse, du1, pack, keep, send = pl.pallas_call(
        main_kernel,
        in_specs=[VMEM] * 25 + [HBM],
        out_specs=[HBM] + [VMEM] * 7,
        out_shape=[
            shape((rows, width), BF16),
            vmem((4 * rows, width), BF16),
            vmem((4 * rows, width), BF16),
            vmem((rows, 128), F32),
            vmem((rows, width), F32),
            vmem((rows + 32, width), BF16),
            vmem((2, part_rows, width), BF16),
            vmem((2, part_rows, width), BF16),
        ],
        scratch_shapes=[
            pltpu.VMEM((hidden, width), BF16),
            pltpu.VMEM((rows, hidden), F32),
            pltpu.VMEM((rows, width), BF16),
            pltpu.SemaphoreType.DMA((1 + hidden // CHUNK,)),
        ],
        compiler_params=params(13),
        cost_estimate=cost(8.0, 20.0),
        name="layer",
    )(
        own,
        far,
        far_mate,
        q,
        kpair,
        vpair,
        bias_a,
        bias_b,
        cot,
        down_one.T,
        dbias_one,
        up_one,
        ubias_one,
        gain_one,
        shift_one,
        down_two.T,
        dbias_two,
        up_two,
        ubias_two,
        gain_two,
        shift_two,
        wk_here,
        wv_here,
        wout_here,
        winner_here,
        in_hbm(w_outer),
    )

    def add(left, right):
        return (left.astype(F32) + right.astype(F32)).astype(BF16)

    def query_back(group, part, pack_now):
        return pl.pallas_call(
            functools.partial(query_back_kernel, group),
            in_specs=[VMEM] * 11,
            out_specs=[VMEM] * 2,
            out_shape=[vmem((4 * rows, GROUP * HEAD), BF16), vmem((rows, width), F32)],
            compiler_params=params(4),
            cost_estimate=cost(1.0, 3.0),
            name=f"query_back_{group}",
        )(far, far_mate, q, kbuf, vbuf, bias_a, bias_b, lse, pack_now, part, wq_here)

    def key_back(group, qbuf, part):
        return pl.pallas_call(
            functools.partial(key_back_kernel, group),
            in_specs=[VMEM] * 12,
            out_specs=VMEM,
            out_shape=vmem((rows, width), F32) if group < 2 else shape((rows, width), BF16),
            scratch_shapes=[pltpu.VMEM((4 * rows, GROUP * HEAD), BF16)],
            compiler_params=params(4),
            cost_estimate=cost(1.0, 3.0),
            name=f"key_back_{group}",
        )(
            pack,
            pack_mate,
            pack_far,
            pack_far_mate,
            qbuf,
            kbuf,
            vbuf,
            back_a,
            back_b,
            part,
            wk_here,
            wv_here,
        )

    pack_mate = swap(pack, 1)
    total = add(keep, swap_all(send, 1))
    pack_now, pack_mate, total = lax.optimization_barrier((pack, pack_mate, total))
    share = near_share(pack_now, pack_mate) + [pack_now[rows:]]
    pack_far = swap(jnp.concatenate(share, axis=0), 2)
    arrived = swap_all(total[1], 2)
    qbuf0, part = query_back(0, du1, pack_now)
    total = add(total[0], after(arrived, part))
    arrived = swap_all(total, 4)
    qbuf1, part = query_back(1, after(part, total), pack_now)
    pack_far, part = lax.optimization_barrier((pack_far, part))
    pack_far_mate = swap(pack_far, 1)
    total = add(total, after(arrived, part))
    masks = []
    while 8 << len(masks) < 4 * dp_size:
        masks.append(8 << len(masks))
    arrived = swap_all(total, masks[0])
    qbuf2, part = query_back(2, after(part, total), pack_now)
    total = add(total, after(arrived, part))
    arrived = swap_all(total, masks[1])
    part = key_back(0, qbuf0, after(part, total))
    part = key_back(1, qbuf1, part)
    total = add(total, after(arrived, part))
    for mask in masks[2:]:
        total = add(total, swap_all(total, mask))
    across = swap_all(total, 2)
    input_grad = key_back(2, qbuf2, after(part, total))
    other_half = swap_all(after(jnp.stack([total, across]), input_grad), 1)

    grads = pl.pallas_call(
        unpack_kernel,
        in_specs=[VMEM] * 4,
        out_specs=[VMEM] * 12,
        out_shape=[
            shape(dims, F32)
            for dims in (
                ((adapt, width), (adapt,), (adapt, width), (width,), (width,), (width,)) * 2
            )
        ],
        compiler_params=params(4),
        name="unpack",
    )(total, other_half[0], across, other_half[1])
    return (mixed.reshape(tokens.shape), input_grad.reshape(tokens.shape)) + tuple(
        grad.T if index in (0, 6) else grad for index, grad in enumerate(grads)
    )


def solution(mesh):
    in_specs = (
        (P("blk", "dp", None),) + (P(),) * 18 + (P("dp", None),) * 2 + (P("blk", "dp", None),)
    )
    out_specs = (P("blk", "dp", None),) * 2 + (P(),) * 12
    return jax.shard_map(
        functools.partial(body, mesh.shape["dp"]),
        mesh=mesh,
        in_specs=in_specs,
        out_specs=out_specs,
        check_vma=False,
    )
```

time: 88.7 us -> 62.4 us (0.70)
  local copies, waits for them, and re-layouts: 14.4 us -> 0.12 us
  starting transfers between devices: 23.4 us -> 15.9 us
  waiting for transfers between devices: 16.6 us -> 10.4 us
  Pallas kernels: 29.9 us -> 33.2 us
  other arithmetic: 2.87 us -> 1.28 us
    unnamed x64 -> x28, local copies, waits for them, and re-layouts: 10.4 us -> 0.09 us
    ppermute x6, starting transfers between devices: 12.2 us -> 5.37 us  [swap(): return lax.ppermute(array, 'blk', [(i, i ^ mask) for i in range(4)])]
    ppermute x7, waiting for transfers between devices: 10.6 us -> 5.06 us  [swap_all(): lax.ppermute(array, ('dp', 'blk'), [(i, i ^ mask) for i in range(4 * dp_s...]
    pallas_call x4 -> x9, Pallas kernels: 29.9 us -> 33.2 us  [the longest x1 15.7 us: body(): pl.pallas_call(main_kernel, in_specs=[VMEM] * 25 + [HBM], out_specs=[HBM]...]
    slice x4 -> x1, local copies, waits for them, and re-layouts: 2.62 us -> 0.01 us  [body(): share = near_share(pack_now, pack_mate) + [pack_now[rows:]]]
    select_n x0 -> x2, other arithmetic: none -> 1.04 us  [near_share(): half = jnp.where(block == index, options[index], half)]
    convert_element_type x1 -> x0, other arithmetic: 1.04 us -> none  [quarter(): return jnp.where(core == index % 2, same, flipped).astype(F32)]
    another operation x1, other arithmetic: 0.99 us -> 0.02 us  [body(): other_half = swap_all(after(jnp.stack([total, across]), input_grad), 1)]
  transfers between devices with their start and end apart: 13 -> 13, of which waited for: 6 -> 10; matrix products, arithmetic and copies ran while one was open for 2% -> 0% of each run, Pallas kernels for 14% -> 27%
where the time goes in v2:
time: 62.4 us; the launch traced here: 61.9 us
  Pallas kernels  33.2 us (53%)
  starting transfers between devices  15.9 us (25%)
  waiting for transfers between devices  10.4 us (17%)
  other arithmetic  1.28 us (2%)
  between operations  0.99 us (2%)
    pallas_call x1, Pallas kernels, body(): pl.pallas_call(main_kernel, in_specs=[VMEM] * 25 + [HBM], out_specs=[HBM]...  15.7 us
    ppermute x7, starting transfers between devices, swap_all(): lax.ppermute(array, ('dp', 'blk'), [(i, i ^ mask) for i in range(4 * dp_s...  10.5 us
    pallas_call x3, Pallas kernels, query_back(): pl.pallas_call(functools.partial(query_back_kernel, group), in_specs=[VME...  6.05 us
    pallas_call x3, Pallas kernels, key_back(): pl.pallas_call(functools.partial(key_back_kernel, group), in_specs=[VMEM]...  5.82 us
    ppermute x6, starting transfers between devices, swap(): return lax.ppermute(array, 'blk', [(i, i ^ mask) for i in range(4)])  5.37 us
    ppermute x6, waiting for transfers between devices, swap(): return lax.ppermute(array, 'blk', [(i, i ^ mask) for i in range(4)])  5.34 us
    ppermute x7, waiting for transfers between devices, swap_all(): lax.ppermute(array, ('dp', 'blk'), [(i, i ^ mask) for i in range(4 * dp_s...  5.06 us
    pallas_call x1, Pallas kernels, body(): pl.pallas_call(project_kernel, in_specs=[SMEM] * 2 + [HBM, VMEM] + [HBM]...  4.59 us
  transfers between devices with their start and end apart: 13, of which 10 were waited for; matrix products, arithmetic and copies ran while one was open for 0% of the time, Pallas kernels for 27%

profile of v2, /device:TPU:1, one launch (start us, length us, event | category | flops | bytes accessed | tf_op | source)
XLA Modules:
  0.0 61.9 jit_solution(199707701090862320)
XLA Ops:
  0.8 1.7 %collective-permute-done.mate_ref = bf16[192,768]{1,0:T(8,128)(2,1)S(1)} collective-permute-done((bf16[192,768]{1,0:T(8,128)(2,1)}, bf16[192,768]{1,0:T(8,128)(2,1)S(1)}, u32[]{:S(2)}, u32[]{:S(2)}) %collective-permute-start) | collective-permute-done | bytes 294944 | tf_op jit(solution)/shard_map/ppermute | solution.py:658
  2.5 1.0 %slice_select_fusion.1 = (bf16[64,768]{1,0:T(8,128)(2,1)S(1)}, bf16[64,768]{1,0:T(8,128)(2,1)S(1)}) fusion(bf16[192,768]{1,0:T(8,128)(2,1)S(1)} %collective-permute-done.mate_ref, pred[]{:T(512)S(6)} %eq.8, pred[]{:T(512)S(6)} %eq.7, pred[]{:T(512)S(6)} %eq.6, bf16[192,1,768]{2,0,1:T(8,128)(2,1)} %param.22), kind=kLoop, calls=%fused_computation.15 | loop fusion | flops 294912 | bytes 688131 | tf_op jit(solution)/shard_map/jit(_where)/select_n | solution.py:675
  3.7 2.4 %collective-permute-start.1 = (bf16[128,768]{1,0:T(8,128)(2,1)S(1)}, bf16[128,768]{1,0:T(8,128)(2,1)S(1)}, u32[]{:S(2)}, u32[]{:S(2)}) collective-permute-start(bf16[128,768]{1,0:T(8,128)(2,1)S(1)} %pad_maximum_fusion.2), channel_id=1, source_target_pairs={{0,2},{1,3},{2,0},{3,1},{4,6},{5,7},{6,4},{7,5},{8,10},{9,11},{10,... | collective-permute-start | bytes 589832 | tf_op jit(solution)/shard_map/ppermute | solution.py:658
  6.1 4.6 %project.1 = (bf16[384,768]{1,0:T(8,128)(2,1)S(1)}, bf16[384,768]{1,0:T(8,128)(2,1)S(1)}, bf16[384,768]{1,0:T(8,128)(2,1)S(1)}, f32[64,512]{1,0:T(8,128)S(1)}, f...) custom-call(s32[1,6]{1,0:T(1,128)} %len_ref.1, ...), custom_call_target="tpu_custom_call" | custom-call | flops 2000000000 | bytes 12000000 | tf_op jit(solution)/shard_map/project/pallas_call | solution.py:694
  12.0 1.1 %collective-permute-done.2.far_mate_ref = bf16[128,768]{1,0:T(8,128)(2,1)S(1)} collective-permute-done((bf16[128,768]{1,0:T(8,128)(2,1)S(1)}, bf16[128,768]{1,0:T(8,128)(2,1)S(1)}, u32[]{:S(2)}, u32[]{:S(2)}) %collective-permute-start.2) | collective-permute-done | bytes 196640 | tf_op jit(solution)/shard_map/ppermute | solution.py:658
  13.2 15.7 %layer.1 = (bf16[192,768]{1,0:T(8,128)(2,1)}, bf16[768,768]{1,0:T(8,128)(2,1)S(1)}, bf16[768,768]{1,0:T(8,128)(2,1)S(1)}, f32[192,128]{1,0:T(8,128)S(1)}, f32[19...) custom-call(bf16[192,768]{1,0:T(8,128)(2,1)S(1)} %bitcast.34, ...), custom_call_target="tpu_custom_call" | custom-call | flops 8000000000 | bytes 20000000 | tf_op jit(solution)/shard_map/layer/pallas_call | solution.py:720
  29.5 1.0 %collective-permute-done.4 = bf16[2,72,768]{2,1,0:T(8,128)(2,1)S(1)} collective-permute-done((bf16[2,72,768]{2,1,0:T(8,128)(2,1)S(1)}, bf16[2,72,768]{2,1,0:T(8,128)(2,1)S(1)}, u32[]{:S(2)}, u32[]{:S(2)}) %collective-permute-start.4) | collective-permute-done | bytes 221216 | tf_op jit(solution)/shard_map/ppermute | solution.py:661
  31.0 1.5 %collective-permute-start.6 = (bf16[72,768]{1,0:T(8,128)(2,1)S(1)}, bf16[72,768]{1,0:T(8,128)(2,1)S(1)}, u32[]{:S(2)}, u32[]{:S(2)}) collective-permute-start(bf16[72,768]{1,0:T(8,128)(2,1)S(1)} %slice_bitcast_fusion.2), channel_id=1, source_target_pairs={{0,2},{1,3},{2,0},{3,1},{4,6},{5,7},{6,4},{7,5},{8,10},{9,11},{10,... | collective-permute-start | bytes 331784 | tf_op jit(solution)/shard_map/ppermute | solution.py:661
  32.7 2.0 %query_back_0.1 = (bf16[768,256]{1,0:T(8,128)(2,1)S(1)}, f32[192,768]{1,0:T(8,128)S(1)}) custom-call(bf16[128,768]{1,0:T(8,128)(2,1)S(1)} %collective-permute-done.1.far_ref, bf16[128,768]{1,0:T(8,128)(2,1)S(1)} %collective-permute-done.2.far_mate_ref, bf16[384,768]{1,0:T(8,128)(2,1)S(1)} %get-tuple-element.67.q_ref, ...), custom_call_target="tpu_custom_call" | custom-call | flops 1000000000 | bytes 3000000 | tf_op jit(solution)/shard_map/query_back_0/pallas_call | solution.py:776
  35.4 1.5 %collective-permute-start.8 = (bf16[72,768]{1,0:T(8,128)(2,1)S(1)}, bf16[72,768]{1,0:T(8,128)(2,1)S(1)}, u32[]{:S(2)}, u32[]{:S(2)}) collective-permute-start(bf16[72,768]{1,0:T(8,128)(2,1)S(1)} %fusion), channel_id=1, source_target_pairs={{0,4},{1,5},{2,6},{3,7},{4,0},{5,1},{6,2},{7,3},{8,12},{9,13},{10,... | collective-permute-start | bytes 331784 | tf_op jit(solution)/shard_map/ppermute | solution.py:661
  37.0 2.0 %query_back_1.1 = (bf16[768,256]{1,0:T(8,128)(2,1)S(1)}, f32[192,768]{1,0:T(8,128)S(1)}) custom-call(bf16[128,768]{1,0:T(8,128)(2,1)S(1)} %collective-permute-done.1.far_ref, bf16[128,768]{1,0:T(8,128)(2,1)S(1)} %collective-permute-done.2.far_mate_ref, bf16[384,768]{1,0:T(8,128)(2,1)S(1)} %get-tuple-element.67.q_ref, ...), custom_call_target="tpu_custom_call" | custom-call | flops 1000000000 | bytes 3000000 | tf_op jit(solution)/shard_map/query_back_1/pallas_call | solution.py:776
  39.0 1.7 %collective-permute-done.5.far_ref = bf16[160,768]{1,0:T(8,128)(2,1)S(1)} collective-permute-done((bf16[160,768]{1,0:T(8,128)(2,1)S(1)}, bf16[160,768]{1,0:T(8,128)(2,1)S(1)}, u32[]{:S(2)}, u32[]{:S(2)}) %collective-permute-start.5) | collective-permute-done | bytes 245792 | tf_op jit(solution)/shard_map/ppermute | solution.py:658
  40.7 1.6 %collective-permute-start.9 = (bf16[72,768]{1,0:T(8,128)(2,1)S(1)}, bf16[72,768]{1,0:T(8,128)(2,1)S(1)}, u32[]{:S(2)}, u32[]{:S(2)}) collective-permute-start(bf16[72,768]{1,0:T(8,128)(2,1)S(1)} %add_convert_fusion.3), channel_id=1, source_target_pairs={{0,8},{1,9},{2,10},{3,11},{4,12},{5,13},{6,14},{7,15},{8,0},{9,1},... | collective-permute-start | bytes 331784 | tf_op jit(solution)/shard_map/ppermute | solution.py:661
  42.3 1.7 %collective-permute-start.7 = (bf16[160,768]{1,0:T(8,128)(2,1)S(1)}, bf16[160,768]{1,0:T(8,128)(2,1)S(1)}, u32[]{:S(2)}, u32[]{:S(2)}) collective-permute-start(bf16[160,768]{1,0:T(8,128)(2,1)S(1)} %collective-permute-done.5.far_ref), channel_id=1, source_target_pairs={{0,1},{1,0},{2,3},{3,2},{4,5},{5,4},{6,7},{7,6},{8,9},{9,8},{10,11... | collective-permute-start | bytes 737288 | tf_op jit(solution)/shard_map/ppermute | solution.py:658
  44.1 2.0 %query_back_2.1 = (bf16[768,256]{1,0:T(8,128)(2,1)S(1)}, f32[192,768]{1,0:T(8,128)S(1)}) custom-call(bf16[128,768]{1,0:T(8,128)(2,1)S(1)} %collective-permute-done.1.far_ref, bf16[128,768]{1,0:T(8,128)(2,1)S(1)} %collective-permute-done.2.far_mate_ref, bf16[384,768]{1,0:T(8,128)(2,1)S(1)} %get-tuple-element.67.q_ref, ...), custom_call_target="tpu_custom_call" | custom-call | flops 1000000000 | bytes 3000000 | tf_op jit(solution)/shard_map/query_back_2/pallas_call | solution.py:776
  46.1 2.4 %collective-permute-start.10 = (bf16[72,768]{1,0:T(8,128)(2,1)S(1)}, bf16[72,768]{1,0:T(8,128)(2,1)S(1)}, u32[]{:S(2)}, u32[]{:S(2)}) collective-permute-start(bf16[72,768]{1,0:T(8,128)(2,1)S(1)} %add_convert_fusion.2), channel_id=1, source_target_pairs={{0,16},{1,17},{2,18},{3,19},{4,20},{5,21},{6,22},{7,23},{8,24},{9,... | collective-permute-start | bytes 331784 | tf_op jit(solution)/shard_map/ppermute | solution.py:661
  48.5 1.7 %key_back_0.1.part_ref = f32[192,768]{1,0:T(8,128)S(1)} custom-call(bf16[224,768]{1,0:T(8,128)(2,1)S(1)} %get-tuple-element.82.pack_ref.own_ref, bf16[224,768]{1,0:T(8,128)(2,1)S(1)} %collective-permute-done.3.mate_ref, bf16[160,768]{1,0:T(8,128)(2,1)S(1)} %collective-permute-done.5.far_ref, bf16[160,768]{1,0:T(8,128)(2,1)S(1)} %collective-permute-done.7.far_mate_ref, ...), custom_call_target="tpu_custom_call" | custom-call | flops 1000000000 | bytes 3000000 | tf_op jit(solution)/shard_map/key_back_0/pallas_call | solution.py:787
  50.2 1.7 %key_back_1.1.part_ref = f32[192,768]{1,0:T(8,128)S(1)} custom-call(bf16[224,768]{1,0:T(8,128)(2,1)S(1)} %get-tuple-element.82.pack_ref.own_ref, bf16[224,768]{1,0:T(8,128)(2,1)S(1)} %collective-permute-done.3.mate_ref, bf16[160,768]{1,0:T(8,128)(2,1)S(1)} %collective-permute-done.5.far_ref, bf16[160,768]{1,0:T(8,128)(2,1)S(1)} %collective-permute-done.7.far_mate_ref, ...), custom_call_target="tpu_custom_call" | custom-call | flops 1000000000 | bytes 3000000 | tf_op jit(solution)/shard_map/key_back_1/pallas_call | solution.py:787
  51.9 2.1 %collective-permute-done.10 = bf16[72,768]{1,0:T(8,128)(2,1)S(1)} collective-permute-done((bf16[72,768]{1,0:T(8,128)(2,1)S(1)}, bf16[72,768]{1,0:T(8,128)(2,1)S(1)}, u32[]{:S(2)}, u32[]{:S(2)}) %collective-permute-start.10) | collective-permute-done | bytes 110624 | tf_op jit(solution)/shard_map/ppermute | solution.py:661
  54.1 1.1 %collective-permute-start.11 = (bf16[72,768]{1,0:T(8,128)(2,1)S(1)}, bf16[72,768]{1,0:T(8,128)(2,1)S(1)}, u32[]{:S(2)}, u32[]{:S(2)}) collective-permute-start(bf16[72,768]{1,0:T(8,128)(2,1)S(1)} %add_convert_fusion.1.refs_0_), channel_id=1, source_target_pairs={{0,2},{1,3},{2,0},{3,1},{4,6},{5,7},{6,4},{7,5},{8,10},{9,11},{10,... | collective-permute-start | bytes 331784 | tf_op jit(solution)/shard_map/ppermute | solution.py:661
  55.1 2.4 %key_back_2.1 = bf16[192,768]{1,0:T(8,128)(2,1)} custom-call(bf16[224,768]{1,0:T(8,128)(2,1)S(1)} %get-tuple-element.82.pack_ref.own_ref, bf16[224,768]{1,0:T(8,128)(2,1)S(1)} %collective-permute-done.3.mate_ref, bf16[160,768]{1,0:T(8,128)(2,1)S(1)} %collective-permute-done.5.far_ref, bf16[160,768]{1,0:T(8,128)(2,1)S(1)} %collective-permute-done.7.far_mate_ref, ...), custom_call_target="tpu_custom_call" | custom-call | flops 1000000000 | bytes 3000000 | tf_op jit(solution)/shard_map/key_back_2/pallas_call | solution.py:787
  57.7 1.9 %collective-permute-start.12 = (bf16[2,72,768]{2,1,0:T(8,128)(2,1)S(1)}, bf16[2,72,768]{2,1,0:T(8,128)(2,1)S(1)}, u32[]{:S(2)}, u32[]{:S(2)}) collective-permute-start(bf16[2,72,768]{2,1,0:T(8,128)(2,1)S(1)} %pad_maximum_fusion.1), channel_id=1, source_target_pairs={{0,1},{1,0},{2,3},{3,2},{4,5},{5,4},{6,7},{7,6},{8,9},{9,8},{10,11... | collective-permute-start | bytes 663560 | tf_op jit(solution)/shard_map/ppermute | solution.py:661
  59.7 1.1 %collective-permute-done.12 = bf16[2,72,768]{2,1,0:T(8,128)(2,1)S(1)} collective-permute-done((bf16[2,72,768]{2,1,0:T(8,128)(2,1)S(1)}, bf16[2,72,768]{2,1,0:T(8,128)(2,1)S(1)}, u32[]{:S(2)}, u32[]{:S(2)}) %collective-permute-start.12) | collective-permute-done | bytes 221216 | tf_op jit(solution)/shard_map/ppermute | solution.py:661
  60.8 1.0 %unpack.1 = (f32[64,768]{1,0:T(8,128)}, f32[64]{0:T(128)}, f32[64,768]{1,0:T(8,128)}, f32[768]{0:T(1024)}, f32[768]{0:T(1024)}, /*index=5*/f32[768]{0:T(1024)}, ...) custom-call(bf16[72,768]{1,0:T(8,128)(2,1)S(1)} %add_convert_fusion.1, ...), custom_call_target="tpu_custom_call" | custom-call | tf_op jit(solution)/shard_map/unpack/pallas_call | solution.py:840
  (52 shorter events, 3.8 us)
Async XLA Ops:
  0.6 1.9 %collective-permute-start = (bf16[192,768]{1,0:T(8,128)(2,1)}, bf16[192,768]{1,0:T(8,128)(2,1)S(1)}, u32[]{:S(2)}, u32[]{:S(2)}) collective-permute-start(bf16[192,768]{1,0:T(8,128)(2,1)} %bitcast.32), channel_id=1, source_target_pairs={{0,1},{1,0},{2,3},{3,2},{4,5},{5,4},{6,7},{7,6},{8,9},{9,8},{10,11... | collective-permute-start | bytes 884744 | tf_op jit(solution)/shard_map/ppermute | solution.py:658
  3.5 9.5 %copy-start = (bf16[192,1,768]{2,0,1:T(8,128)(2,1)S(1)}, bf16[192,1,768]{2,0,1:T(8,128)(2,1)}, u32[]{:S(2)}) copy-start(bf16[192,1,768]{2,0,1:T(8,128)(2,1)} %param.22) | copy-start | bytes 884740
  3.6 9.5 %copy-start.1 = (bf16[192,1,768]{2,0,1:T(8,128)(2,1)S(1)}, bf16[192,1,768]{2,0,1:T(8,128)(2,1)}, u32[]{:S(2)}) copy-start(bf16[192,1,768]{2,0,1:T(8,128)(2,1)} %param.43) | copy-start | bytes 884740
  3.6 9.5 %copy-start.2 = (bf16[768,64]{0,1:T(8,128)(2,1)S(1)}, bf16[768,64]{0,1:T(8,128)(2,1)}, u32[]{:S(2)}) copy-start(bf16[768,64]{0,1:T(8,128)(2,1)} %param.29) | copy-start | bytes 294916
  3.6 9.5 %copy-start.3 = (bf16[64,768]{1,0:T(8,128)(2,1)S(1)}, bf16[64,768]{1,0:T(8,128)(2,1)}, u32[]{:S(2)}) copy-start(bf16[64,768]{1,0:T(8,128)(2,1)} %up1_ref.1) | copy-start | bytes 294916
  3.6 9.5 %copy-start.4 = (bf16[768,64]{0,1:T(8,128)(2,1)S(1)}, bf16[768,64]{0,1:T(8,128)(2,1)}, u32[]{:S(2)}) copy-start(bf16[768,64]{0,1:T(8,128)(2,1)} %param.35) | copy-start | bytes 294916
  3.6 9.5 %copy-start.5 = (bf16[64,768]{1,0:T(8,128)(2,1)S(1)}, bf16[64,768]{1,0:T(8,128)(2,1)}, u32[]{:S(2)}) copy-start(bf16[64,768]{1,0:T(8,128)(2,1)} %up2_ref.1) | copy-start | bytes 294916
  3.6 9.5 %copy-start.6 = (f32[768]{0:T(1024)S(1)}, f32[768]{0:T(1024)}, u32[]{:S(2)}) copy-start(f32[768]{0:T(1024)} %ubias1_ref.1) | copy-start | bytes 9220
  3.6 9.5 %copy-start.7 = (f32[768]{0:T(1024)S(1)}, f32[768]{0:T(1024)}, u32[]{:S(2)}) copy-start(f32[768]{0:T(1024)} %gain1_ref.1) | copy-start | bytes 9220
  3.6 9.5 %copy-start.8 = (f32[768]{0:T(1024)S(1)}, f32[768]{0:T(1024)}, u32[]{:S(2)}) copy-start(f32[768]{0:T(1024)} %shift1_ref.1) | copy-start | bytes 9220
  3.7 9.5 %copy-start.9 = (f32[768]{0:T(1024)S(1)}, f32[768]{0:T(1024)}, u32[]{:S(2)}) copy-start(f32[768]{0:T(1024)} %ubias2_ref.1) | copy-start | bytes 9220
  3.7 9.5 %copy-start.10 = (f32[768]{0:T(1024)S(1)}, f32[768]{0:T(1024)}, u32[]{:S(2)}) copy-start(f32[768]{0:T(1024)} %gain2_ref.1) | copy-start | bytes 9220
  3.7 7.4 %collective-permute-start.1 = (bf16[128,768]{1,0:T(8,128)(2,1)S(1)}, bf16[128,768]{1,0:T(8,128)(2,1)S(1)}, u32[]{:S(2)}, u32[]{:S(2)}) collective-permute-start(bf16[128,768]{1,0:T(8,128)(2,1)S(1)} %pad_maximum_fusion.2), channel_id=1, source_target_pairs={{0,2},{1,3},{2,0},{3,1},{4,6},{5,7},{6,4},{7,5},{8,10},{9,11},{10,... | collective-permute-start | bytes 589832 | tf_op jit(solution)/shard_map/ppermute | solution.py:658
  11.1 2.0 %collective-permute-start.2 = (bf16[128,768]{1,0:T(8,128)(2,1)S(1)}, bf16[128,768]{1,0:T(8,128)(2,1)S(1)}, u32[]{:S(2)}, u32[]{:S(2)}) collective-permute-start(bf16[128,768]{1,0:T(8,128)(2,1)S(1)} %collective-permute-done.1.far_ref), channel_id=1, source_target_pairs={{0,1},{1,0},{2,3},{3,2},{4,5},{5,4},{6,7},{7,6},{8,9},{9,8},{10,11... | collective-permute-start | bytes 589832 | tf_op jit(solution)/shard_map/ppermute | solution.py:658
  28.9 1.6 %collective-permute-start.4 = (bf16[2,72,768]{2,1,0:T(8,128)(2,1)S(1)}, bf16[2,72,768]{2,1,0:T(8,128)(2,1)S(1)}, u32[]{:S(2)}, u32[]{:S(2)}) collective-permute-start(bf16[2,72,768]{2,1,0:T(8,128)(2,1)S(1)} %get-tuple-element.80), channel_id=1, source_target_pairs={{0,1},{1,0},{2,3},{3,2},{4,5},{5,4},{6,7},{7,6},{8,9},{9,8},{10,11... | collective-permute-start | bytes 663560 | tf_op jit(solution)/shard_map/ppermute | solution.py:661
  29.3 1.7 %collective-permute-start.3 = (bf16[224,768]{1,0:T(8,128)(2,1)S(1)}, bf16[224,768]{1,0:T(8,128)(2,1)S(1)}, u32[]{:S(2)}, u32[]{:S(2)}) collective-permute-start(bf16[224,768]{1,0:T(8,128)(2,1)S(1)} %get-tuple-element.82.pack_ref.own_ref), channel_id=1, source_target_pairs={{0,1},{1,0},{2,3},{3,2},{4,5},{5,4},{6,7},{7,6},{8,9},{9,8},{10,11... | collective-permute-start | bytes 1032200 | tf_op jit(solution)/shard_map/ppermute | solution.py:658
  31.0 4.4 %collective-permute-start.6 = (bf16[72,768]{1,0:T(8,128)(2,1)S(1)}, bf16[72,768]{1,0:T(8,128)(2,1)S(1)}, u32[]{:S(2)}, u32[]{:S(2)}) collective-permute-start(bf16[72,768]{1,0:T(8,128)(2,1)S(1)} %slice_bitcast_fusion.2), channel_id=1, source_target_pairs={{0,2},{1,3},{2,0},{3,1},{4,6},{5,7},{6,4},{7,5},{8,10},{9,11},{10,... | collective-permute-start | bytes 331784 | tf_op jit(solution)/shard_map/ppermute | solution.py:661
  32.6 8.1 %collective-permute-start.5 = (bf16[160,768]{1,0:T(8,128)(2,1)S(1)}, bf16[160,768]{1,0:T(8,128)(2,1)S(1)}, u32[]{:S(2)}, u32[]{:S(2)}) collective-permute-start(bf16[160,768]{1,0:T(8,128)(2,1)S(1)} %pad_maximum_fusion), channel_id=1, source_target_pairs={{0,2},{1,3},{2,0},{3,1},{4,6},{5,7},{6,4},{7,5},{8,10},{9,11},{10,... | collective-permute-start | bytes 737288 | tf_op jit(solution)/shard_map/ppermute | solution.py:658
  35.4 5.2 %collective-permute-start.8 = (bf16[72,768]{1,0:T(8,128)(2,1)S(1)}, bf16[72,768]{1,0:T(8,128)(2,1)S(1)}, u32[]{:S(2)}, u32[]{:S(2)}) collective-permute-start(bf16[72,768]{1,0:T(8,128)(2,1)S(1)} %fusion), channel_id=1, source_target_pairs={{0,4},{1,5},{2,6},{3,7},{4,0},{5,1},{6,2},{7,3},{8,12},{9,13},{10,... | collective-permute-start | bytes 331784 | tf_op jit(solution)/shard_map/ppermute | solution.py:661
  40.7 5.4 %collective-permute-start.9 = (bf16[72,768]{1,0:T(8,128)(2,1)S(1)}, bf16[72,768]{1,0:T(8,128)(2,1)S(1)}, u32[]{:S(2)}, u32[]{:S(2)}) collective-permute-start(bf16[72,768]{1,0:T(8,128)(2,1)S(1)} %add_convert_fusion.3), channel_id=1, source_target_pairs={{0,8},{1,9},{2,10},{3,11},{4,12},{5,13},{6,14},{7,15},{8,0},{9,1},... | collective-permute-start | bytes 331784 | tf_op jit(solution)/shard_map/ppermute | solution.py:661
  42.3 6.2 %collective-permute-start.7 = (bf16[160,768]{1,0:T(8,128)(2,1)S(1)}, bf16[160,768]{1,0:T(8,128)(2,1)S(1)}, u32[]{:S(2)}, u32[]{:S(2)}) collective-permute-start(bf16[160,768]{1,0:T(8,128)(2,1)S(1)} %collective-permute-done.5.far_ref), channel_id=1, source_target_pairs={{0,1},{1,0},{2,3},{3,2},{4,5},{5,4},{6,7},{7,6},{8,9},{9,8},{10,11... | collective-permute-start | bytes 737288 | tf_op jit(solution)/shard_map/ppermute | solution.py:658
  46.1 7.9 %collective-permute-start.10 = (bf16[72,768]{1,0:T(8,128)(2,1)S(1)}, bf16[72,768]{1,0:T(8,128)(2,1)S(1)}, u32[]{:S(2)}, u32[]{:S(2)}) collective-permute-start(bf16[72,768]{1,0:T(8,128)(2,1)S(1)} %add_convert_fusion.2), channel_id=1, source_target_pairs={{0,16},{1,17},{2,18},{3,19},{4,20},{5,21},{6,22},{7,23},{8,24},{9,... | collective-permute-start | bytes 331784 | tf_op jit(solution)/shard_map/ppermute | solution.py:661
  54.1 3.7 %collective-permute-start.11 = (bf16[72,768]{1,0:T(8,128)(2,1)S(1)}, bf16[72,768]{1,0:T(8,128)(2,1)S(1)}, u32[]{:S(2)}, u32[]{:S(2)}) collective-permute-start(bf16[72,768]{1,0:T(8,128)(2,1)S(1)} %add_convert_fusion.1.refs_0_), channel_id=1, source_target_pairs={{0,2},{1,3},{2,0},{3,1},{4,6},{5,7},{6,4},{7,5},{8,10},{9,11},{10,... | collective-permute-start | bytes 331784 | tf_op jit(solution)/shard_map/ppermute | solution.py:661
  57.7 3.1 %collective-permute-start.12 = (bf16[2,72,768]{2,1,0:T(8,128)(2,1)S(1)}, bf16[2,72,768]{2,1,0:T(8,128)(2,1)S(1)}, u32[]{:S(2)}, u32[]{:S(2)}) collective-permute-start(bf16[2,72,768]{2,1,0:T(8,128)(2,1)S(1)} %pad_maximum_fusion.1), channel_id=1, source_target_pairs={{0,1},{1,0},{2,3},{3,2},{4,5},{5,4},{6,7},{7,6},{8,9},{9,8},{10,11... | collective-permute-start | bytes 663560 | tf_op jit(solution)/shard_map/ppermute | solution.py:661
  (3 other events, 28.4 us)

commit v3 on v2

--- a/solution.py
+++ b/solution.py
@@ -12,8 +12,9 @@
 LONG_AT = 128
 LONG = 512
 ROWS_A = 64
+WIDE = GROUP * HEAD
 SHARE = 128
-CHUNK = 512
+CHUNK = 768
 SMALL = 8
 ROWS_B = 128
 NEG = -1e30
@@ -38,15 +39,8 @@
 
 
 def gelu_both(values):
-    size = jnp.abs(values) * 0.7071067811865476
-    inv = 1.0 / (1.0 + 0.3275911 * size)
-    bell = jnp.exp(-size * size)
-    poly = inv * (
-        0.254829592
-        + inv * (-0.284496736 + inv * (1.421413741 + inv * (-1.453152027 + inv * 1.061405429)))
-    )
-    tail = 0.5 * poly * bell
-    phi = jnp.where(values >= 0, 1.0 - tail, tail)
+    phi = 0.5 + 0.5 * lax.erf(values * 0.7071067811865476)
+    bell = jnp.exp(-0.5 * values * values)
     return values * phi, phi + values * bell * 0.3989422804014327
 
 
@@ -185,9 +179,13 @@
         pltpu.make_async_copy(source, target, sems.at[index])
         for index, (source, target) in enumerate(moves)
     ]
-    for copy in copies:
-        copy.start()
     block = lax.axis_index("blk")
+
+    @pl.when(block < 4)
+    def _():
+        for copy in copies:
+            copy.start()
+
     core = block % 2
     rows = own_ref.shape[0]
     first = block * rows
@@ -246,21 +244,27 @@
     vbuf,
     lse_ref,
     du1_ref,
-    pack_ref,
+    attended_ref,
+    dbranch_ref,
     keep_ref,
     send_ref,
     wouter_ref,
+    wouter_t_ref,
+    winner_t_ref,
     slope_ref,
     mixed_ref,
     sems,
 ):
     hidden_units = winner_ref.shape[1]
-    outer_copies = []
-    for index in range(hidden_units // CHUNK):
-        part = pl.ds(index * CHUNK, CHUNK)
-        copy = pltpu.make_async_copy(wouter_hbm.at[part], wouter_ref.at[part], sems.at[1 + index])
-        copy.start()
-        outer_copies.append(copy)
+
+    def outer_copy(index):
+        part = pl.ds(pl.multiple_of(index * CHUNK, CHUNK), CHUNK)
+        return pltpu.make_async_copy(wouter_hbm.at[part], wouter_ref.at[part], sems.at[1 + index])
+
+    @pl.loop(0, hidden_units // CHUNK)
+    def _(index):
+        outer_copy(index).start()
+
     mixed_copy = pltpu.make_async_copy(mixed_ref, mixed_hbm, sems.at[0])
     block = lax.axis_index("blk")
     core = block % 2
@@ -275,10 +279,6 @@
     def put(ref, value):
         ref[pl.ds(at_a, ROWS_A), :] = value[:ROWS_A]
         ref[pl.ds(at_b, ROWS_B), :] = value[ROWS_A:]
-
-    def natural(value):
-        rolled = jnp.concatenate([value[:, ROWS_A:], value[:, :ROWS_A]], axis=1)
-        return jnp.where(block == 0, rolled, value)
 
     near = pl.multiple_of(chip * 2 * rows, 2 * rows)
     kbuf[pl.ds(near, 2 * rows), :] = kpair_ref[...]
@@ -313,8 +313,8 @@
         attended_parts.append(jnp.concatenate(pieces, axis=1))
         lse_parts.append(lse)
     attended_f = jnp.concatenate(attended_parts, axis=0)
-    lse_own = jnp.concatenate(lse_parts, axis=0)
-    put(lse_ref, lse_own)
+    put(lse_ref, jnp.concatenate(lse_parts, axis=0))
+    put(attended_ref, attended_f)
     attended = attended_f.astype(BF16)
     branch = nn(attended, wout_ref[...]).astype(BF16)
 
@@ -328,11 +328,14 @@
     gain1 = row_of(gain1_ref)
     mid = (normal1 * gain1 + row_of(shift1_ref)).astype(BF16)
 
+    for index in range(hidden_units // CHUNK):
+        outer_copy(index).wait()
     ffn_f = jnp.zeros((rows, width), F32)
     for at in range(0, hidden_units, CHUNK):
         hidden_f, slope = gelu_both(nn(mid, winner_ref[:, at : at + CHUNK]))
         slope_ref[:, at : at + CHUNK] = slope
-        outer_copies[at // CHUNK].wait()
+        wouter_t_ref[:, at : at + CHUNK] = wouter_ref[at : at + CHUNK, :].T
+        winner_t_ref[at : at + CHUNK, :] = winner_ref[:, at : at + CHUNK].T
         ffn_f = ffn_f + nn(hidden_f.astype(BF16), wouter_ref[at : at + CHUNK, :])
     ffn = ffn_f.astype(BF16)
 
@@ -365,10 +368,10 @@
     dffn = (du2 + back2).astype(BF16)
     dmid = du2
     for at in range(0, hidden_units, CHUNK):
-        dhidden = (nt(dffn, wouter_ref[at : at + CHUNK, :]) * slope_ref[:, at : at + CHUNK]).astype(
+        dhidden = (nn(dffn, wouter_t_ref[:, at : at + CHUNK]) * slope_ref[:, at : at + CHUNK]).astype(
             BF16
         )
-        dmid = dmid + nt(dhidden, winner_ref[:, at : at + CHUNK])
+        dmid = dmid + nn(dhidden, winner_t_ref[at : at + CHUNK, :])
 
     grad_gain1 = jnp.sum(dmid * normal1, axis=0, keepdims=True)
     grad_shift1 = jnp.sum(dmid, axis=0, keepdims=True)
@@ -397,48 +400,53 @@
     for index, (matrix, one, two) in enumerate(quarters):
         small = jnp.concatenate([one, two, jnp.zeros((SMALL - 2, width), F32)], axis=0)
         whole = jnp.concatenate([matrix, small], axis=0).astype(BF16)
-        place = jnp.where(chip == index // 2, 0, 1)
-
-        @pl.when(core == index % 2)
-        def _(place=place, whole=whole):
-            keep_ref[place] = whole
-
-        @pl.when(core != index % 2)
-        def _(place=place, whole=whole):
-            send_ref[place] = whole
-
-    dbranch = (du1 + back1).astype(BF16)
-    dattended = nt(dbranch, wout_ref[...]).astype(BF16)
-    put(pack_ref, dattended)
-    product = dattended.astype(F32) * attended_f
+        for side in range(2):
+            half = whole[:, side * width // 2 : (side + 1) * width // 2]
+            place = 2 * (chip ^ (index // 2)) + (lax.axis_index("dp") % 2 ^ side)
+
+            @pl.when(core == index % 2)
+            def _(place=place, half=half):
+                keep_ref[place] = half
+
+            @pl.when(core != index % 2)
+            def _(place=place, half=half):
+                send_ref[place] = half
+
+    put(dbranch_ref, (du1 + back1).astype(BF16))
+    mixed_copy.wait()
+
+
+def attended_back_kernel(dbranch_ref, attended_ref, lse_ref, wout_ref, pack_ref, delta_ref):
+    rows, width = dbranch_ref.shape
+    dattended = nt(dbranch_ref[...], wout_ref[...]).astype(BF16)
+    pack_ref[:rows, :] = dattended
+    product = dattended.astype(F32) * attended_ref[...]
     product_hi = product.astype(BF16)
     product_lo = (product - product_hi.astype(F32)).astype(BF16)
-    head_of = lax.broadcasted_iota(jnp.int32, (16, width), 1) // HEAD
-    picks = (head_of == lax.broadcasted_iota(jnp.int32, (16, width), 0)).astype(BF16)
-    delta = natural(nt(picks, product_hi) + nt(picks, product_lo))
-    lse_rows = natural(
-        jnp.transpose(jnp.concatenate([lse_own, jnp.zeros((256 - rows, 128), F32)], axis=0))[
-            :16, :rows
-        ]
-    )
+    head_of = lax.broadcasted_iota(jnp.int32, (128, width), 1) // HEAD
+    picks = (head_of == lax.broadcasted_iota(jnp.int32, (128, width), 0)).astype(BF16)
+    delta = nt(product_hi, picks) + nt(product_lo, picks)
+    delta_ref[...] = delta
+    blank = jnp.zeros((256 - rows, 128), F32)
+    delta_rows = jnp.transpose(jnp.concatenate([delta, blank], axis=0))[:16]
+    lse_rows = jnp.transpose(jnp.concatenate([lse_ref[...], blank], axis=0))[:16]
 
     def pieces_of(value, count):
         out = []
         for _ in range(count):
             piece = value.astype(BF16)
             value = value - piece.astype(F32)
-            out.append(jnp.concatenate([piece, jnp.zeros((16, 256 - rows), BF16)], axis=1))
+            out.append(piece)
         return out
 
     pack_ref[rows : rows + 16, :] = jnp.concatenate(pieces_of(lse_rows, 3), axis=1)
     pack_ref[rows + 16 : rows + 32, :] = jnp.concatenate(
-        pieces_of(delta, 2) + [jnp.zeros((16, 256), BF16)], axis=1
-    )
-    mixed_copy.wait()
+        pieces_of(delta_rows, 2) + [jnp.zeros((16, 256), BF16)], axis=1
+    )
 
 
 def query_back_kernel(
-    group,
+    groups,
     far_ref,
     far_mate_ref,
     q_ref,
@@ -447,153 +455,157 @@
     bias_a_ref,
     bias_b_ref,
     lse_ref,
+    delta_ref,
     pack_ref,
     part_in_ref,
     wq_ref,
-    qbuf,
-    part_ref,
+    *outs,
 ):
     block = lax.axis_index("blk")
     rows = q_ref.shape[0] // 2
     core, chip = block % 2, block // 2
     at_a, at_b = own_rows(block)
     meet_b = partner_offset(block)
-    columns = slice(group * GROUP * HEAD, (group + 1) * GROUP * HEAD)
-    wq = wq_ref[:, columns]
+    all_columns = slice(groups[0] * WIDE, (groups[-1] + 1) * WIDE)
+    wq = wq_ref[:, all_columns]
     queries_far = (nn(far_tokens(core, far_ref, far_mate_ref), wq) * 0.125).astype(BF16)
-    qbuf[pl.ds(pl.multiple_of(chip * 2 * rows, rows), 2 * rows), :] = q_ref[:, columns]
-    qbuf[pl.ds(far_place(chip), 2 * SHARE), :] = queries_far
-    lane = lax.broadcasted_iota(jnp.int32, (1, 128), 1)
+    part_ref = outs[-1]
+    for index, (group, qbuf) in enumerate(zip(groups, outs)):
+        near = pl.ds(pl.multiple_of(chip * 2 * rows, rows), 2 * rows)
+        qbuf[near, :] = q_ref[:, group * WIDE : (group + 1) * WIDE]
+        qbuf[pl.ds(far_place(chip), 2 * SHARE), :] = queries_far[
+            :, index * WIDE : (index + 1) * WIDE
+        ]
     for at, count, meet, bias_ref in (
         (at_a, ROWS_A, LONG_AT, bias_a_ref),
         (at_b, ROWS_B, meet_b, bias_b_ref),
     ):
         lse = lse_ref[pl.ds(at, count), :]
-        log_total = jnp.concatenate(
-            [
-                jnp.sum(jnp.where(lane == group * GROUP + head, lse, 0.0), axis=-1, keepdims=True)
-                for head in range(GROUP)
-            ],
-            axis=0,
-        )
-        keys = kbuf[pl.ds(meet, LONG), columns]
-        scores = nt(spread_heads(q_ref[pl.ds(core * rows + at, count), columns]), keys)
-        scores = masked(scores, bias_ref[...])
-        probs = jnp.exp(scores - log_total)
-        dprobs = nt(
-            spread_heads(pack_ref[pl.ds(at, count), columns]), vbuf[pl.ds(meet, LONG), columns]
-        )
-        delta = jnp.sum(probs * dprobs, axis=-1, keepdims=True)
-        dscores = (probs * (dprobs - delta)).astype(BF16)
-        dquery = join_heads(nn(dscores, keys)).astype(BF16)
+        delta = delta_ref[pl.ds(at, count), :]
+        pieces = []
+        for group in groups:
+            columns = slice(group * WIDE, (group + 1) * WIDE)
+            heads = range(group * GROUP, (group + 1) * GROUP)
+            log_total = jnp.concatenate([lse[:, head : head + 1] for head in heads], axis=0)
+            deltas = jnp.concatenate([delta[:, head : head + 1] for head in heads], axis=0)
+            keys = kbuf[pl.ds(meet, LONG), columns]
+            scores = nt(spread_heads(q_ref[pl.ds(core * rows + at, count), columns]), keys)
+            scores = masked(scores, bias_ref[...])
+            probs = jnp.exp(scores - log_total)
+            dprobs = nt(
+                spread_heads(pack_ref[pl.ds(at, count), columns]), vbuf[pl.ds(meet, LONG), columns]
+            )
+            dscores = (probs * (dprobs - deltas)).astype(BF16)
+            pieces.append(join_heads(nn(dscores, keys)).astype(BF16))
+        dquery = jnp.concatenate(pieces, axis=1)
         part_ref[pl.ds(at, count), :] = part_in_ref[pl.ds(at, count), :] + nt(dquery, wq) * 0.125
 
 
-def key_back_kernel(
-    group,
-    own_ref,
-    mate_ref,
-    far_ref,
-    far_mate_ref,
-    qbuf,
-    kbuf,
-    vbuf,
-    back_a_ref,
-    back_b_ref,
-    part_ref,
-    wk_ref,
-    wv_ref,
-    out_ref,
-    abuf,
-):
+def gather_kernel(own_ref, mate_ref, far_ref, far_mate_ref, grads_ref, stats_ref):
     block = lax.axis_index("blk")
-    rows, width = out_ref.shape
+    rows = own_ref.shape[0] - 32
     core, chip = block % 2, block // 2
-    at_a, at_b = own_rows(block)
     meet_b = partner_offset(block)
-    first = block * rows
-    columns = slice(group * GROUP * HEAD, (group + 1) * GROUP * HEAD)
-    abuf[pl.ds(pl.multiple_of(first, rows), rows), :] = own_ref[:rows, columns]
-    abuf[pl.ds(pl.multiple_of((block ^ 1) * rows, rows), rows), :] = mate_ref[:rows, columns]
+    grads_ref[pl.ds(pl.multiple_of(block * rows, rows), rows), :] = own_ref[:rows, :]
+    grads_ref[pl.ds(pl.multiple_of((block ^ 1) * rows, rows), rows), :] = mate_ref[:rows, :]
     far_at = far_place(chip)
     far_first = pl.multiple_of(far_at + SHARE * core, 128)
     far_second = pl.multiple_of(far_at + SHARE * (1 - core), 128)
-    abuf[pl.ds(far_first, SHARE), :] = far_ref[:SHARE, columns]
-    abuf[pl.ds(far_second, SHARE), :] = far_mate_ref[:SHARE, columns]
+    grads_ref[pl.ds(far_first, SHARE), :] = far_ref[:SHARE, :]
+    grads_ref[pl.ds(far_second, SHARE), :] = far_mate_ref[:SHARE, :]
     stats = []
     for ref, at in ((own_ref, rows), (mate_ref, rows), (far_ref, SHARE), (far_mate_ref, SHARE)):
         lse = ref[at : at + 16, :].astype(F32)
         delta = ref[at + 16 : at + 32, :].astype(F32)
         stats.append(
-            (
-                (lse[:, :256] + (lse[:, 256:512] + lse[:, 512:]))[:, :rows],
-                (delta[:, :256] + delta[:, 256:512])[:, :rows],
-            )
+            jnp.concatenate(
+                [
+                    lse[:, :256] + (lse[:, 256:512] + lse[:, 512:]),
+                    delta[:, :256] + delta[:, 256:512],
+                ],
+                axis=0,
+            )[:, :rows]
         )
-
-    def in_order(which):
-        ordered = []
-        for place in range(4):
-            pick = stats[place][which]
-            for index in range(4):
-                pick = jnp.where(block ^ index == place, stats[index][which], pick)
-            ordered.append(pick)
-        return jnp.concatenate(ordered, axis=1)
-
-    lse_all, delta_all = in_order(0), in_order(1)
-
-    def window(stat, meet):
-        stat = stat[group * GROUP : (group + 1) * GROUP]
-        if isinstance(meet, int):
-            return stat[:, meet : meet + LONG]
-        here = stat[:, :LONG]
-        for start in (128, 256):
-            here = jnp.where(meet == start, stat[:, start : start + LONG], here)
-        return here
-
-    for at, count, meet, bias_ref in (
-        (at_a, ROWS_A, LONG_AT, back_a_ref),
-        (at_b, ROWS_B, meet_b, back_b_ref),
+    ordered = []
+    for place in range(4):
+        pick = stats[place]
+        for index in range(4):
+            if index != place:
+                pick = jnp.where(block ^ index == place, stats[index], pick)
+        ordered.append(pick)
+    whole = jnp.concatenate(ordered, axis=1)
+    stats_ref[:32, :] = whole[:, LONG_AT : LONG_AT + LONG]
+    here = whole[:, :LONG]
+    for start in (128, 256):
+        here = jnp.where(meet_b == start, whole[:, start : start + LONG], here)
+    stats_ref[32:, :] = here
+
+
+def key_back_kernel(groups, grads_ref, stats_ref, kbuf, vbuf, back_a_ref, back_b_ref, part_ref, *refs):
+    qbufs, (wk_ref, wv_ref, out_ref) = refs[:-3], refs[-3:]
+    block = lax.axis_index("blk")
+    rows = out_ref.shape[0]
+    at_a, at_b = own_rows(block)
+    first = block * rows
+    all_columns = slice(groups[0] * WIDE, (groups[-1] + 1) * WIDE)
+    for at, count, meet, bias_ref, at_stats in (
+        (at_a, ROWS_A, LONG_AT, back_a_ref, 0),
+        (at_b, ROWS_B, partner_offset(block), back_b_ref, 32),
     ):
-        queries = qbuf[pl.ds(meet, LONG), :]
-        grads = abuf[pl.ds(meet, LONG), :]
         own_at = pl.multiple_of(first + at, 64)
-        scores = nt(spread_heads(kbuf[pl.ds(own_at, count), columns]), queries)
-        scores = masked(scores, bias_ref[...])
-        probs = jnp.exp(less_rows(scores, window(lse_all, meet)))
-        dprobs = nt(spread_heads(vbuf[pl.ds(own_at, count), columns]), grads)
-        dscores = (probs * less_rows(dprobs, window(delta_all, meet))).astype(BF16)
-        dkey = join_heads(nn(dscores, queries)).astype(BF16)
-        dvalue = join_heads(nn(probs.astype(BF16), grads)).astype(BF16)
+        dkeys, dvalues = [], []
+        for group, qbuf in zip(groups, qbufs):
+            columns = slice(group * WIDE, (group + 1) * WIDE)
+            at_lse = at_stats + group * GROUP
+            at_delta = at_lse + 16
+            queries = qbuf[pl.ds(meet, LONG), :]
+            grads = grads_ref[pl.ds(meet, LONG), columns]
+            scores = nt(spread_heads(kbuf[pl.ds(own_at, count), columns]), queries)
+            scores = masked(scores, bias_ref[...])
+            probs = jnp.exp(less_rows(scores, stats_ref[at_lse : at_lse + GROUP, :]))
+            dprobs = nt(spread_heads(vbuf[pl.ds(own_at, count), columns]), grads)
+            dprobs = less_rows(dprobs, stats_ref[at_delta : at_delta + GROUP, :])
+            dscores = (probs * dprobs).astype(BF16)
+            dkeys.append(join_heads(nn(dscores, queries)).astype(BF16))
+            dvalues.append(join_heads(nn(probs.astype(BF16), grads)).astype(BF16))
         out_ref[pl.ds(at, count), :] = (
             part_ref[pl.ds(at, count), :]
-            + nt(dkey, wk_ref[:, columns])
-            + nt(dvalue, wv_ref[:, columns])
+            + nt(jnp.concatenate(dkeys, axis=1), wk_ref[:, all_columns])
+            + nt(jnp.concatenate(dvalues, axis=1), wv_ref[:, all_columns])
         ).astype(out_ref.dtype)
 
 
-def unpack_kernel(*refs):
-    parts, outs = refs[:4], refs[4:]
+def unpack_kernel(here_ref, other_ref, grad_ref, *refs):
+    places, outs, sems = refs[:13], refs[13:25], refs[25]
     block = lax.axis_index("blk")
+    side_here = lax.axis_index("dp") % 2
     core, chip = block % 2, block // 2
     adapt = outs[0].shape[0]
-    matrices = (outs[2], outs[0], outs[8], outs[6])
-    vectors = ((outs[3], None), (outs[4], outs[5]), (outs[9], None), (outs[10], outs[11]))
+    copies = [
+        pltpu.make_async_copy(source, target, sems.at[index])
+        for index, (source, target) in enumerate(zip((grad_ref, *outs), places))
+    ]
+    copies[0].start()
+    matrices = (2, 0, 8, 6)
+    vectors = ((3,), (4, 5), (9,), (10, 11))
     for index in range(4):
-        place = (core ^ (index % 2)) + 2 * (chip ^ (index // 2))
-        for at, part in enumerate(parts):
-
-            @pl.when(place == at)
-            def _(index=index, part=part):
-                matrices[index][...] = part[:adapt, :].astype(F32)
-                small = part[adapt : adapt + SMALL, :].astype(F32)
-                one, two = vectors[index]
-                one[...] = small[0]
-                if two is not None:
-                    two[...] = small[1]
-                if index == 0:
-                    outs[1][...] = small[1, :adapt]
-                    outs[7][...] = small[1, 128 : 128 + adapt]
+        halves = []
+        for side in range(2):
+            place = 2 * (chip ^ (index // 2)) + (side_here ^ side)
+            halves.append(jnp.where(core == index % 2, here_ref[place], other_ref[place]))
+        whole = jnp.concatenate(halves, axis=1).astype(F32)
+        outs[matrices[index]][...] = whole[:adapt]
+        ready = [matrices[index], *vectors[index]]
+        for row, vector in enumerate(vectors[index]):
+            outs[vector][...] = whole[adapt + row]
+        if index == 0:
+            outs[1][...] = whole[adapt + 1, :adapt]
+            outs[7][...] = whole[adapt + 1, 128 : 128 + adapt]
+            ready += [1, 7]
+        for out in ready:
+            copies[1 + out].start()
+    for copy in copies:
+        copy.wait()
 
 
 def params(megabytes):
@@ -717,27 +729,30 @@
     far_mate = swap(after(far, q), 1)
 
     part_rows = adapt + SMALL
-    mixed, kbuf, vbuf, lse, du1, pack, keep, send = pl.pallas_call(
+    mixed, kbuf, vbuf, lse, du1, attended, dbranch, keep, send = pl.pallas_call(
         main_kernel,
         in_specs=[VMEM] * 25 + [HBM],
-        out_specs=[HBM] + [VMEM] * 7,
+        out_specs=[HBM] + [VMEM] * 8,
         out_shape=[
             shape((rows, width), BF16),
             vmem((4 * rows, width), BF16),
             vmem((4 * rows, width), BF16),
             vmem((rows, 128), F32),
             vmem((rows, width), F32),
-            vmem((rows + 32, width), BF16),
-            vmem((2, part_rows, width), BF16),
-            vmem((2, part_rows, width), BF16),
+            vmem((rows, width), F32),
+            vmem((rows, width), BF16),
+            vmem((4, part_rows, width // 2), BF16),
+            vmem((4, part_rows, width // 2), BF16),
         ],
         scratch_shapes=[
+            pltpu.VMEM((hidden, width), BF16),
+            pltpu.VMEM((width, hidden), BF16),
             pltpu.VMEM((hidden, width), BF16),
             pltpu.VMEM((rows, hidden), F32),
             pltpu.VMEM((rows, width), BF16),
             pltpu.SemaphoreType.DMA((1 + hidden // CHUNK,)),
         ],
-        compiler_params=params(13),
+        compiler_params=params(30),
         cost_estimate=cost(8.0, 20.0),
         name="layer",
     )(
@@ -769,87 +784,87 @@
         in_hbm(w_outer),
     )
 
-    def add(left, right):
-        return (left.astype(F32) + right.astype(F32)).astype(BF16)
-
-    def query_back(group, part, pack_now):
+    def add(*terms):
+        return functools.reduce(jnp.add, [term.astype(F32) for term in terms]).astype(BF16)
+
+    pack, delta = pl.pallas_call(
+        attended_back_kernel,
+        in_specs=[VMEM] * 4,
+        out_specs=[VMEM] * 2,
+        out_shape=[vmem((rows + 32, width), BF16), vmem((rows, 128), F32)],
+        compiler_params=params(5),
+        cost_estimate=cost(0.5, 2.0),
+        name="attended_back",
+    )(dbranch, attended, lse, wout_here)
+
+    def query_back(groups, part):
         return pl.pallas_call(
-            functools.partial(query_back_kernel, group),
-            in_specs=[VMEM] * 11,
-            out_specs=[VMEM] * 2,
-            out_shape=[vmem((4 * rows, GROUP * HEAD), BF16), vmem((rows, width), F32)],
-            compiler_params=params(4),
-            cost_estimate=cost(1.0, 3.0),
-            name=f"query_back_{group}",
-        )(far, far_mate, q, kbuf, vbuf, bias_a, bias_b, lse, pack_now, part, wq_here)
-
-    def key_back(group, qbuf, part):
+            functools.partial(query_back_kernel, groups),
+            in_specs=[VMEM] * 12,
+            out_specs=[VMEM] * (len(groups) + 1),
+            out_shape=[vmem((4 * rows, WIDE), BF16)] * len(groups) + [vmem((rows, width), F32)],
+            compiler_params=params(5),
+            cost_estimate=cost(1.0 * len(groups), 3.0),
+            name=f"query_back_{groups[0]}",
+        )(far, far_mate, q, kbuf, vbuf, bias_a, bias_b, lse, delta, pack, part, wq_here)
+
+    def key_back(groups, qbufs, part, dtype):
         return pl.pallas_call(
-            functools.partial(key_back_kernel, group),
-            in_specs=[VMEM] * 12,
+            functools.partial(key_back_kernel, groups),
+            in_specs=[VMEM] * (9 + len(groups)),
             out_specs=VMEM,
-            out_shape=vmem((rows, width), F32) if group < 2 else shape((rows, width), BF16),
-            scratch_shapes=[pltpu.VMEM((4 * rows, GROUP * HEAD), BF16)],
-            compiler_params=params(4),
-            cost_estimate=cost(1.0, 3.0),
-            name=f"key_back_{group}",
-        )(
-            pack,
-            pack_mate,
-            pack_far,
-            pack_far_mate,
-            qbuf,
-            kbuf,
-            vbuf,
-            back_a,
-            back_b,
-            part,
-            wk_here,
-            wv_here,
-        )
-
-    pack_mate = swap(pack, 1)
-    total = add(keep, swap_all(send, 1))
-    pack_now, pack_mate, total = lax.optimization_barrier((pack, pack_mate, total))
-    share = near_share(pack_now, pack_mate) + [pack_now[rows:]]
-    pack_far = swap(jnp.concatenate(share, axis=0), 2)
-    arrived = swap_all(total[1], 2)
-    qbuf0, part = query_back(0, du1, pack_now)
-    total = add(total[0], after(arrived, part))
-    arrived = swap_all(total, 4)
-    qbuf1, part = query_back(1, after(part, total), pack_now)
-    pack_far, part = lax.optimization_barrier((pack_far, part))
-    pack_far_mate = swap(pack_far, 1)
-    total = add(total, after(arrived, part))
+            out_shape=vmem((rows, width), dtype),
+            compiler_params=params(5),
+            cost_estimate=cost(1.0 * len(groups), 3.0),
+            name=f"key_back_{groups[0]}",
+        )(grads_row, stats_row, kbuf, vbuf, back_a, back_b, part, *qbufs, wk_here, wv_here)
+
+    total = add(keep, after(swap_all(send, 1), pack))
+    arrived = [swap_all(total[index], mask) for index, mask in ((1, 4), (2, 2), (3, 6))]
+    pack_mate = swap(after(pack, total), 1)
+    qbuf0, qbuf1, part = query_back((0, 1), after(du1, total))
+    total = add(total[0], *lax.optimization_barrier((*arrived, part, pack_mate))[:3])
     masks = []
     while 8 << len(masks) < 4 * dp_size:
         masks.append(8 << len(masks))
     arrived = swap_all(total, masks[0])
-    qbuf2, part = query_back(2, after(part, total), pack_now)
-    total = add(total, after(arrived, part))
+    pack_now = after(pack, total)
+    share = near_share(pack_now, pack_mate) + [pack_now[rows:]]
+    pack_far = swap(jnp.concatenate(share, axis=0), 2)
+    total = add(total, arrived)
     arrived = swap_all(total, masks[1])
-    part = key_back(0, qbuf0, after(part, total))
-    part = key_back(1, qbuf1, part)
+    qbuf2, part = query_back((2,), after(part, total))
+    pack_far, part = lax.optimization_barrier((pack_far, part))
+    pack_far_mate = swap(pack_far, 1)
     total = add(total, after(arrived, part))
     for mask in masks[2:]:
         total = add(total, swap_all(total, mask))
-    across = swap_all(total, 2)
-    input_grad = key_back(2, qbuf2, after(part, total))
-    other_half = swap_all(after(jnp.stack([total, across]), input_grad), 1)
-
-    grads = pl.pallas_call(
+    others = [swap_all(total, mask) for mask in (4, 2, 6)]
+    grads_row, stats_row = pl.pallas_call(
+        gather_kernel,
+        in_specs=[VMEM] * 4,
+        out_specs=[VMEM] * 2,
+        out_shape=[vmem((4 * rows, width), BF16), vmem((64, LONG), F32)],
+        compiler_params=params(3),
+        cost_estimate=cost(0.1, 1.0),
+        name="gather",
+    )(pack, pack_mate, pack_far, after(pack_far_mate, total))
+    part = key_back((0, 1), (qbuf0, qbuf1), after(part, total), F32)
+    here = jnp.stack([total, *lax.optimization_barrier((*others, part))[:3]])
+    other = swap_all(here, 1)
+    input_grad = key_back((2,), (qbuf2,), after(part, here), BF16)
+
+    grad_dims = ((adapt, width), (adapt,), (adapt, width), (width,), (width,), (width,)) * 2
+    input_grad, *grads = pl.pallas_call(
         unpack_kernel,
-        in_specs=[VMEM] * 4,
-        out_specs=[VMEM] * 12,
-        out_shape=[
-            shape(dims, F32)
-            for dims in (
-                ((adapt, width), (adapt,), (adapt, width), (width,), (width,), (width,)) * 2
-            )
-        ],
-        compiler_params=params(4),
+        in_specs=[VMEM] * 3,
+        out_specs=[HBM] * 13,
+        out_shape=[shape((rows, width), BF16)] + [shape(dims, F32) for dims in grad_dims],
+        scratch_shapes=[pltpu.VMEM(dims, F32) for dims in grad_dims]
+        + [pltpu.SemaphoreType.DMA((13,))],
+        compiler_params=params(5),
         name="unpack",
-    )(total, other_half[0], across, other_half[1])
+    )(here, other, input_grad)
     return (mixed.reshape(tokens.shape), input_grad.reshape(tokens.shape)) + tuple(
         grad.T if index in (0, 6) else grad for index, grad in enumerate(grads)
     )

time: 62.4 us -> 53.4 us (0.86)
  waiting for transfers between devices: 10.4 us -> 3.79 us
  Pallas kernels: 33.2 us -> 26.7 us
  starting transfers between devices: 15.9 us -> 20.2 us
    pallas_call x1, Pallas kernels: 15.7 us -> 11 us  [body(): pl.pallas_call(main_kernel, in_specs=[VMEM] * 25 + [HBM], out_specs=[HBM]...]
    ppermute x7 -> x10, waiting for transfers between devices: 5.06 us -> 0.6 us  [swap_all(): lax.ppermute(array, ('dp', 'blk'), [(i, i ^ mask) for i in range(4 * dp_s...]
    ppermute x6, starting transfers between devices: 5.37 us -> 8.86 us  [swap(): return lax.ppermute(array, 'blk', [(i, i ^ mask) for i in range(4)])]
    ppermute x6, waiting for transfers between devices: 5.34 us -> 3.19 us  [swap(): return lax.ppermute(array, 'blk', [(i, i ^ mask) for i in range(4)])]
    pallas_call x7, Pallas kernels: 12.9 us -> 11.1 us  [the longest x2 4.72 us: key_back(): pl.pallas_call(functools.partial(key_back_kernel, groups), in_specs=[VMEM...]
    ppermute x7 -> x10, starting transfers between devices: 10.5 us -> 11.3 us  [swap_all(): lax.ppermute(array, ('dp', 'blk'), [(i, i ^ mask) for i in range(4 * dp_s...]
  transfers between devices with their start and end apart: 13 -> 16, of which waited for: 10 -> 6; matrix products, arithmetic and copies ran while one was open for 0% -> 0% of each run, Pallas kernels for 27% -> 27%
where the time goes in v3:
time: 53.4 us; the launch traced here: 53.2 us
  Pallas kernels  26.7 us (50%)
  starting transfers between devices  20.2 us (38%)
  waiting for transfers between devices  3.79 us (7%)
  other arithmetic  1.24 us (2%)
  between operations  1.16 us (2%)
    ppermute x10, starting transfers between devices, swap_all(): lax.ppermute(array, ('dp', 'blk'), [(i, i ^ mask) for i in range(4 * dp_s...  11.3 us
    pallas_call x1, Pallas kernels, body(): pl.pallas_call(main_kernel, in_specs=[VMEM] * 25 + [HBM], out_specs=[HBM]...  11 us
    ppermute x6, starting transfers between devices, swap(): return lax.ppermute(array, 'blk', [(i, i ^ mask) for i in range(4)])  8.86 us
    pallas_call x2, Pallas kernels, key_back(): pl.pallas_call(functools.partial(key_back_kernel, groups), in_specs=[VMEM...  4.72 us
    pallas_call x1, Pallas kernels, body(): pl.pallas_call(project_kernel, in_specs=[SMEM] * 2 + [HBM, VMEM] + [HBM]...  4.59 us
    pallas_call x2, Pallas kernels, query_back(): pl.pallas_call(functools.partial(query_back_kernel, groups), in_specs=[VM...  4.14 us
    ppermute x6, waiting for transfers between devices, swap(): return lax.ppermute(array, 'blk', [(i, i ^ mask) for i in range(4)])  3.19 us
    pallas_call x1, Pallas kernels, body(): pl.pallas_call(unpack_kernel, in_specs=[VMEM] * 3, out_specs=[HBM] * 13,...  1.12 us
  transfers between devices with their start and end apart: 16, of which 6 were waited for; matrix products, arithmetic and copies ran while one was open for 0% of the time, Pallas kernels for 27%

profile of v3, /device:TPU:1, one launch (start us, length us, event | category | flops | bytes accessed | tf_op | source)
XLA Modules:
  0.0 53.2 jit_solution(12999721907777335287)
XLA Ops:
  0.8 1.7 %collective-permute-done.mate_ref = bf16[192,768]{1,0:T(8,128)(2,1)S(1)} collective-permute-done((bf16[192,768]{1,0:T(8,128)(2,1)}, bf16[192,768]{1,0:T(8,128)(2,1)S(1)}, u32[]{:S(2)}, u32[]{:S(2)}) %collective-permute-start) | collective-permute-done | bytes 294944 | tf_op jit(solution)/shard_map/ppermute | solution.py:670
  2.5 1.0 %slice_select_fusion.3 = (bf16[64,768]{1,0:T(8,128)(2,1)S(1)}, bf16[64,768]{1,0:T(8,128)(2,1)S(1)}) fusion(bf16[192,768]{1,0:T(8,128)(2,1)S(1)} %collective-permute-done.mate_ref, pred[]{:T(512)S(6)} %eq.8, pred[]{:T(512)S(6)} %eq.7, pred[]{:T(512)S(6)} %eq.6, bf16[192,1,768]{2,0,1:T(8,128)(2,1)} %param.22), kind=kLoop, calls=%fused_computation.17 | loop fusion | flops 294912 | bytes 688131 | tf_op jit(solution)/shard_map/jit(_where)/select_n | solution.py:687
  3.7 2.4 %collective-permute-start.1 = (bf16[128,768]{1,0:T(8,128)(2,1)S(1)}, bf16[128,768]{1,0:T(8,128)(2,1)S(1)}, u32[]{:S(2)}, u32[]{:S(2)}) collective-permute-start(bf16[128,768]{1,0:T(8,128)(2,1)S(1)} %pad_maximum_fusion.2), channel_id=1, source_target_pairs={{0,2},{1,3},{2,0},{3,1},{4,6},{5,7},{6,4},{7,5},{8,10},{9,11},{10,... | collective-permute-start | bytes 589832 | tf_op jit(solution)/shard_map/ppermute | solution.py:670
  6.1 4.6 %project.1 = (bf16[384,768]{1,0:T(8,128)(2,1)S(1)}, bf16[384,768]{1,0:T(8,128)(2,1)S(1)}, bf16[384,768]{1,0:T(8,128)(2,1)S(1)}, f32[64,512]{1,0:T(8,128)S(1)}, f...) custom-call(s32[1,6]{1,0:T(1,128)} %len_ref.1, ...), custom_call_target="tpu_custom_call" | custom-call | flops 2000000000 | bytes 12000000 | tf_op jit(solution)/shard_map/project/pallas_call | solution.py:706
  10.7 0.4 collective-permute-done.1.far_ref
  11.1 0.9 %collective-permute-start.2 = (bf16[128,768]{1,0:T(8,128)(2,1)S(1)}, bf16[128,768]{1,0:T(8,128)(2,1)S(1)}, u32[]{:S(2)}, u32[]{:S(2)}) collective-permute-start(bf16[128,768]{1,0:T(8,128)(2,1)S(1)} %collective-permute-done.1.far_ref), channel_id=1, source_target_pairs={{0,1},{1,0},{2,3},{3,2},{4,5},{5,4},{6,7},{7,6},{8,9},{9,8},{10,11... | collective-permute-start | bytes 589832 | tf_op jit(solution)/shard_map/ppermute | solution.py:670
  12.0 1.1 %collective-permute-done.2.far_mate_ref = bf16[128,768]{1,0:T(8,128)(2,1)S(1)} collective-permute-done((bf16[128,768]{1,0:T(8,128)(2,1)S(1)}, bf16[128,768]{1,0:T(8,128)(2,1)S(1)}, u32[]{:S(2)}, u32[]{:S(2)}) %collective-permute-start.2) | collective-permute-done | bytes 196640 | tf_op jit(solution)/shard_map/ppermute | solution.py:670
  13.2 11.0 %layer.1 = (bf16[192,768]{1,0:T(8,128)(2,1)}, bf16[768,768]{1,0:T(8,128)(2,1)S(1)}, bf16[768,768]{1,0:T(8,128)(2,1)S(1)}, f32[192,128]{1,0:T(8,128)S(1)}, f32[19...) custom-call(bf16[192,768]{1,0:T(8,128)(2,1)S(1)} %bitcast.38, ...), custom_call_target="tpu_custom_call" | custom-call | flops 8000000000 | bytes 20000000 | tf_op jit(solution)/shard_map/layer/pallas_call | solution.py:732
  24.2 0.4 collective-permute-start.3
  24.7 1.0 %attended_back.1 = (bf16[224,768]{1,0:T(8,128)(2,1)S(1)}, f32[192,128]{1,0:T(8,128)S(1)}) custom-call(bf16[192,768]{1,0:T(8,128)(2,1)S(1)} %get-tuple-element.88.dbranch_ref, f32[192,768]{1,0:T(8,128)S(1)} %get-tuple-element.89.attended_ref, f32[192,128]{1,0:T(8,128)S(1)} %get-tuple-element.90.lse_ref, bf16[768,768]{1,0:T(8,128)(2,1)S(1)} %get-tuple-element.83.wout_ref), custom_call_target="tpu_custom_call" | custom-call | flops 500000000 | bytes 2000000 | tf_op jit(solution)/shard_map/attended_back/pallas_call | solution.py:790
  25.8 0.4 collective-permute-start.7
  26.3 2.5 %collective-permute-start.6 = (bf16[72,384]{1,0:T(8,128)(2,1)S(1)}, bf16[72,384]{1,0:T(8,128)(2,1)S(1)}, u32[]{:S(2)}, u32[]{:S(2)}) collective-permute-start(bf16[72,384]{1,0:T(8,128)(2,1)S(1)} %get-tuple-element.140), channel_id=1, source_target_pairs={{0,6},{1,7},{2,4},{3,5},{4,2},{5,3},{6,0},{7,1},{8,14},{9,15},{10,... | collective-permute-start | bytes 165896 | tf_op jit(solution)/shard_map/ppermute | solution.py:673
  29.1 2.4 %query_back_0.1 = (bf16[768,256]{1,0:T(8,128)(2,1)S(1)}, bf16[768,256]{1,0:T(8,128)(2,1)S(1)}, f32[192,768]{1,0:T(8,128)S(1)}) custom-call(bf16[128,768]{1,0:T(8,128)(2,1)S(1)} %collective-permute-done.1.far_ref, bf16[128,768]{1,0:T(8,128)(2,1)S(1)} %collective-permute-done.2.far_mate_ref, bf16[384,768]{1,0:T(8,128)(2,1)S(1)} %get-tuple-element.75.q_ref, ...), custom_call_target="tpu_custom_call" | custom-call | flops 2000000000 | bytes 3000000 | tf_op jit(solution)/shard_map/query_back_0/pallas_call | solution.py:801
  32.0 1.4 %collective-permute-start.8 = (bf16[72,384]{1,0:T(8,128)(2,1)S(1)}, bf16[72,384]{1,0:T(8,128)(2,1)S(1)}, u32[]{:S(2)}, u32[]{:S(2)}) collective-permute-start(bf16[72,384]{1,0:T(8,128)(2,1)S(1)} %fusion.2), channel_id=1, source_target_pairs={{0,8},{1,9},{2,10},{3,11},{4,12},{5,13},{6,14},{7,15},{8,0},{9,1},... | collective-permute-start | bytes 165896 | tf_op jit(solution)/shard_map/ppermute | solution.py:673
  33.5 1.7 %collective-permute-start.10 = (bf16[160,768]{1,0:T(8,128)(2,1)S(1)}, bf16[160,768]{1,0:T(8,128)(2,1)S(1)}, u32[]{:S(2)}, u32[]{:S(2)}) collective-permute-start(bf16[160,768]{1,0:T(8,128)(2,1)S(1)} %pad_maximum_fusion), channel_id=1, source_target_pairs={{0,2},{1,3},{2,0},{3,1},{4,6},{5,7},{6,4},{7,5},{8,10},{9,11},{10,... | collective-permute-start | bytes 737288 | tf_op jit(solution)/shard_map/ppermute | solution.py:670
  35.2 2.4 %collective-permute-start.9 = (bf16[72,384]{1,0:T(8,128)(2,1)S(1)}, bf16[72,384]{1,0:T(8,128)(2,1)S(1)}, u32[]{:S(2)}, u32[]{:S(2)}) collective-permute-start(bf16[72,384]{1,0:T(8,128)(2,1)S(1)} %add_convert_fusion.2), channel_id=1, source_target_pairs={{0,16},{1,17},{2,18},{3,19},{4,20},{5,21},{6,22},{7,23},{8,24},{9,... | collective-permute-start | bytes 165896 | tf_op jit(solution)/shard_map/ppermute | solution.py:673
  37.5 1.7 %query_back_2.1 = (bf16[768,256]{1,0:T(8,128)(2,1)S(1)}, f32[192,768]{1,0:T(8,128)S(1)}) custom-call(bf16[128,768]{1,0:T(8,128)(2,1)S(1)} %collective-permute-done.1.far_ref, bf16[128,768]{1,0:T(8,128)(2,1)S(1)} %collective-permute-done.2.far_mate_ref, bf16[384,768]{1,0:T(8,128)(2,1)S(1)} %get-tuple-element.75.q_ref, ...), custom_call_target="tpu_custom_call" | custom-call | flops 1000000000 | bytes 3000000 | tf_op jit(solution)/shard_map/query_back_2/pallas_call | solution.py:801
  39.3 3.3 %collective-permute-start.14 = (bf16[160,768]{1,0:T(8,128)(2,1)S(1)}, bf16[160,768]{1,0:T(8,128)(2,1)S(1)}, u32[]{:S(2)}, u32[]{:S(2)}) collective-permute-start(bf16[160,768]{1,0:T(8,128)(2,1)S(1)} %collective-permute-done.10.far_ref), channel_id=1, source_target_pairs={{0,1},{1,0},{2,3},{3,2},{4,5},{5,4},{6,7},{7,6},{8,9},{9,8},{10,11... | collective-permute-start | bytes 737288 | tf_op jit(solution)/shard_map/ppermute | solution.py:670
  42.6 1.5 %collective-permute-start.13 = (bf16[72,384]{1,0:T(8,128)(2,1)S(1)}, bf16[72,384]{1,0:T(8,128)(2,1)S(1)}, u32[]{:S(2)}, u32[]{:S(2)}) collective-permute-start(bf16[72,384]{1,0:T(8,128)(2,1)S(1)} %add_convert_fusion.1), channel_id=1, source_target_pairs={{0,6},{1,7},{2,4},{3,5},{4,2},{5,3},{6,0},{7,1},{8,14},{9,15},{10,... | collective-permute-start | bytes 165896 | tf_op jit(solution)/shard_map/ppermute | solution.py:673
  44.4 0.9 %collective-permute-start.11 = (bf16[72,384]{1,0:T(8,128)(2,1)S(1)}, bf16[72,384]{1,0:T(8,128)(2,1)S(1)}, u32[]{:S(2)}, u32[]{:S(2)}) collective-permute-start(bf16[72,384]{1,0:T(8,128)(2,1)S(1)} %add_convert_fusion.1), channel_id=1, source_target_pairs={{0,4},{1,5},{2,6},{3,7},{4,0},{5,1},{6,2},{7,3},{8,12},{9,13},{10,... | collective-permute-start | bytes 165896 | tf_op jit(solution)/shard_map/ppermute | solution.py:673
  45.5 3.0 %key_back_0.1.part_ref = f32[192,768]{1,0:T(8,128)S(1)} custom-call(bf16[768,768]{1,0:T(8,128)(2,1)S(1)} %get-tuple-element.111.grads_ref, f32[64,512]{1,0:T(8,128)S(1)} %get-tuple-element.112.stats_ref, bf16[768,768]{1,0:T(8,128)(2,1)S(1)} %get-tuple-element.93.kbuf, bf16[768,768]{1,0:T(8,128)(2,1)S(1)} %get-tuple-element.94.vbuf, ...), custom_call_target="tpu_custom_call" | custom-call | flops 2000000000 | bytes 3000000 | tf_op jit(solution)/shard_map/key_back_0/pallas_call | solution.py:812
  48.6 1.6 %collective-permute-start.15 = (bf16[4,72,384]{2,1,0:T(8,128)(2,1)S(1)}, bf16[4,72,384]{2,1,0:T(8,128)(2,1)S(1)}, u32[]{:S(2)}, u32[]{:S(2)}) collective-permute-start(bf16[4,72,384]{2,1,0:T(8,128)(2,1)S(1)} %pad_maximum_fusion.1.here_ref), channel_id=1, source_target_pairs={{0,1},{1,0},{2,3},{3,2},{4,5},{5,4},{6,7},{7,6},{8,9},{9,8},{10,11... | collective-permute-start | bytes 663560 | tf_op jit(solution)/shard_map/ppermute | solution.py:673
  50.2 1.7 %key_back_2.1.grad_ref = bf16[192,768]{1,0:T(8,128)(2,1)S(1)} custom-call(bf16[768,768]{1,0:T(8,128)(2,1)S(1)} %get-tuple-element.111.grads_ref, f32[64,512]{1,0:T(8,128)S(1)} %get-tuple-element.112.stats_ref, bf16[768,768]{1,0:T(8,128)(2,1)S(1)} %get-tuple-element.93.kbuf, bf16[768,768]{1,0:T(8,128)(2,1)S(1)} %get-tuple-element.94.vbuf, ...), custom_call_target="tpu_custom_call" | custom-call | flops 1000000000 | bytes 3000000 | tf_op jit(solution)/shard_map/key_back_2/pallas_call | solution.py:812
  51.9 1.1 %unpack.1 = (bf16[192,768]{1,0:T(8,128)(2,1)}, f32[64,768]{1,0:T(8,128)}, f32[64]{0:T(128)}, f32[64,768]{1,0:T(8,128)}, f32[768]{0:T(1024)}, /*index=5*/f32[768]...) custom-call(bf16[4,72,384]{2,1,0:T(8,128)(2,1)S(1)} %pad_maximum_fus, ...), custom_call_target="tpu_custom_call" | custom-call | tf_op jit(solution)/shard_map/unpack/pallas_call | solution.py:858
  (56 shorter events, 1.9 us)
Async XLA Ops:
  0.6 1.9 %collective-permute-start = (bf16[192,768]{1,0:T(8,128)(2,1)}, bf16[192,768]{1,0:T(8,128)(2,1)S(1)}, u32[]{:S(2)}, u32[]{:S(2)}) collective-permute-start(bf16[192,768]{1,0:T(8,128)(2,1)} %bitcast.36), channel_id=1, source_target_pairs={{0,1},{1,0},{2,3},{3,2},{4,5},{5,4},{6,7},{7,6},{8,9},{9,8},{10,11... | collective-permute-start | bytes 884744 | tf_op jit(solution)/shard_map/ppermute | solution.py:670
  3.5 9.5 %copy-start = (bf16[192,1,768]{2,0,1:T(8,128)(2,1)S(1)}, bf16[192,1,768]{2,0,1:T(8,128)(2,1)}, u32[]{:S(2)}) copy-start(bf16[192,1,768]{2,0,1:T(8,128)(2,1)} %param.22) | copy-start | bytes 884740
  3.6 9.5 %copy-start.1 = (bf16[192,1,768]{2,0,1:T(8,128)(2,1)S(1)}, bf16[192,1,768]{2,0,1:T(8,128)(2,1)}, u32[]{:S(2)}) copy-start(bf16[192,1,768]{2,0,1:T(8,128)(2,1)} %param.43) | copy-start | bytes 884740
  3.6 9.5 %copy-start.2 = (bf16[768,64]{0,1:T(8,128)(2,1)S(1)}, bf16[768,64]{0,1:T(8,128)(2,1)}, u32[]{:S(2)}) copy-start(bf16[768,64]{0,1:T(8,128)(2,1)} %param.29) | copy-start | bytes 294916
  3.6 9.5 %copy-start.3 = (bf16[64,768]{1,0:T(8,128)(2,1)S(1)}, bf16[64,768]{1,0:T(8,128)(2,1)}, u32[]{:S(2)}) copy-start(bf16[64,768]{1,0:T(8,128)(2,1)} %up1_ref.1) | copy-start | bytes 294916
  3.6 9.5 %copy-start.4 = (bf16[768,64]{0,1:T(8,128)(2,1)S(1)}, bf16[768,64]{0,1:T(8,128)(2,1)}, u32[]{:S(2)}) copy-start(bf16[768,64]{0,1:T(8,128)(2,1)} %param.35) | copy-start | bytes 294916
  3.6 9.5 %copy-start.5 = (bf16[64,768]{1,0:T(8,128)(2,1)S(1)}, bf16[64,768]{1,0:T(8,128)(2,1)}, u32[]{:S(2)}) copy-start(bf16[64,768]{1,0:T(8,128)(2,1)} %up2_ref.1) | copy-start | bytes 294916
  3.6 9.5 %copy-start.6 = (f32[768]{0:T(1024)S(1)}, f32[768]{0:T(1024)}, u32[]{:S(2)}) copy-start(f32[768]{0:T(1024)} %ubias1_ref.1) | copy-start | bytes 9220
  3.6 9.5 %copy-start.7 = (f32[768]{0:T(1024)S(1)}, f32[768]{0:T(1024)}, u32[]{:S(2)}) copy-start(f32[768]{0:T(1024)} %gain1_ref.1) | copy-start | bytes 9220
  3.7 7.4 %collective-permute-start.1 = (bf16[128,768]{1,0:T(8,128)(2,1)S(1)}, bf16[128,768]{1,0:T(8,128)(2,1)S(1)}, u32[]{:S(2)}, u32[]{:S(2)}) collective-permute-start(bf16[128,768]{1,0:T(8,128)(2,1)S(1)} %pad_maximum_fusion.2), channel_id=1, source_target_pairs={{0,2},{1,3},{2,0},{3,1},{4,6},{5,7},{6,4},{7,5},{8,10},{9,11},{10,... | collective-permute-start | bytes 589832 | tf_op jit(solution)/shard_map/ppermute | solution.py:670
  11.1 2.0 %collective-permute-start.2 = (bf16[128,768]{1,0:T(8,128)(2,1)S(1)}, bf16[128,768]{1,0:T(8,128)(2,1)S(1)}, u32[]{:S(2)}, u32[]{:S(2)}) collective-permute-start(bf16[128,768]{1,0:T(8,128)(2,1)S(1)} %collective-permute-done.1.far_ref), channel_id=1, source_target_pairs={{0,1},{1,0},{2,3},{3,2},{4,5},{5,4},{6,7},{7,6},{8,9},{9,8},{10,11... | collective-permute-start | bytes 589832 | tf_op jit(solution)/shard_map/ppermute | solution.py:670
  24.2 1.5 %collective-permute-start.3 = (bf16[4,72,384]{2,1,0:T(8,128)(2,1)S(1)}, bf16[4,72,384]{2,1,0:T(8,128)(2,1)S(1)}, u32[]{:S(2)}, u32[]{:S(2)}) collective-permute-start(bf16[4,72,384]{2,1,0:T(8,128)(2,1)S(1)} %get-tuple-element.87), channel_id=1, source_target_pairs={{0,1},{1,0},{2,3},{3,2},{4,5},{5,4},{6,7},{7,6},{8,9},{9,8},{10,11... | collective-permute-start | bytes 663560 | tf_op jit(solution)/shard_map/ppermute | solution.py:673
  25.8 6.2 %collective-permute-start.7 = (bf16[224,768]{1,0:T(8,128)(2,1)S(1)}, bf16[224,768]{1,0:T(8,128)(2,1)S(1)}, u32[]{:S(2)}, u32[]{:S(2)}) collective-permute-start(bf16[224,768]{1,0:T(8,128)(2,1)S(1)} %get-tuple-element.104.pack_ref.own_ref), channel_id=1, source_target_pairs={{0,1},{1,0},{2,3},{3,2},{4,5},{5,4},{6,7},{7,6},{8,9},{9,8},{10,11... | collective-permute-start | bytes 1032200 | tf_op jit(solution)/shard_map/ppermute | solution.py:670
  26.3 5.3 %collective-permute-start.6 = (bf16[72,384]{1,0:T(8,128)(2,1)S(1)}, bf16[72,384]{1,0:T(8,128)(2,1)S(1)}, u32[]{:S(2)}, u32[]{:S(2)}) collective-permute-start(bf16[72,384]{1,0:T(8,128)(2,1)S(1)} %get-tuple-element.140), channel_id=1, source_target_pairs={{0,6},{1,7},{2,4},{3,5},{4,2},{5,3},{6,0},{7,1},{8,14},{9,15},{10,... | collective-permute-start | bytes 165896 | tf_op jit(solution)/shard_map/ppermute | solution.py:673
  28.8 3.0 %collective-permute-start.5 = (bf16[72,384]{1,0:T(8,128)(2,1)S(1)}, bf16[72,384]{1,0:T(8,128)(2,1)S(1)}, u32[]{:S(2)}, u32[]{:S(2)}) collective-permute-start(bf16[72,384]{1,0:T(8,128)(2,1)S(1)} %get-tuple-element.141), channel_id=1, source_target_pairs={{0,2},{1,3},{2,0},{3,1},{4,6},{5,7},{6,4},{7,5},{8,10},{9,11},{10,... | collective-permute-start | bytes 165896 | tf_op jit(solution)/shard_map/ppermute | solution.py:673
  29.0 3.0 %collective-permute-start.4 = (bf16[72,384]{1,0:T(8,128)(2,1)S(1)}, bf16[72,384]{1,0:T(8,128)(2,1)S(1)}, u32[]{:S(2)}, u32[]{:S(2)}) collective-permute-start(bf16[72,384]{1,0:T(8,128)(2,1)S(1)} %get-tuple-element.142), channel_id=1, source_target_pairs={{0,4},{1,5},{2,6},{3,7},{4,0},{5,1},{6,2},{7,3},{8,12},{9,13},{10,... | collective-permute-start | bytes 165896 | tf_op jit(solution)/shard_map/ppermute | solution.py:673
  32.0 3.1 %collective-permute-start.8 = (bf16[72,384]{1,0:T(8,128)(2,1)S(1)}, bf16[72,384]{1,0:T(8,128)(2,1)S(1)}, u32[]{:S(2)}, u32[]{:S(2)}) collective-permute-start(bf16[72,384]{1,0:T(8,128)(2,1)S(1)} %fusion.2), channel_id=1, source_target_pairs={{0,8},{1,9},{2,10},{3,11},{4,12},{5,13},{6,14},{7,15},{8,0},{9,1},... | collective-permute-start | bytes 165896 | tf_op jit(solution)/shard_map/ppermute | solution.py:673
  33.5 5.8 %collective-permute-start.10 = (bf16[160,768]{1,0:T(8,128)(2,1)S(1)}, bf16[160,768]{1,0:T(8,128)(2,1)S(1)}, u32[]{:S(2)}, u32[]{:S(2)}) collective-permute-start(bf16[160,768]{1,0:T(8,128)(2,1)S(1)} %pad_maximum_fusion), channel_id=1, source_target_pairs={{0,2},{1,3},{2,0},{3,1},{4,6},{5,7},{6,4},{7,5},{8,10},{9,11},{10,... | collective-permute-start | bytes 737288 | tf_op jit(solution)/shard_map/ppermute | solution.py:670
  35.2 7.4 %collective-permute-start.9 = (bf16[72,384]{1,0:T(8,128)(2,1)S(1)}, bf16[72,384]{1,0:T(8,128)(2,1)S(1)}, u32[]{:S(2)}, u32[]{:S(2)}) collective-permute-start(bf16[72,384]{1,0:T(8,128)(2,1)S(1)} %add_convert_fusion.2), channel_id=1, source_target_pairs={{0,16},{1,17},{2,18},{3,19},{4,20},{5,21},{6,22},{7,23},{8,24},{9,... | collective-permute-start | bytes 165896 | tf_op jit(solution)/shard_map/ppermute | solution.py:673
  39.3 6.1 %collective-permute-start.14 = (bf16[160,768]{1,0:T(8,128)(2,1)S(1)}, bf16[160,768]{1,0:T(8,128)(2,1)S(1)}, u32[]{:S(2)}, u32[]{:S(2)}) collective-permute-start(bf16[160,768]{1,0:T(8,128)(2,1)S(1)} %collective-permute-done.10.far_ref), channel_id=1, source_target_pairs={{0,1},{1,0},{2,3},{3,2},{4,5},{5,4},{6,7},{7,6},{8,9},{9,8},{10,11... | collective-permute-start | bytes 737288 | tf_op jit(solution)/shard_map/ppermute | solution.py:670
  42.6 5.9 %collective-permute-start.13 = (bf16[72,384]{1,0:T(8,128)(2,1)S(1)}, bf16[72,384]{1,0:T(8,128)(2,1)S(1)}, u32[]{:S(2)}, u32[]{:S(2)}) collective-permute-start(bf16[72,384]{1,0:T(8,128)(2,1)S(1)} %add_convert_fusion.1), channel_id=1, source_target_pairs={{0,6},{1,7},{2,4},{3,5},{4,2},{5,3},{6,0},{7,1},{8,14},{9,15},{10,... | collective-permute-start | bytes 165896 | tf_op jit(solution)/shard_map/ppermute | solution.py:673
  44.2 4.4 %collective-permute-start.12 = (bf16[72,384]{1,0:T(8,128)(2,1)S(1)}, bf16[72,384]{1,0:T(8,128)(2,1)S(1)}, u32[]{:S(2)}, u32[]{:S(2)}) collective-permute-start(bf16[72,384]{1,0:T(8,128)(2,1)S(1)} %add_convert_fusion.1), channel_id=1, source_target_pairs={{0,2},{1,3},{2,0},{3,1},{4,6},{5,7},{6,4},{7,5},{8,10},{9,11},{10,... | collective-permute-start | bytes 165896 | tf_op jit(solution)/shard_map/ppermute | solution.py:673
  44.4 4.1 %collective-permute-start.11 = (bf16[72,384]{1,0:T(8,128)(2,1)S(1)}, bf16[72,384]{1,0:T(8,128)(2,1)S(1)}, u32[]{:S(2)}, u32[]{:S(2)}) collective-permute-start(bf16[72,384]{1,0:T(8,128)(2,1)S(1)} %add_convert_fusion.1), channel_id=1, source_target_pairs={{0,4},{1,5},{2,6},{3,7},{4,0},{5,1},{6,2},{7,3},{8,12},{9,13},{10,... | collective-permute-start | bytes 165896 | tf_op jit(solution)/shard_map/ppermute | solution.py:673
  48.6 3.3 %collective-permute-start.15 = (bf16[4,72,384]{2,1,0:T(8,128)(2,1)S(1)}, bf16[4,72,384]{2,1,0:T(8,128)(2,1)S(1)}, u32[]{:S(2)}, u32[]{:S(2)}) collective-permute-start(bf16[4,72,384]{2,1,0:T(8,128)(2,1)S(1)} %pad_maximum_fusion.1.here_ref), channel_id=1, source_target_pairs={{0,1},{1,0},{2,3},{3,2},{4,5},{5,4},{6,7},{7,6},{8,9},{9,8},{10,11... | collective-permute-start | bytes 663560 | tf_op jit(solution)/shard_map/ppermute | solution.py:673
  (6 other events, 56.8 us)

commit v4 on v3

--- a/solution.py
+++ b/solution.py
@@ -13,6 +13,7 @@
 LONG = 512
 ROWS_A = 64
 WIDE = GROUP * HEAD
+HALF = 256
 SHARE = 128
 CHUNK = 768
 SMALL = 8
@@ -72,6 +73,17 @@
 
 def far_place(chip):
     return pl.multiple_of(LONG_AT + 2 * SHARE * (1 - chip), 128)
+
+
+def near_places(block):
+    chip = block // 2
+    long_at = LONG_AT * (1 - chip)
+    short_at = LONG_AT * chip
+    outer = (block == 0) | (block == 3)
+    return (
+        pl.multiple_of(long_at, 128),
+        pl.multiple_of(jnp.where(outer, short_at, long_at), 128),
+    )
 
 
 def far_tokens(core, far_ref, far_mate_ref):
@@ -99,10 +111,10 @@
     return low, high
 
 
-def bias_of(len_ref, valid_ref, query_at, key_at, rows):
+def bias_of(len_ref, valid_ref, query_at, key_at, rows, columns=LONG):
     places = query_at + lax.broadcasted_iota(jnp.int32, (rows, 1), 0)
     low, high = bounds(len_ref, valid_ref, places)
-    keys = key_at + lax.broadcasted_iota(jnp.int32, (rows, LONG), 1)
+    keys = key_at + lax.broadcasted_iota(jnp.int32, (rows, columns), 1)
     return jnp.where((keys >= low) & (keys < high), 0.0, NEG)
 
 
@@ -142,10 +154,16 @@
     )
 
 
+def fetch_kernel(source, target, sem):
+    copy = pltpu.make_async_copy(source, target, sem)
+    copy.start()
+    copy.wait()
+
+
 def project_kernel(
     len_ref,
     valid_ref,
-    own_hbm,
+    own_ref,
     mate_ref,
     wq_hbm,
     wk_hbm,
@@ -159,16 +177,18 @@
     bias_b_ref,
     back_a_ref,
     back_b_ref,
+    near_a_ref,
+    near_b_ref,
+    far_a_ref,
+    far_b_ref,
     wq_ref,
     wk_ref,
     wv_ref,
     wout_ref,
     winner_ref,
-    own_ref,
     sems,
 ):
     moves = (
-        (own_hbm, own_ref),
         (wq_hbm, wq_ref),
         (wk_hbm, wk_ref),
         (wv_hbm, wv_ref),
@@ -193,34 +213,96 @@
     meet_b = partner_offset(block)
     bias_a_ref[...] = bias_of(len_ref, valid_ref, first + at_a, LONG_AT, ROWS_A)
     bias_b_ref[...] = bias_of(len_ref, valid_ref, first + at_b, meet_b, ROWS_B)
+    chip = block // 2
+    near_a, near_b = near_places(block)
+    pair_at = chip * 2 * rows
+    far_at = far_place(chip)
+    for at, count, near, near_ref, far_ref in (
+        (at_a, ROWS_A, near_a, near_a_ref, far_a_ref),
+        (at_b, ROWS_B, near_b, near_b_ref, far_b_ref),
+    ):
+        near_ref[...] = bias_of(len_ref, valid_ref, first + at, pair_at + near, count, HALF)
+        far_ref[...] = bias_of(len_ref, valid_ref, first + at, far_at, count, HALF)
     back_a_ref[...] = bias_back_of(len_ref, valid_ref, first + at_a, LONG_AT, ROWS_A)
     back_b_ref[...] = bias_back_of(len_ref, valid_ref, first + at_b, meet_b, ROWS_B)
     mine = pl.multiple_of(core * rows, rows)
     other = pl.multiple_of((1 - core) * rows, rows)
-    copies[0].wait()
     both = jnp.concatenate([own_ref[...], mate_ref[...]], axis=0)
     for copy, weight, out, scale in (
-        (copies[1], wq_ref, q_ref, 0.125),
-        (copies[2], wk_ref, k_ref, 1.0),
-        (copies[3], wv_ref, v_ref, 1.0),
+        (copies[0], wq_ref, q_ref, 0.125),
+        (copies[1], wk_ref, k_ref, 1.0),
+        (copies[2], wv_ref, v_ref, 1.0),
     ):
         copy.wait()
         product = (nn(both, weight[...]) * scale).astype(BF16)
         out[pl.ds(mine, rows), :] = product[:rows]
         out[pl.ds(other, rows), :] = product[rows:]
+    copies[3].wait()
     copies[4].wait()
-    copies[5].wait()
+
+
+def over_heads(stat):
+    count = stat.shape[0] // GROUP
+    parts = [stat[head * count : (head + 1) * count] for head in range(GROUP)]
+    left = lax.broadcasted_iota(jnp.int32, (1, 128), 1) < HEAD
+    return jnp.concatenate(
+        [jnp.where(left, parts[0], parts[1]), jnp.where(left, parts[2], parts[3])], axis=1
+    )
+
+
+def near_kernel(
+    far_ref,
+    q_ref,
+    kpair_ref,
+    vpair_ref,
+    near_a_ref,
+    near_b_ref,
+    wk_ref,
+    wv_ref,
+    kfar_ref,
+    vfar_ref,
+    sums_ref,
+    tops_ref,
+    totals_ref,
+):
+    kfar_ref[...] = nn(far_ref[...], wk_ref[...]).astype(BF16)
+    vfar_ref[...] = nn(far_ref[...], wv_ref[...]).astype(BF16)
+    block = lax.axis_index("blk")
+    rows, width = sums_ref.shape
+    core = block % 2
+    at_a, at_b = own_rows(block)
+    near_a, near_b = near_places(block)
+    for at, count, near, bias_ref, at_stat in (
+        (at_a, ROWS_A, near_a, near_a_ref, 0),
+        (at_b, ROWS_B, near_b, near_b_ref, GROUP * ROWS_A),
+    ):
+        stacked = pl.ds(at_stat, GROUP * count)
+        for group in range(width // WIDE):
+            columns = slice(group * WIDE, (group + 1) * WIDE)
+            queries = spread_heads(q_ref[pl.ds(core * rows + at, count), columns])
+            scores = masked(nt(queries, kpair_ref[pl.ds(near, HALF), columns]), bias_ref[...])
+            top = jnp.max(scores, axis=-1, keepdims=True)
+            weights = jnp.exp(scores - top)
+            total = jnp.sum(weights, axis=-1, keepdims=True)
+            sums = nn(weights.astype(BF16), vpair_ref[pl.ds(near, HALF), columns])
+            sums_ref[pl.ds(at, count), columns] = join_heads(sums)
+            tops_ref[group, stacked, :] = jnp.broadcast_to(top, (GROUP * count, 128))
+            totals_ref[group, stacked, :] = jnp.broadcast_to(total, (GROUP * count, 128))
 
 
 def main_kernel(
     own_ref,
-    far_ref,
     far_mate_ref,
     q_ref,
     kpair_ref,
     vpair_ref,
-    bias_a_ref,
-    bias_b_ref,
+    kfar_ref,
+    vfar_ref,
+    sums_ref,
+    tops_ref,
+    totals_ref,
+    far_a_ref,
+    far_b_ref,
     cot_ref,
     down1_ref,
     dbias1_ref,
@@ -245,7 +327,7 @@
     lse_ref,
     du1_ref,
     attended_ref,
-    dbranch_ref,
+    grad_pre_ref,
     keep_ref,
     send_ref,
     wouter_ref,
@@ -271,7 +353,6 @@
     chip = block // 2
     rows, width = own_ref.shape
     at_a, at_b = own_rows(block)
-    meet_b = partner_offset(block)
 
     def mine(ref):
         return jnp.concatenate([ref[pl.ds(at_a, ROWS_A), :], ref[pl.ds(at_b, ROWS_B), :]], axis=0)
@@ -283,33 +364,42 @@
     near = pl.multiple_of(chip * 2 * rows, 2 * rows)
     kbuf[pl.ds(near, 2 * rows), :] = kpair_ref[...]
     vbuf[pl.ds(near, 2 * rows), :] = vpair_ref[...]
-    far = far_tokens(core, far_ref, far_mate_ref)
-    kbuf[pl.ds(far_place(chip), 2 * SHARE), :] = nn(far, wk_ref[...]).astype(BF16)
-    vbuf[pl.ds(far_place(chip), 2 * SHARE), :] = nn(far, wv_ref[...]).astype(BF16)
+    far_at = far_place(chip)
+    far_first = pl.multiple_of(far_at + SHARE * core, 128)
+    far_second = pl.multiple_of(far_at + SHARE * (1 - core), 128)
+    kbuf[pl.ds(far_first, SHARE), :] = kfar_ref[...]
+    vbuf[pl.ds(far_first, SHARE), :] = vfar_ref[...]
+    kbuf[pl.ds(far_second, SHARE), :] = nn(far_mate_ref[...], wk_ref[...]).astype(BF16)
+    vbuf[pl.ds(far_second, SHARE), :] = nn(far_mate_ref[...], wv_ref[...]).astype(BF16)
 
     lane = lax.broadcasted_iota(jnp.int32, (1, 128), 1)
     attended_parts = []
     lse_parts = []
-    for at, count, meet, bias_ref in (
-        (at_a, ROWS_A, LONG_AT, bias_a_ref),
-        (at_b, ROWS_B, meet_b, bias_b_ref),
+    for at, count, bias_ref, at_stat in (
+        (at_a, ROWS_A, far_a_ref, 0),
+        (at_b, ROWS_B, far_b_ref, GROUP * ROWS_A),
     ):
         pieces = []
         lse = jnp.zeros((count, 128), F32)
-        for group in range(width // (GROUP * HEAD)):
-            columns = slice(group * GROUP * HEAD, (group + 1) * GROUP * HEAD)
+        stacked = pl.ds(at_stat, GROUP * count)
+        for group in range(width // WIDE):
+            columns = slice(group * WIDE, (group + 1) * WIDE)
             queries = spread_heads(q_ref[pl.ds(core * rows + at, count), columns])
-            scores = masked(nt(queries, kbuf[pl.ds(meet, LONG), columns]), bias_ref[...])
-            top = jnp.max(scores, axis=-1, keepdims=True)
-            weights = jnp.exp(scores - top)
-            total = jnp.sum(weights, axis=-1, keepdims=True)
-            mixed_values = nn(weights.astype(BF16), vbuf[pl.ds(meet, LONG), columns])
-            pieces.append(join_heads(mixed_values * (1.0 / total)))
+            scores = masked(nt(queries, kbuf[pl.ds(far_at, HALF), columns]), bias_ref[...])
+            top_near = tops_ref[group, stacked, :]
+            top = jnp.maximum(top_near, jnp.max(scores, axis=-1, keepdims=True))
+            weights = jnp.exp(scores - jnp.concatenate([top, top], axis=1))
+            shrink = jnp.exp(top_near - top)
+            total = shrink * totals_ref[group, stacked, :] + jnp.sum(
+                weights, axis=-1, keepdims=True
+            )
+            sums = join_heads(nn(weights.astype(BF16), vbuf[pl.ds(far_at, HALF), columns]))
+            sums = sums + sums_ref[pl.ds(at, count), columns] * over_heads(shrink)
+            pieces.append(sums * over_heads(1.0 / total))
             log_total = top + jnp.log(total)
             for head in range(GROUP):
-                lse = jnp.where(
-                    lane == group * GROUP + head, log_total[head * count : (head + 1) * count], lse
-                )
+                one = log_total[head * count : (head + 1) * count]
+                lse = jnp.where(lane == group * GROUP + head, one, lse)
         attended_parts.append(jnp.concatenate(pieces, axis=1))
         lse_parts.append(lse)
     attended_f = jnp.concatenate(attended_parts, axis=0)
@@ -353,19 +443,19 @@
     grad_shift2 = jnp.sum(cot, axis=0, keepdims=True)
     du2 = norm_back(cot, gain2, normal2, scale2)
 
-    def adapter_back(source, down, up, inner, slope, incoming):
+    def adapter_back(source, up, inner, slope, incoming):
         out_grad = incoming.astype(BF16)
         grad_up = tn(inner, out_grad)
         grad_ubias = jnp.sum(out_grad.astype(F32), axis=0, keepdims=True)
         grad_pre = (nt(out_grad, up) * slope).astype(BF16)
         grad_down = tn(grad_pre, source)
         grad_dbias = jnp.sum(grad_pre.astype(F32), axis=0, keepdims=True)
-        return nn(grad_pre, down), grad_down, grad_dbias, grad_up, grad_ubias
-
-    back2, grad_down2, grad_dbias2, grad_up2, grad_ubias2 = adapter_back(
-        ffn, down2_ref[...], up2_ref[...], inner2, slope2, du2
-    )
-    dffn = (du2 + back2).astype(BF16)
+        return grad_pre, grad_down, grad_dbias, grad_up, grad_ubias
+
+    grad_pre2, grad_down2, grad_dbias2, grad_up2, grad_ubias2 = adapter_back(
+        ffn, up2_ref[...], inner2, slope2, du2
+    )
+    dffn = (du2 + nn(grad_pre2, down2_ref[...])).astype(BF16)
     dmid = du2
     for at in range(0, hidden_units, CHUNK):
         dhidden = (nn(dffn, wouter_t_ref[:, at : at + CHUNK]) * slope_ref[:, at : at + CHUNK]).astype(
@@ -376,10 +466,11 @@
     grad_gain1 = jnp.sum(dmid * normal1, axis=0, keepdims=True)
     grad_shift1 = jnp.sum(dmid, axis=0, keepdims=True)
     du1 = norm_back(dmid, gain1, normal1, scale1)
-    back1, grad_down1, grad_dbias1, grad_up1, grad_ubias1 = adapter_back(
-        branch, down1_ref[...], up1_ref[...], inner1, slope1, du1
+    grad_pre1, grad_down1, grad_dbias1, grad_up1, grad_ubias1 = adapter_back(
+        branch, up1_ref[...], inner1, slope1, du1
     )
     put(du1_ref, du1)
+    put(grad_pre_ref, grad_pre1)
 
     blank = jnp.zeros((1, width), F32)
     both_dbias = jnp.concatenate(
@@ -397,28 +488,31 @@
         (grad_up2, grad_ubias2, blank),
         (grad_down2, grad_gain2, grad_shift2),
     )
-    for index, (matrix, one, two) in enumerate(quarters):
-        small = jnp.concatenate([one, two, jnp.zeros((SMALL - 2, width), F32)], axis=0)
-        whole = jnp.concatenate([matrix, small], axis=0).astype(BF16)
+    filler = jnp.zeros((SMALL - 2, width), F32)
+    wholes = [
+        jnp.concatenate([matrix, one, two, filler], axis=0).astype(BF16)
+        for matrix, one, two in quarters
+    ]
+    side_here = lax.axis_index("dp") % 2
+    for chip_of in range(2):
+        even, odd = wholes[2 * chip_of], wholes[2 * chip_of + 1]
+        kept = jnp.where(core == 0, even, odd)
+        sent = jnp.where(core == 0, odd, even)
         for side in range(2):
-            half = whole[:, side * width // 2 : (side + 1) * width // 2]
-            place = 2 * (chip ^ (index // 2)) + (lax.axis_index("dp") % 2 ^ side)
-
-            @pl.when(core == index % 2)
-            def _(place=place, half=half):
-                keep_ref[place] = half
-
-            @pl.when(core != index % 2)
-            def _(place=place, half=half):
-                send_ref[place] = half
-
-    put(dbranch_ref, (du1 + back1).astype(BF16))
+            half = slice(side * width // 2, (side + 1) * width // 2)
+            place = 2 * (chip ^ chip_of) + (side_here ^ side)
+            keep_ref[place] = kept[:, half]
+            send_ref[place] = sent[:, half]
+
     mixed_copy.wait()
 
 
-def attended_back_kernel(dbranch_ref, attended_ref, lse_ref, wout_ref, pack_ref, delta_ref):
-    rows, width = dbranch_ref.shape
-    dattended = nt(dbranch_ref[...], wout_ref[...]).astype(BF16)
+def attended_back_kernel(
+    du1_ref, grad_pre_ref, down1_ref, attended_ref, lse_ref, wout_ref, pack_ref, delta_ref
+):
+    rows, width = du1_ref.shape
+    dbranch = (du1_ref[...] + nn(grad_pre_ref[...], down1_ref[...])).astype(BF16)
+    dattended = nt(dbranch, wout_ref[...]).astype(BF16)
     pack_ref[:rows, :] = dattended
     product = dattended.astype(F32) * attended_ref[...]
     product_hi = product.astype(BF16)
@@ -476,6 +570,7 @@
         qbuf[pl.ds(far_place(chip), 2 * SHARE), :] = queries_far[
             :, index * WIDE : (index + 1) * WIDE
         ]
+    parts = []
     for at, count, meet, bias_ref in (
         (at_a, ROWS_A, LONG_AT, bias_a_ref),
         (at_b, ROWS_B, meet_b, bias_b_ref),
@@ -497,8 +592,11 @@
             )
             dscores = (probs * (dprobs - deltas)).astype(BF16)
             pieces.append(join_heads(nn(dscores, keys)).astype(BF16))
-        dquery = jnp.concatenate(pieces, axis=1)
-        part_ref[pl.ds(at, count), :] = part_in_ref[pl.ds(at, count), :] + nt(dquery, wq) * 0.125
+        parts.append(jnp.concatenate(pieces, axis=1))
+    added = nt(jnp.concatenate(parts, axis=0), wq) * 0.125
+    for at, rows_of in ((at_a, slice(0, ROWS_A)), (at_b, slice(ROWS_A, rows))):
+        place = pl.ds(at, rows_of.stop - rows_of.start)
+        part_ref[place, :] = part_in_ref[place, :] + added[rows_of]
 
 
 def gather_kernel(own_ref, mate_ref, far_ref, far_mate_ref, grads_ref, stats_ref):
@@ -548,6 +646,7 @@
     at_a, at_b = own_rows(block)
     first = block * rows
     all_columns = slice(groups[0] * WIDE, (groups[-1] + 1) * WIDE)
+    parts = []
     for at, count, meet, bias_ref, at_stats in (
         (at_a, ROWS_A, LONG_AT, back_a_ref, 0),
         (at_b, ROWS_B, partner_offset(block), back_b_ref, 32),
@@ -568,11 +667,12 @@
             dscores = (probs * dprobs).astype(BF16)
             dkeys.append(join_heads(nn(dscores, queries)).astype(BF16))
             dvalues.append(join_heads(nn(probs.astype(BF16), grads)).astype(BF16))
-        out_ref[pl.ds(at, count), :] = (
-            part_ref[pl.ds(at, count), :]
-            + nt(jnp.concatenate(dkeys, axis=1), wk_ref[:, all_columns])
-            + nt(jnp.concatenate(dvalues, axis=1), wv_ref[:, all_columns])
-        ).astype(out_ref.dtype)
+        parts.append((jnp.concatenate(dkeys, axis=1), jnp.concatenate(dvalues, axis=1)))
+    dkey, dvalue = (jnp.concatenate(both, axis=0) for both in zip(*parts))
+    added = nt(dkey, wk_ref[:, all_columns]) + nt(dvalue, wv_ref[:, all_columns])
+    for at, rows_of in ((at_a, slice(0, ROWS_A)), (at_b, slice(ROWS_A, rows))):
+        place = pl.ds(at, rows_of.stop - rows_of.start)
+        out_ref[place, :] = (part_ref[place, :] + added[rows_of]).astype(out_ref.dtype)
 
 
 def unpack_kernel(here_ref, other_ref, grad_ref, *refs):
@@ -675,6 +775,16 @@
         )
 
     mate = swap(own, 1)
+    own = pl.pallas_call(
+        fetch_kernel,
+        in_specs=[HBM],
+        out_specs=VMEM,
+        out_shape=vmem((rows, width), BF16),
+        scratch_shapes=[pltpu.SemaphoreType.DMA],
+        compiler_params=params(1),
+        cost_estimate=cost(0.1, 1.0),
+        name="fetch",
+    )(in_hbm(own))
     def near_share(own, mate):
         choices = (
             (own[128:192], own[64:128], own[:64], mate[128:192]),
@@ -689,6 +799,7 @@
         return halves
 
     far = swap(jnp.concatenate(near_share(own, mate), axis=0), 2)
+    half_mask_shapes = [vmem((count, HALF), F32) for count in (ROWS_A, ROWS_B)] * 2
     mask_shapes = [vmem((count, LONG), F32) for count in (ROWS_A, ROWS_B)] * 2
     (
         q,
@@ -698,6 +809,10 @@
         bias_b,
         back_a,
         back_b,
+        near_a,
+        near_b,
+        far_a,
+        far_b,
         wq_here,
         wk_here,
         wv_here,
@@ -705,20 +820,21 @@
         winner_here,
     ) = pl.pallas_call(
         project_kernel,
-        in_specs=[SMEM] * 2 + [HBM, VMEM] + [HBM] * 5,
-        out_specs=[VMEM] * 12,
+        in_specs=[SMEM] * 2 + [VMEM] * 2 + [HBM] * 5,
+        out_specs=[VMEM] * 16,
         out_shape=[vmem((2 * rows, width), BF16)] * 3
         + mask_shapes
+        + half_mask_shapes
         + [vmem((width, width), BF16)] * 4
         + [vmem((width, hidden), BF16)],
-        scratch_shapes=[pltpu.VMEM((rows, width), BF16), pltpu.SemaphoreType.DMA((6,))],
+        scratch_shapes=[pltpu.SemaphoreType.DMA((5,))],
         compiler_params=params(4),
         cost_estimate=cost(2.0, 12.0),
         name="project",
     )(
         in_hbm(seg_len),
         in_hbm(seg_valid),
-        in_hbm(own),
+        own,
         mate,
         in_hbm(w_query),
         in_hbm(w_key),
@@ -727,11 +843,22 @@
         in_hbm(w_inner),
     )
     far_mate = swap(after(far, q), 1)
+    kfar, vfar, sums, tops, totals = pl.pallas_call(
+        near_kernel,
+        in_specs=[VMEM] * 8,
+        out_specs=[VMEM] * 5,
+        out_shape=[vmem((SHARE, width), BF16)] * 2
+        + [vmem((rows, width), F32)]
+        + [vmem((width // WIDE, GROUP * rows, 128), F32)] * 2,
+        compiler_params=params(5),
+        cost_estimate=cost(1.0, 2.0),
+        name="near",
+    )(far, q, kpair, vpair, near_a, near_b, wk_here, wv_here)
 
     part_rows = adapt + SMALL
-    mixed, kbuf, vbuf, lse, du1, attended, dbranch, keep, send = pl.pallas_call(
+    mixed, kbuf, vbuf, lse, du1, attended, grad_pre, keep, send = pl.pallas_call(
         main_kernel,
-        in_specs=[VMEM] * 25 + [HBM],
+        in_specs=[VMEM] * 29 + [HBM],
         out_specs=[HBM] + [VMEM] * 8,
         out_shape=[
             shape((rows, width), BF16),
@@ -740,7 +867,7 @@
             vmem((rows, 128), F32),
             vmem((rows, width), F32),
             vmem((rows, width), F32),
-            vmem((rows, width), BF16),
+            vmem((rows, adapt), BF16),
             vmem((4, part_rows, width // 2), BF16),
             vmem((4, part_rows, width // 2), BF16),
         ],
@@ -752,18 +879,22 @@
             pltpu.VMEM((rows, width), BF16),
             pltpu.SemaphoreType.DMA((1 + hidden // CHUNK,)),
         ],
-        compiler_params=params(30),
+        compiler_params=params(22),
         cost_estimate=cost(8.0, 20.0),
         name="layer",
     )(
         own,
-        far,
         far_mate,
         q,
         kpair,
         vpair,
-        bias_a,
-        bias_b,
+        kfar,
+        vfar,
+        sums,
+        tops,
+        totals,
+        far_a,
+        far_b,
         cot,
         down_one.T,
         dbias_one,
@@ -789,13 +920,13 @@
 
     pack, delta = pl.pallas_call(
         attended_back_kernel,
-        in_specs=[VMEM] * 4,
+        in_specs=[VMEM] * 6,
         out_specs=[VMEM] * 2,
         out_shape=[vmem((rows + 32, width), BF16), vmem((rows, 128), F32)],
         compiler_params=params(5),
         cost_estimate=cost(0.5, 2.0),
         name="attended_back",
-    )(dbranch, attended, lse, wout_here)
+    )(du1, grad_pre, down_one.T, attended, lse, wout_here)
 
     def query_back(groups, part):
         return pl.pallas_call(

time: 53.4 us -> 51 us (0.955)
  waiting for transfers between devices: 3.79 us -> 2.46 us
  other arithmetic: 1.24 us -> 0.25 us
    ppermute x6, waiting for transfers between devices: 3.19 us -> 1.26 us  [swap(): return lax.ppermute(array, 'blk', [(i, i ^ mask) for i in range(4)])]
    pallas_call x3 -> x5, Pallas kernels: 16.6 us -> 17.9 us  [the longest x1 9.82 us: body(): pl.pallas_call(main_kernel, in_specs=[VMEM] * 29 + [HBM], out_specs=[HBM]...]
    select_n x2, other arithmetic: 1.04 us -> 0.05 us  [near_share(): half = jnp.where(block == index, options[index], half)]
    pallas_call x2, Pallas kernels: 4.72 us -> 4.04 us  [key_back(): pl.pallas_call(functools.partial(key_back_kernel, groups), in_specs=[VMEM...]
    pallas_call x2, Pallas kernels: 4.14 us -> 3.52 us  [query_back(): pl.pallas_call(functools.partial(query_back_kernel, groups), in_specs=[VM...]
    ppermute x10, waiting for transfers between devices: 0.6 us -> 1.19 us  [swap_all(): lax.ppermute(array, ('dp', 'blk'), [(i, i ^ mask) for i in range(4 * dp_s...]
  transfers between devices with their start and end apart: 16 -> 16, of which waited for: 6 -> 5; matrix products, arithmetic and copies ran while one was open for 0% -> 0% of each run, Pallas kernels for 27% -> 31%
where the time goes in v4:
time: 51 us; the launch traced here: 50.8 us
  Pallas kernels  26.8 us (53%)
  starting transfers between devices  20 us (39%)
  waiting for transfers between devices  2.46 us (5%)
  between operations  1.18 us (2%)
    ppermute x10, starting transfers between devices, swap_all(): lax.ppermute(array, ('dp', 'blk'), [(i, i ^ mask) for i in range(4 * dp_s...  11.1 us
    pallas_call x1, Pallas kernels, body(): pl.pallas_call(main_kernel, in_specs=[VMEM] * 29 + [HBM], out_specs=[HBM]...  9.82 us
    ppermute x6, starting transfers between devices, swap(): return lax.ppermute(array, 'blk', [(i, i ^ mask) for i in range(4)])  8.88 us
    pallas_call x1, Pallas kernels, body(): pl.pallas_call(project_kernel, in_specs=[SMEM] * 2 + [VMEM] * 2 + [HBM] *...  4.49 us
    pallas_call x2, Pallas kernels, key_back(): pl.pallas_call(functools.partial(key_back_kernel, groups), in_specs=[VMEM...  4.04 us
    pallas_call x2, Pallas kernels, query_back(): pl.pallas_call(functools.partial(query_back_kernel, groups), in_specs=[VM...  3.52 us
    pallas_call x1, Pallas kernels, body(): pl.pallas_call(near_kernel, in_specs=[VMEM] * 8, out_specs=[VMEM] * 5, ou...  1.54 us
    ppermute x6, waiting for transfers between devices, swap(): return lax.ppermute(array, 'blk', [(i, i ^ mask) for i in range(4)])  1.26 us
  transfers between devices with their start and end apart: 16, of which 5 were waited for; matrix products, arithmetic and copies ran while one was open for 0% of the time, Pallas kernels for 31%

profile of v4, /device:TPU:1, one launch (start us, length us, event | category | flops | bytes accessed | tf_op | source)
XLA Modules:
  0.0 50.8 jit_solution(6721946974874174419)
XLA Ops:
  0.8 1.0 %fetch.1.own_ref = bf16[192,768]{1,0:T(8,128)(2,1)S(1)} custom-call(bf16[192,768]{1,0:T(8,128)(2,1)} %bitcast.28), custom_call_target="tpu_custom_call" | custom-call | flops 100000000 | bytes 1000000 | tf_op jit(solution)/shard_map/fetch/pallas_call | solution.py:778
  1.7 0.8 %collective-permute-done.mate_ref = bf16[192,768]{1,0:T(8,128)(2,1)S(1)} collective-permute-done((bf16[192,768]{1,0:T(8,128)(2,1)}, bf16[192,768]{1,0:T(8,128)(2,1)S(1)}, u32[]{:S(2)}, u32[]{:S(2)}) %collective-permute-start) | collective-permute-done | bytes 294944 | tf_op jit(solution)/shard_map/ppermute | solution.py:770
  2.6 2.4 %collective-permute-start.1 = (bf16[128,768]{1,0:T(8,128)(2,1)S(1)}, bf16[128,768]{1,0:T(8,128)(2,1)S(1)}, u32[]{:S(2)}, u32[]{:S(2)}) collective-permute-start(bf16[128,768]{1,0:T(8,128)(2,1)S(1)} %pad_maximum_fusion.2), channel_id=1, source_target_pairs={{0,2},{1,3},{2,0},{3,1},{4,6},{5,7},{6,4},{7,5},{8,10},{9,11},{10,... | collective-permute-start | bytes 589832 | tf_op jit(solution)/shard_map/ppermute | solution.py:770
  5.0 4.5 %project.1 = (bf16[384,768]{1,0:T(8,128)(2,1)S(1)}, bf16[384,768]{1,0:T(8,128)(2,1)S(1)}, bf16[384,768]{1,0:T(8,128)(2,1)S(1)}, f32[64,512]{1,0:T(8,128)S(1)}, f...) custom-call(s32[1,6]{1,0:T(1,128)} %len_ref.1, ...), custom_call_target="tpu_custom_call" | custom-call | flops 2000000000 | bytes 12000000 | tf_op jit(solution)/shard_map/project/pallas_call | solution.py:821
  9.5 0.5 collective-permute-done.1.far_ref
  9.9 0.9 %collective-permute-start.2 = (bf16[128,768]{1,0:T(8,128)(2,1)S(1)}, bf16[128,768]{1,0:T(8,128)(2,1)S(1)}, u32[]{:S(2)}, u32[]{:S(2)}) collective-permute-start(bf16[128,768]{1,0:T(8,128)(2,1)S(1)} %collective-permute-done.1.far_ref), channel_id=1, source_target_pairs={{0,1},{1,0},{2,3},{3,2},{4,5},{5,4},{6,7},{7,6},{8,9},{9,8},{10,11... | collective-permute-start | bytes 589832 | tf_op jit(solution)/shard_map/ppermute | solution.py:770
  10.9 1.5 %near.1 = (bf16[128,768]{1,0:T(8,128)(2,1)S(1)}, bf16[128,768]{1,0:T(8,128)(2,1)S(1)}, f32[192,768]{1,0:T(8,128)S(1)}, f32[3,768,128]{2,1,0:T(8,128)S(1)}, f32[3,768,128]{2,1,0:T(8,128)S(1)}) custom-call(bf16[128,768]{1,0:T(8,128)(2,1)S(1)} %collective-permute-done.1.far_ref, bf16[384,768]{1,0:T(8,128)(2,1)S(1)} %get-tuple-element.84.q_ref, ...), custom_call_target="tpu_custom_call" | custom-call | flops 1000000000 | bytes 2000000 | tf_op jit(solution)/shard_map/near/pallas_call | solution.py:846
  12.6 9.8 %layer.1 = (bf16[192,768]{1,0:T(8,128)(2,1)}, bf16[768,768]{1,0:T(8,128)(2,1)S(1)}, bf16[768,768]{1,0:T(8,128)(2,1)S(1)}, f32[192,128]{1,0:T(8,128)S(1)}, f32[19...) custom-call(bf16[192,768]{1,0:T(8,128)(2,1)S(1)} %fetch.1.own_ref, ...), custom_call_target="tpu_custom_call" | custom-call | flops 8000000000 | bytes 20000000 | tf_op jit(solution)/shard_map/layer/pallas_call | solution.py:859
  22.5 1.1 %attended_back.1 = (bf16[224,768]{1,0:T(8,128)(2,1)S(1)}, f32[192,128]{1,0:T(8,128)S(1)}) custom-call(f32[192,768]{1,0:T(8,128)S(1)} %get-tuple-element.115.du1_ref.part_in_ref, bf16[192,64]{1,0:T(8,128)(2,1)S(1)} %get-tuple-element.105.grad_pre_ref, bf16[64,768]{1,0:T(8,128)(2,1)S(1)} %bitcast.24, f32[192,768]{1,0:T(8,128)S(1)} %get-tuple-element.106.attended_ref, ...), custom_call_target="tpu_custom_call" | custom-call | flops 500000000 | bytes 2000000 | tf_op jit(solution)/shard_map/attended_back/pallas_call | solution.py:921
  24.3 2.5 %collective-permute-start.6 = (bf16[72,384]{1,0:T(8,128)(2,1)S(1)}, bf16[72,384]{1,0:T(8,128)(2,1)S(1)}, u32[]{:S(2)}, u32[]{:S(2)}) collective-permute-start(bf16[72,384]{1,0:T(8,128)(2,1)S(1)} %get-tuple-element.158), channel_id=1, source_target_pairs={{0,6},{1,7},{2,4},{3,5},{4,2},{5,3},{6,0},{7,1},{8,14},{9,15},{10,... | collective-permute-start | bytes 165896 | tf_op jit(solution)/shard_map/ppermute | solution.py:773
  27.2 2.0 %query_back_0.1 = (bf16[768,256]{1,0:T(8,128)(2,1)S(1)}, bf16[768,256]{1,0:T(8,128)(2,1)S(1)}, f32[192,768]{1,0:T(8,128)S(1)}) custom-call(bf16[128,768]{1,0:T(8,128)(2,1)S(1)} %collective-permute-done.1.far_ref, bf16[128,768]{1,0:T(8,128)(2,1)S(1)} %collective-permute-done.2.far_mate_ref, bf16[384,768]{1,0:T(8,128)(2,1)S(1)} %get-tuple-element.84.q_ref, ...), custom_call_target="tpu_custom_call" | custom-call | flops 2000000000 | bytes 3000000 | tf_op jit(solution)/shard_map/query_back_0/pallas_call | solution.py:932
  29.2 0.8 %collective-permute-done.5 = bf16[72,384]{1,0:T(8,128)(2,1)S(1)} collective-permute-done((bf16[72,384]{1,0:T(8,128)(2,1)S(1)}, bf16[72,384]{1,0:T(8,128)(2,1)S(1)}, u32[]{:S(2)}, u32[]{:S(2)}) %collective-permute-start.5) | collective-permute-done | bytes 55328 | tf_op jit(solution)/shard_map/ppermute | solution.py:773
  30.1 1.4 %collective-permute-start.8 = (bf16[72,384]{1,0:T(8,128)(2,1)S(1)}, bf16[72,384]{1,0:T(8,128)(2,1)S(1)}, u32[]{:S(2)}, u32[]{:S(2)}) collective-permute-start(bf16[72,384]{1,0:T(8,128)(2,1)S(1)} %fusion.2), channel_id=1, source_target_pairs={{0,8},{1,9},{2,10},{3,11},{4,12},{5,13},{6,14},{7,15},{8,0},{9,1},... | collective-permute-start | bytes 165896 | tf_op jit(solution)/shard_map/ppermute | solution.py:773
  31.6 1.7 %collective-permute-start.10 = (bf16[160,768]{1,0:T(8,128)(2,1)S(1)}, bf16[160,768]{1,0:T(8,128)(2,1)S(1)}, u32[]{:S(2)}, u32[]{:S(2)}) collective-permute-start(bf16[160,768]{1,0:T(8,128)(2,1)S(1)} %pad_maximum_fusion), channel_id=1, source_target_pairs={{0,2},{1,3},{2,0},{3,1},{4,6},{5,7},{6,4},{7,5},{8,10},{9,11},{10,... | collective-permute-start | bytes 737288 | tf_op jit(solution)/shard_map/ppermute | solution.py:770
  33.3 2.4 %collective-permute-start.9 = (bf16[72,384]{1,0:T(8,128)(2,1)S(1)}, bf16[72,384]{1,0:T(8,128)(2,1)S(1)}, u32[]{:S(2)}, u32[]{:S(2)}) collective-permute-start(bf16[72,384]{1,0:T(8,128)(2,1)S(1)} %add_convert_fusion.2), channel_id=1, source_target_pairs={{0,16},{1,17},{2,18},{3,19},{4,20},{5,21},{6,22},{7,23},{8,24},{9,... | collective-permute-start | bytes 165896 | tf_op jit(solution)/shard_map/ppermute | solution.py:773
  35.7 1.5 %query_back_2.1 = (bf16[768,256]{1,0:T(8,128)(2,1)S(1)}, f32[192,768]{1,0:T(8,128)S(1)}) custom-call(bf16[128,768]{1,0:T(8,128)(2,1)S(1)} %collective-permute-done.1.far_ref, bf16[128,768]{1,0:T(8,128)(2,1)S(1)} %collective-permute-done.2.far_mate_ref, bf16[384,768]{1,0:T(8,128)(2,1)S(1)} %get-tuple-element.84.q_ref, ...), custom_call_target="tpu_custom_call" | custom-call | flops 1000000000 | bytes 3000000 | tf_op jit(solution)/shard_map/query_back_2/pallas_call | solution.py:932
  37.2 3.5 %collective-permute-start.14 = (bf16[160,768]{1,0:T(8,128)(2,1)S(1)}, bf16[160,768]{1,0:T(8,128)(2,1)S(1)}, u32[]{:S(2)}, u32[]{:S(2)}) collective-permute-start(bf16[160,768]{1,0:T(8,128)(2,1)S(1)} %collective-permute-done.10.far_ref), channel_id=1, source_target_pairs={{0,1},{1,0},{2,3},{3,2},{4,5},{5,4},{6,7},{7,6},{8,9},{9,8},{10,11... | collective-permute-start | bytes 737288 | tf_op jit(solution)/shard_map/ppermute | solution.py:770
  40.8 1.2 %collective-permute-start.13 = (bf16[72,384]{1,0:T(8,128)(2,1)S(1)}, bf16[72,384]{1,0:T(8,128)(2,1)S(1)}, u32[]{:S(2)}, u32[]{:S(2)}) collective-permute-start(bf16[72,384]{1,0:T(8,128)(2,1)S(1)} %add_convert_fusion.1), channel_id=1, source_target_pairs={{0,6},{1,7},{2,4},{3,5},{4,2},{5,3},{6,0},{7,1},{8,14},{9,15},{10,... | collective-permute-start | bytes 165896 | tf_op jit(solution)/shard_map/ppermute | solution.py:773
  42.0 0.4 collective-permute-start.12
  42.4 1.0 %collective-permute-start.11 = (bf16[72,384]{1,0:T(8,128)(2,1)S(1)}, bf16[72,384]{1,0:T(8,128)(2,1)S(1)}, u32[]{:S(2)}, u32[]{:S(2)}) collective-permute-start(bf16[72,384]{1,0:T(8,128)(2,1)S(1)} %add_convert_fusion.1), channel_id=1, source_target_pairs={{0,4},{1,5},{2,6},{3,7},{4,0},{5,1},{6,2},{7,3},{8,12},{9,13},{10,... | collective-permute-start | bytes 165896 | tf_op jit(solution)/shard_map/ppermute | solution.py:773
  43.7 2.6 %key_back_0.1.part_ref = f32[192,768]{1,0:T(8,128)S(1)} custom-call(bf16[768,768]{1,0:T(8,128)(2,1)S(1)} %get-tuple-element.129.grads_ref, f32[64,512]{1,0:T(8,128)S(1)} %get-tuple-element.130.stats_ref, bf16[768,768]{1,0:T(8,128)(2,1)S(1)} %get-tuple-element.110.kbuf, bf16[768,768]{1,0:T(8,128)(2,1)S(1)} %get-tuple-element.111.vbuf, ...), custom_call_target="tpu_custom_call" | custom-call | flops 2000000000 | bytes 3000000 | tf_op jit(solution)/shard_map/key_back_0/pallas_call | solution.py:943
  46.3 1.7 %collective-permute-start.15 = (bf16[4,72,384]{2,1,0:T(8,128)(2,1)S(1)}, bf16[4,72,384]{2,1,0:T(8,128)(2,1)S(1)}, u32[]{:S(2)}, u32[]{:S(2)}) collective-permute-start(bf16[4,72,384]{2,1,0:T(8,128)(2,1)S(1)} %pad_maximum_fusion.1.here_ref), channel_id=1, source_target_pairs={{0,1},{1,0},{2,3},{3,2},{4,5},{5,4},{6,7},{7,6},{8,9},{9,8},{10,11... | collective-permute-start | bytes 663560 | tf_op jit(solution)/shard_map/ppermute | solution.py:773
  48.0 1.5 %key_back_2.1.grad_ref = bf16[192,768]{1,0:T(8,128)(2,1)S(1)} custom-call(bf16[768,768]{1,0:T(8,128)(2,1)S(1)} %get-tuple-element.129.grads_ref, f32[64,512]{1,0:T(8,128)S(1)} %get-tuple-element.130.stats_ref, bf16[768,768]{1,0:T(8,128)(2,1)S(1)} %get-tuple-element.110.kbuf, bf16[768,768]{1,0:T(8,128)(2,1)S(1)} %get-tuple-element.111.vbuf, ...), custom_call_target="tpu_custom_call" | custom-call | flops 1000000000 | bytes 3000000 | tf_op jit(solution)/shard_map/key_back_2/pallas_call | solution.py:943
  49.5 1.1 %unpack.1 = (bf16[192,768]{1,0:T(8,128)(2,1)}, f32[64,768]{1,0:T(8,128)}, f32[64]{0:T(128)}, f32[64,768]{1,0:T(8,128)}, f32[768]{0:T(1024)}, /*index=5*/f32[768]...) custom-call(bf16[4,72,384]{2,1,0:T(8,128)(2,1)S(1)} %pad_maximum_fus, ...), custom_call_target="tpu_custom_call" | custom-call | tf_op jit(solution)/shard_map/unpack/pallas_call | solution.py:989
  (56 shorter events, 1.8 us)
Async XLA Ops:
  0.6 1.9 %collective-permute-start = (bf16[192,768]{1,0:T(8,128)(2,1)}, bf16[192,768]{1,0:T(8,128)(2,1)S(1)}, u32[]{:S(2)}, u32[]{:S(2)}) collective-permute-start(bf16[192,768]{1,0:T(8,128)(2,1)} %bitcast.27), channel_id=1, source_target_pairs={{0,1},{1,0},{2,3},{3,2},{4,5},{5,4},{6,7},{7,6},{8,9},{9,8},{10,11... | collective-permute-start | bytes 884744 | tf_op jit(solution)/shard_map/ppermute | solution.py:770
  2.6 7.4 %collective-permute-start.1 = (bf16[128,768]{1,0:T(8,128)(2,1)S(1)}, bf16[128,768]{1,0:T(8,128)(2,1)S(1)}, u32[]{:S(2)}, u32[]{:S(2)}) collective-permute-start(bf16[128,768]{1,0:T(8,128)(2,1)S(1)} %pad_maximum_fusion.2), channel_id=1, source_target_pairs={{0,2},{1,3},{2,0},{3,1},{4,6},{5,7},{6,4},{7,5},{8,10},{9,11},{10,... | collective-permute-start | bytes 589832 | tf_op jit(solution)/shard_map/ppermute | solution.py:770
  9.9 2.6 %collective-permute-start.2 = (bf16[128,768]{1,0:T(8,128)(2,1)S(1)}, bf16[128,768]{1,0:T(8,128)(2,1)S(1)}, u32[]{:S(2)}, u32[]{:S(2)}) collective-permute-start(bf16[128,768]{1,0:T(8,128)(2,1)S(1)} %collective-permute-done.1.far_ref), channel_id=1, source_target_pairs={{0,1},{1,0},{2,3},{3,2},{4,5},{5,4},{6,7},{7,6},{8,9},{9,8},{10,11... | collective-permute-start | bytes 589832 | tf_op jit(solution)/shard_map/ppermute | solution.py:770
  10.8 1.7 %copy-start.3 = (bf16[768,64]{0,1:T(8,128)(2,1)S(1)}, bf16[768,64]{0,1:T(8,128)(2,1)}, u32[]{:S(2)}) copy-start(bf16[768,64]{0,1:T(8,128)(2,1)} %param.35) | copy-start | bytes 294916
  10.8 1.7 %copy-start.4 = (bf16[64,768]{1,0:T(8,128)(2,1)S(1)}, bf16[64,768]{1,0:T(8,128)(2,1)}, u32[]{:S(2)}) copy-start(bf16[64,768]{1,0:T(8,128)(2,1)} %up2_ref.1) | copy-start | bytes 294916
  10.8 1.7 %copy-start.5 = (f32[768]{0:T(1024)S(1)}, f32[768]{0:T(1024)}, u32[]{:S(2)}) copy-start(f32[768]{0:T(1024)} %ubias1_ref.1) | copy-start | bytes 9220
  10.9 1.7 %copy-start.6 = (f32[768]{0:T(1024)S(1)}, f32[768]{0:T(1024)}, u32[]{:S(2)}) copy-start(f32[768]{0:T(1024)} %gain1_ref.1) | copy-start | bytes 9220
  10.9 1.7 %copy-start.7 = (f32[768]{0:T(1024)S(1)}, f32[768]{0:T(1024)}, u32[]{:S(2)}) copy-start(f32[768]{0:T(1024)} %shift1_ref.1) | copy-start | bytes 9220
  10.9 1.7 %copy-start.8 = (f32[768]{0:T(1024)S(1)}, f32[768]{0:T(1024)}, u32[]{:S(2)}) copy-start(f32[768]{0:T(1024)} %ubias2_ref.1) | copy-start | bytes 9220
  10.9 1.7 %copy-start.9 = (f32[768]{0:T(1024)S(1)}, f32[768]{0:T(1024)}, u32[]{:S(2)}) copy-start(f32[768]{0:T(1024)} %gain2_ref.1) | copy-start | bytes 9220
  10.9 1.7 %copy-start.10 = (f32[768]{0:T(1024)S(1)}, f32[768]{0:T(1024)}, u32[]{:S(2)}) copy-start(f32[768]{0:T(1024)} %shift2_ref.1) | copy-start | bytes 9220
  22.5 1.5 %collective-permute-start.3 = (bf16[4,72,384]{2,1,0:T(8,128)(2,1)S(1)}, bf16[4,72,384]{2,1,0:T(8,128)(2,1)S(1)}, u32[]{:S(2)}, u32[]{:S(2)}) collective-permute-start(bf16[4,72,384]{2,1,0:T(8,128)(2,1)S(1)} %get-tuple-element.103), channel_id=1, source_target_pairs={{0,1},{1,0},{2,3},{3,2},{4,5},{5,4},{6,7},{7,6},{8,9},{9,8},{10,11... | collective-permute-start | bytes 663560 | tf_op jit(solution)/shard_map/ppermute | solution.py:773
  24.1 6.0 %collective-permute-start.7 = (bf16[224,768]{1,0:T(8,128)(2,1)S(1)}, bf16[224,768]{1,0:T(8,128)(2,1)S(1)}, u32[]{:S(2)}, u32[]{:S(2)}) collective-permute-start(bf16[224,768]{1,0:T(8,128)(2,1)S(1)} %get-tuple-element.122.pack_ref.own_ref), channel_id=1, source_target_pairs={{0,1},{1,0},{2,3},{3,2},{4,5},{5,4},{6,7},{7,6},{8,9},{9,8},{10,11... | collective-permute-start | bytes 1032200 | tf_op jit(solution)/shard_map/ppermute | solution.py:770
  24.3 4.9 %collective-permute-start.6 = (bf16[72,384]{1,0:T(8,128)(2,1)S(1)}, bf16[72,384]{1,0:T(8,128)(2,1)S(1)}, u32[]{:S(2)}, u32[]{:S(2)}) collective-permute-start(bf16[72,384]{1,0:T(8,128)(2,1)S(1)} %get-tuple-element.158), channel_id=1, source_target_pairs={{0,6},{1,7},{2,4},{3,5},{4,2},{5,3},{6,0},{7,1},{8,14},{9,15},{10,... | collective-permute-start | bytes 165896 | tf_op jit(solution)/shard_map/ppermute | solution.py:773
  26.8 3.2 %collective-permute-start.5 = (bf16[72,384]{1,0:T(8,128)(2,1)S(1)}, bf16[72,384]{1,0:T(8,128)(2,1)S(1)}, u32[]{:S(2)}, u32[]{:S(2)}) collective-permute-start(bf16[72,384]{1,0:T(8,128)(2,1)S(1)} %get-tuple-element.159), channel_id=1, source_target_pairs={{0,2},{1,3},{2,0},{3,1},{4,6},{5,7},{6,4},{7,5},{8,10},{9,11},{10,... | collective-permute-start | bytes 165896 | tf_op jit(solution)/shard_map/ppermute | solution.py:773
  27.1 3.0 %collective-permute-start.4 = (bf16[72,384]{1,0:T(8,128)(2,1)S(1)}, bf16[72,384]{1,0:T(8,128)(2,1)S(1)}, u32[]{:S(2)}, u32[]{:S(2)}) collective-permute-start(bf16[72,384]{1,0:T(8,128)(2,1)S(1)} %get-tuple-element.160), channel_id=1, source_target_pairs={{0,4},{1,5},{2,6},{3,7},{4,0},{5,1},{6,2},{7,3},{8,12},{9,13},{10,... | collective-permute-start | bytes 165896 | tf_op jit(solution)/shard_map/ppermute | solution.py:773
  30.1 3.2 %collective-permute-start.8 = (bf16[72,384]{1,0:T(8,128)(2,1)S(1)}, bf16[72,384]{1,0:T(8,128)(2,1)S(1)}, u32[]{:S(2)}, u32[]{:S(2)}) collective-permute-start(bf16[72,384]{1,0:T(8,128)(2,1)S(1)} %fusion.2), channel_id=1, source_target_pairs={{0,8},{1,9},{2,10},{3,11},{4,12},{5,13},{6,14},{7,15},{8,0},{9,1},... | collective-permute-start | bytes 165896 | tf_op jit(solution)/shard_map/ppermute | solution.py:773
  31.6 5.6 %collective-permute-start.10 = (bf16[160,768]{1,0:T(8,128)(2,1)S(1)}, bf16[160,768]{1,0:T(8,128)(2,1)S(1)}, u32[]{:S(2)}, u32[]{:S(2)}) collective-permute-start(bf16[160,768]{1,0:T(8,128)(2,1)S(1)} %pad_maximum_fusion), channel_id=1, source_target_pairs={{0,2},{1,3},{2,0},{3,1},{4,6},{5,7},{6,4},{7,5},{8,10},{9,11},{10,... | collective-permute-start | bytes 737288 | tf_op jit(solution)/shard_map/ppermute | solution.py:770
  33.3 7.4 %collective-permute-start.9 = (bf16[72,384]{1,0:T(8,128)(2,1)S(1)}, bf16[72,384]{1,0:T(8,128)(2,1)S(1)}, u32[]{:S(2)}, u32[]{:S(2)}) collective-permute-start(bf16[72,384]{1,0:T(8,128)(2,1)S(1)} %add_convert_fusion.2), channel_id=1, source_target_pairs={{0,16},{1,17},{2,18},{3,19},{4,20},{5,21},{6,22},{7,23},{8,24},{9,... | collective-permute-start | bytes 165896 | tf_op jit(solution)/shard_map/ppermute | solution.py:773
  37.2 6.3 %collective-permute-start.14 = (bf16[160,768]{1,0:T(8,128)(2,1)S(1)}, bf16[160,768]{1,0:T(8,128)(2,1)S(1)}, u32[]{:S(2)}, u32[]{:S(2)}) collective-permute-start(bf16[160,768]{1,0:T(8,128)(2,1)S(1)} %collective-permute-done.10.far_ref), channel_id=1, source_target_pairs={{0,1},{1,0},{2,3},{3,2},{4,5},{5,4},{6,7},{7,6},{8,9},{9,8},{10,11... | collective-permute-start | bytes 737288 | tf_op jit(solution)/shard_map/ppermute | solution.py:770
  40.8 5.5 %collective-permute-start.13 = (bf16[72,384]{1,0:T(8,128)(2,1)S(1)}, bf16[72,384]{1,0:T(8,128)(2,1)S(1)}, u32[]{:S(2)}, u32[]{:S(2)}) collective-permute-start(bf16[72,384]{1,0:T(8,128)(2,1)S(1)} %add_convert_fusion.1), channel_id=1, source_target_pairs={{0,6},{1,7},{2,4},{3,5},{4,2},{5,3},{6,0},{7,1},{8,14},{9,15},{10,... | collective-permute-start | bytes 165896 | tf_op jit(solution)/shard_map/ppermute | solution.py:773
  42.0 4.3 %collective-permute-start.12 = (bf16[72,384]{1,0:T(8,128)(2,1)S(1)}, bf16[72,384]{1,0:T(8,128)(2,1)S(1)}, u32[]{:S(2)}, u32[]{:S(2)}) collective-permute-start(bf16[72,384]{1,0:T(8,128)(2,1)S(1)} %add_convert_fusion.1), channel_id=1, source_target_pairs={{0,2},{1,3},{2,0},{3,1},{4,6},{5,7},{6,4},{7,5},{8,10},{9,11},{10,... | collective-permute-start | bytes 165896 | tf_op jit(solution)/shard_map/ppermute | solution.py:773
  42.4 3.9 %collective-permute-start.11 = (bf16[72,384]{1,0:T(8,128)(2,1)S(1)}, bf16[72,384]{1,0:T(8,128)(2,1)S(1)}, u32[]{:S(2)}, u32[]{:S(2)}) collective-permute-start(bf16[72,384]{1,0:T(8,128)(2,1)S(1)} %add_convert_fusion.1), channel_id=1, source_target_pairs={{0,4},{1,5},{2,6},{3,7},{4,0},{5,1},{6,2},{7,3},{8,12},{9,13},{10,... | collective-permute-start | bytes 165896 | tf_op jit(solution)/shard_map/ppermute | solution.py:773
  46.3 3.1 %collective-permute-start.15 = (bf16[4,72,384]{2,1,0:T(8,128)(2,1)S(1)}, bf16[4,72,384]{2,1,0:T(8,128)(2,1)S(1)}, u32[]{:S(2)}, u32[]{:S(2)}) collective-permute-start(bf16[4,72,384]{2,1,0:T(8,128)(2,1)S(1)} %pad_maximum_fusion.1.here_ref), channel_id=1, source_target_pairs={{0,1},{1,0},{2,3},{3,2},{4,5},{5,4},{6,7},{7,6},{8,9},{9,8},{10,11... | collective-permute-start | bytes 663560 | tf_op jit(solution)/shard_map/ppermute | solution.py:773
  (5 other events, 8.5 us)

commit v5 on v4

--- a/solution.py
+++ b/solution.py
@@ -170,6 +170,28 @@
     wv_hbm,
     wout_hbm,
     winner_hbm,
+    *refs,
+):
+    rest = (len(refs) - 17) // 2
+    smalls_hbm, refs, sems = refs[:rest], refs[rest:-1], refs[-1]
+    project_rows(
+        len_ref,
+        valid_ref,
+        own_ref,
+        mate_ref,
+        (wq_hbm, wk_hbm, wv_hbm, wout_hbm, winner_hbm),
+        *refs[:16],
+        tuple(zip(smalls_hbm, refs[16:])),
+        sems,
+    )
+
+
+def project_rows(
+    len_ref,
+    valid_ref,
+    own_ref,
+    mate_ref,
+    weights_hbm,
     q_ref,
     k_ref,
     v_ref,
@@ -186,15 +208,11 @@
     wv_ref,
     wout_ref,
     winner_ref,
+    smalls,
     sems,
 ):
-    moves = (
-        (wq_hbm, wq_ref),
-        (wk_hbm, wk_ref),
-        (wv_hbm, wv_ref),
-        (wout_hbm, wout_ref),
-        (winner_hbm, winner_ref),
-    )
+    weights = (wq_ref, wk_ref, wv_ref, wout_ref, winner_ref)
+    moves = tuple(zip(weights_hbm, weights)) + smalls
     copies = [
         pltpu.make_async_copy(source, target, sems.at[index])
         for index, (source, target) in enumerate(moves)
@@ -237,8 +255,8 @@
         product = (nn(both, weight[...]) * scale).astype(BF16)
         out[pl.ds(mine, rows), :] = product[:rows]
         out[pl.ds(other, rows), :] = product[rows:]
-    copies[3].wait()
-    copies[4].wait()
+    for copy in copies[3:]:
+        copy.wait()
 
 
 def over_heads(stat):
@@ -799,6 +817,21 @@
         return halves
 
     far = swap(jnp.concatenate(near_share(own, mate), axis=0), 2)
+    smalls = (
+        cot,
+        down_one.T,
+        dbias_one,
+        up_one,
+        ubias_one,
+        gain_one,
+        shift_one,
+        down_two.T,
+        dbias_two,
+        up_two,
+        ubias_two,
+        gain_two,
+        shift_two,
+    )
     half_mask_shapes = [vmem((count, HALF), F32) for count in (ROWS_A, ROWS_B)] * 2
     mask_shapes = [vmem((count, LONG), F32) for count in (ROWS_A, ROWS_B)] * 2
     (
@@ -818,16 +851,18 @@
         wv_here,
         wout_here,
         winner_here,
+        *smalls_here,
     ) = pl.pallas_call(
         project_kernel,
-        in_specs=[SMEM] * 2 + [VMEM] * 2 + [HBM] * 5,
-        out_specs=[VMEM] * 16,
+        in_specs=[SMEM] * 2 + [VMEM] * 2 + [HBM] * (5 + len(smalls)),
+        out_specs=[VMEM] * (16 + len(smalls)),
         out_shape=[vmem((2 * rows, width), BF16)] * 3
         + mask_shapes
         + half_mask_shapes
         + [vmem((width, width), BF16)] * 4
-        + [vmem((width, hidden), BF16)],
-        scratch_shapes=[pltpu.SemaphoreType.DMA((5,))],
+        + [vmem((width, hidden), BF16)]
+        + [vmem(small.shape, small.dtype) for small in smalls],
+        scratch_shapes=[pltpu.SemaphoreType.DMA((5 + len(smalls),))],
         compiler_params=params(4),
         cost_estimate=cost(2.0, 12.0),
         name="project",
@@ -841,6 +876,7 @@
         in_hbm(w_value),
         in_hbm(w_out),
         in_hbm(w_inner),
+        *(in_hbm(small) for small in smalls),
     )
     far_mate = swap(after(far, q), 1)
     kfar, vfar, sums, tops, totals = pl.pallas_call(
@@ -895,19 +931,7 @@
         totals,
         far_a,
         far_b,
-        cot,
-        down_one.T,
-        dbias_one,
-        up_one,
-        ubias_one,
-        gain_one,
-        shift_one,
-        down_two.T,
-        dbias_two,
-        up_two,
-        ubias_two,
-        gain_two,
-        shift_two,
+        *smalls_here,
         wk_here,
         wv_here,
         wout_here,
@@ -926,7 +950,7 @@
         compiler_params=params(5),
         cost_estimate=cost(0.5, 2.0),
         name="attended_back",
-    )(du1, grad_pre, down_one.T, attended, lse, wout_here)
+    )(du1, grad_pre, smalls_here[1], attended, lse, wout_here)
 
     def query_back(groups, part):
         return pl.pallas_call(

time: 51 us -> 50.7 us (level)
  transfers between devices with their start and end apart: 16 -> 16, of which waited for: 5 -> 5; matrix products, arithmetic and copies ran while one was open for 0% -> 0% of each run, Pallas kernels for 31% -> 32%
where the time goes in v5:
time: 50.7 us; the launch traced here: 50.5 us
  Pallas kernels  27 us (53%)
  starting transfers between devices  20 us (39%)
  waiting for transfers between devices  2.27 us (4%)
  between operations  1.01 us (2%)
    ppermute x10, starting transfers between devices, swap_all(): lax.ppermute(array, ('dp', 'blk'), [(i, i ^ mask) for i in range(4 * dp_s...  11.1 us
    pallas_call x1, Pallas kernels, body(): pl.pallas_call(main_kernel, in_specs=[VMEM] * 29 + [HBM], out_specs=[HBM]...  9.83 us
    ppermute x6, starting transfers between devices, swap(): return lax.ppermute(array, 'blk', [(i, i ^ mask) for i in range(4)])  8.87 us
    pallas_call x1, Pallas kernels, body(): pl.pallas_call(project_kernel, in_specs=[SMEM] * 2 + [VMEM] * 2 + [HBM] *...  4.69 us
    pallas_call x2, Pallas kernels, key_back(): pl.pallas_call(functools.partial(key_back_kernel, groups), in_specs=[VMEM...  4.04 us
    pallas_call x2, Pallas kernels, query_back(): pl.pallas_call(functools.partial(query_back_kernel, groups), in_specs=[VM...  3.53 us
    pallas_call x1, Pallas kernels, body(): pl.pallas_call(near_kernel, in_specs=[VMEM] * 8, out_specs=[VMEM] * 5, ou...  1.54 us
    ppermute x10, waiting for transfers between devices, swap_all(): lax.ppermute(array, ('dp', 'blk'), [(i, i ^ mask) for i in range(4 * dp_s...  1.18 us
  transfers between devices with their start and end apart: 16, of which 5 were waited for; matrix products, arithmetic and copies ran while one was open for 0% of the time, Pallas kernels for 32%

profile of v5, /device:TPU:1, one launch (start us, length us, event | category | flops | bytes accessed | tf_op | source)
XLA Modules:
  0.0 50.5 jit_solution(4635079103860069301)
XLA Ops:
  0.8 1.0 %fetch.1.own_ref = bf16[192,768]{1,0:T(8,128)(2,1)S(1)} custom-call(bf16[192,768]{1,0:T(8,128)(2,1)} %bitcast.25), custom_call_target="tpu_custom_call" | custom-call | flops 100000000 | bytes 1000000 | tf_op jit(solution)/shard_map/fetch/pallas_call | solution.py:796
  1.7 0.8 %collective-permute-done.mate_ref = bf16[192,768]{1,0:T(8,128)(2,1)S(1)} collective-permute-done((bf16[192,768]{1,0:T(8,128)(2,1)}, bf16[192,768]{1,0:T(8,128)(2,1)S(1)}, u32[]{:S(2)}, u32[]{:S(2)}) %collective-permute-start) | collective-permute-done | bytes 294944 | tf_op jit(solution)/shard_map/ppermute | solution.py:788
  2.6 2.4 %collective-permute-start.1 = (bf16[128,768]{1,0:T(8,128)(2,1)S(1)}, bf16[128,768]{1,0:T(8,128)(2,1)S(1)}, u32[]{:S(2)}, u32[]{:S(2)}) collective-permute-start(bf16[128,768]{1,0:T(8,128)(2,1)S(1)} %pad_maximum_fusion.2), channel_id=1, source_target_pairs={{0,2},{1,3},{2,0},{3,1},{4,6},{5,7},{6,4},{7,5},{8,10},{9,11},{10,... | collective-permute-start | bytes 589832 | tf_op jit(solution)/shard_map/ppermute | solution.py:788
  5.0 4.7 %project.1 = (bf16[384,768]{1,0:T(8,128)(2,1)S(1)}, bf16[384,768]{1,0:T(8,128)(2,1)S(1)}, bf16[384,768]{1,0:T(8,128)(2,1)S(1)}, f32[64,512]{1,0:T(8,128)S(1)}, f...) custom-call(s32[1,6]{1,0:T(1,128)} %len_ref.1, ...), custom_call_target="tpu_custom_call" | custom-call | flops 2000000000 | bytes 12000000 | tf_op jit(solution)/shard_map/project/pallas_call | solution.py:855
  9.9 0.9 %collective-permute-start.2 = (bf16[128,768]{1,0:T(8,128)(2,1)S(1)}, bf16[128,768]{1,0:T(8,128)(2,1)S(1)}, u32[]{:S(2)}, u32[]{:S(2)}) collective-permute-start(bf16[128,768]{1,0:T(8,128)(2,1)S(1)} %collective-permute-done.1.far_ref), channel_id=1, source_target_pairs={{0,1},{1,0},{2,3},{3,2},{4,5},{5,4},{6,7},{7,6},{8,9},{9,8},{10,11... | collective-permute-start | bytes 589832 | tf_op jit(solution)/shard_map/ppermute | solution.py:788
  10.8 1.5 %near.1 = (bf16[128,768]{1,0:T(8,128)(2,1)S(1)}, bf16[128,768]{1,0:T(8,128)(2,1)S(1)}, f32[192,768]{1,0:T(8,128)S(1)}, f32[3,768,128]{2,1,0:T(8,128)S(1)}, f32[3,768,128]{2,1,0:T(8,128)S(1)}) custom-call(bf16[128,768]{1,0:T(8,128)(2,1)S(1)} %collective-permute-done.1.far_ref, bf16[384,768]{1,0:T(8,128)(2,1)S(1)} %get-tuple-element.97.q_ref, ...), custom_call_target="tpu_custom_call" | custom-call | flops 1000000000 | bytes 2000000 | tf_op jit(solution)/shard_map/near/pallas_call | solution.py:882
  12.4 9.8 %layer.1 = (bf16[192,768]{1,0:T(8,128)(2,1)}, bf16[768,768]{1,0:T(8,128)(2,1)S(1)}, bf16[768,768]{1,0:T(8,128)(2,1)S(1)}, f32[192,128]{1,0:T(8,128)S(1)}, f32[19...) custom-call(bf16[192,768]{1,0:T(8,128)(2,1)S(1)} %fetch.1.own_ref, ...), custom_call_target="tpu_custom_call" | custom-call | flops 8000000000 | bytes 20000000 | tf_op jit(solution)/shard_map/layer/pallas_call | solution.py:895
  22.3 1.1 %attended_back.1 = (bf16[224,768]{1,0:T(8,128)(2,1)S(1)}, f32[192,128]{1,0:T(8,128)S(1)}) custom-call(f32[192,768]{1,0:T(8,128)S(1)} %get-tuple-element.141.du1_ref.part_in_ref, bf16[192,64]{1,0:T(8,128)(2,1)S(1)} %get-tuple-element.131.grad_pre_ref, bf16[64,768]{1,0:T(8,128)(2,1)S(1)} %get-tuple-element.113.down1_ref, ...), custom_call_target="tpu_custom_call" | custom-call | flops 500000000 | bytes 2000000 | tf_op jit(solution)/shard_map/attended_back/pallas_call | solution.py:945
  23.4 0.3 collective-permute-done.3
  24.1 2.5 %collective-permute-start.6 = (bf16[72,384]{1,0:T(8,128)(2,1)S(1)}, bf16[72,384]{1,0:T(8,128)(2,1)S(1)}, u32[]{:S(2)}, u32[]{:S(2)}) collective-permute-start(bf16[72,384]{1,0:T(8,128)(2,1)S(1)} %get-tuple-element.184), channel_id=1, source_target_pairs={{0,6},{1,7},{2,4},{3,5},{4,2},{5,3},{6,0},{7,1},{8,14},{9,15},{10,... | collective-permute-start | bytes 165896 | tf_op jit(solution)/shard_map/ppermute | solution.py:791
  26.9 2.0 %query_back_0.1 = (bf16[768,256]{1,0:T(8,128)(2,1)S(1)}, bf16[768,256]{1,0:T(8,128)(2,1)S(1)}, f32[192,768]{1,0:T(8,128)S(1)}) custom-call(bf16[128,768]{1,0:T(8,128)(2,1)S(1)} %collective-permute-done.1.far_ref, bf16[128,768]{1,0:T(8,128)(2,1)S(1)} %collective-permute-done.2.far_mate_ref, bf16[384,768]{1,0:T(8,128)(2,1)S(1)} %get-tuple-element.97.q_ref, ...), custom_call_target="tpu_custom_call" | custom-call | flops 2000000000 | bytes 3000000 | tf_op jit(solution)/shard_map/query_back_0/pallas_call | solution.py:956
  29.0 0.8 %collective-permute-done.5 = bf16[72,384]{1,0:T(8,128)(2,1)S(1)} collective-permute-done((bf16[72,384]{1,0:T(8,128)(2,1)S(1)}, bf16[72,384]{1,0:T(8,128)(2,1)S(1)}, u32[]{:S(2)}, u32[]{:S(2)}) %collective-permute-start.5) | collective-permute-done | bytes 55328 | tf_op jit(solution)/shard_map/ppermute | solution.py:791
  29.8 1.4 %collective-permute-start.8 = (bf16[72,384]{1,0:T(8,128)(2,1)S(1)}, bf16[72,384]{1,0:T(8,128)(2,1)S(1)}, u32[]{:S(2)}, u32[]{:S(2)}) collective-permute-start(bf16[72,384]{1,0:T(8,128)(2,1)S(1)} %fusion.2), channel_id=1, source_target_pairs={{0,8},{1,9},{2,10},{3,11},{4,12},{5,13},{6,14},{7,15},{8,0},{9,1},... | collective-permute-start | bytes 165896 | tf_op jit(solution)/shard_map/ppermute | solution.py:791
  31.3 1.7 %collective-permute-start.10 = (bf16[160,768]{1,0:T(8,128)(2,1)S(1)}, bf16[160,768]{1,0:T(8,128)(2,1)S(1)}, u32[]{:S(2)}, u32[]{:S(2)}) collective-permute-start(bf16[160,768]{1,0:T(8,128)(2,1)S(1)} %pad_maximum_fusion), channel_id=1, source_target_pairs={{0,2},{1,3},{2,0},{3,1},{4,6},{5,7},{6,4},{7,5},{8,10},{9,11},{10,... | collective-permute-start | bytes 737288 | tf_op jit(solution)/shard_map/ppermute | solution.py:788
  33.1 2.4 %collective-permute-start.9 = (bf16[72,384]{1,0:T(8,128)(2,1)S(1)}, bf16[72,384]{1,0:T(8,128)(2,1)S(1)}, u32[]{:S(2)}, u32[]{:S(2)}) collective-permute-start(bf16[72,384]{1,0:T(8,128)(2,1)S(1)} %add_convert_fusion.2), channel_id=1, source_target_pairs={{0,16},{1,17},{2,18},{3,19},{4,20},{5,21},{6,22},{7,23},{8,24},{9,... | collective-permute-start | bytes 165896 | tf_op jit(solution)/shard_map/ppermute | solution.py:791
  35.4 1.5 %query_back_2.1 = (bf16[768,256]{1,0:T(8,128)(2,1)S(1)}, f32[192,768]{1,0:T(8,128)S(1)}) custom-call(bf16[128,768]{1,0:T(8,128)(2,1)S(1)} %collective-permute-done.1.far_ref, bf16[128,768]{1,0:T(8,128)(2,1)S(1)} %collective-permute-done.2.far_mate_ref, bf16[384,768]{1,0:T(8,128)(2,1)S(1)} %get-tuple-element.97.q_ref, ...), custom_call_target="tpu_custom_call" | custom-call | flops 1000000000 | bytes 3000000 | tf_op jit(solution)/shard_map/query_back_2/pallas_call | solution.py:956
  37.0 3.5 %collective-permute-start.14 = (bf16[160,768]{1,0:T(8,128)(2,1)S(1)}, bf16[160,768]{1,0:T(8,128)(2,1)S(1)}, u32[]{:S(2)}, u32[]{:S(2)}) collective-permute-start(bf16[160,768]{1,0:T(8,128)(2,1)S(1)} %collective-permute-done.10.far_ref), channel_id=1, source_target_pairs={{0,1},{1,0},{2,3},{3,2},{4,5},{5,4},{6,7},{7,6},{8,9},{9,8},{10,11... | collective-permute-start | bytes 737288 | tf_op jit(solution)/shard_map/ppermute | solution.py:788
  40.5 1.2 %collective-permute-start.13 = (bf16[72,384]{1,0:T(8,128)(2,1)S(1)}, bf16[72,384]{1,0:T(8,128)(2,1)S(1)}, u32[]{:S(2)}, u32[]{:S(2)}) collective-permute-start(bf16[72,384]{1,0:T(8,128)(2,1)S(1)} %add_convert_fusion.1), channel_id=1, source_target_pairs={{0,6},{1,7},{2,4},{3,5},{4,2},{5,3},{6,0},{7,1},{8,14},{9,15},{10,... | collective-permute-start | bytes 165896 | tf_op jit(solution)/shard_map/ppermute | solution.py:791
  41.7 0.4 collective-permute-start.12
  42.2 1.1 %collective-permute-start.11 = (bf16[72,384]{1,0:T(8,128)(2,1)S(1)}, bf16[72,384]{1,0:T(8,128)(2,1)S(1)}, u32[]{:S(2)}, u32[]{:S(2)}) collective-permute-start(bf16[72,384]{1,0:T(8,128)(2,1)S(1)} %add_convert_fusion.1), channel_id=1, source_target_pairs={{0,4},{1,5},{2,6},{3,7},{4,0},{5,1},{6,2},{7,3},{8,12},{9,13},{10,... | collective-permute-start | bytes 165896 | tf_op jit(solution)/shard_map/ppermute | solution.py:791
  43.4 2.6 %key_back_0.1.part_ref = f32[192,768]{1,0:T(8,128)S(1)} custom-call(bf16[768,768]{1,0:T(8,128)(2,1)S(1)} %get-tuple-element.155.grads_ref, f32[64,512]{1,0:T(8,128)S(1)} %get-tuple-element.156.stats_ref, bf16[768,768]{1,0:T(8,128)(2,1)S(1)} %get-tuple-element.136.kbuf, bf16[768,768]{1,0:T(8,128)(2,1)S(1)} %get-tuple-element.137.vbuf, ...), custom_call_target="tpu_custom_call" | custom-call | flops 2000000000 | bytes 3000000 | tf_op jit(solution)/shard_map/key_back_0/pallas_call | solution.py:967
  46.1 1.7 %collective-permute-start.15 = (bf16[4,72,384]{2,1,0:T(8,128)(2,1)S(1)}, bf16[4,72,384]{2,1,0:T(8,128)(2,1)S(1)}, u32[]{:S(2)}, u32[]{:S(2)}) collective-permute-start(bf16[4,72,384]{2,1,0:T(8,128)(2,1)S(1)} %pad_maximum_fusion.1.here_ref), channel_id=1, source_target_pairs={{0,1},{1,0},{2,3},{3,2},{4,5},{5,4},{6,7},{7,6},{8,9},{9,8},{10,11... | collective-permute-start | bytes 663560 | tf_op jit(solution)/shard_map/ppermute | solution.py:791
  47.8 1.4 %key_back_2.1.grad_ref = bf16[192,768]{1,0:T(8,128)(2,1)S(1)} custom-call(bf16[768,768]{1,0:T(8,128)(2,1)S(1)} %get-tuple-element.155.grads_ref, f32[64,512]{1,0:T(8,128)S(1)} %get-tuple-element.156.stats_ref, bf16[768,768]{1,0:T(8,128)(2,1)S(1)} %get-tuple-element.136.kbuf, bf16[768,768]{1,0:T(8,128)(2,1)S(1)} %get-tuple-element.137.vbuf, ...), custom_call_target="tpu_custom_call" | custom-call | flops 1000000000 | bytes 3000000 | tf_op jit(solution)/shard_map/key_back_2/pallas_call | solution.py:967
  49.2 1.1 %unpack.1 = (bf16[192,768]{1,0:T(8,128)(2,1)}, f32[64,768]{1,0:T(8,128)}, f32[64]{0:T(128)}, f32[64,768]{1,0:T(8,128)}, f32[768]{0:T(1024)}, /*index=5*/f32[768]...) custom-call(bf16[4,72,384]{2,1,0:T(8,128)(2,1)S(1)} %pad_maximum_fus, ...), custom_call_target="tpu_custom_call" | custom-call | tf_op jit(solution)/shard_map/unpack/pallas_call | solution.py:1013
  (30 shorter events, 1.7 us)
Async XLA Ops:
  0.6 1.9 %collective-permute-start = (bf16[192,768]{1,0:T(8,128)(2,1)}, bf16[192,768]{1,0:T(8,128)(2,1)S(1)}, u32[]{:S(2)}, u32[]{:S(2)}) collective-permute-start(bf16[192,768]{1,0:T(8,128)(2,1)} %bitcast.24), channel_id=1, source_target_pairs={{0,1},{1,0},{2,3},{3,2},{4,5},{5,4},{6,7},{7,6},{8,9},{9,8},{10,11... | collective-permute-start | bytes 884744 | tf_op jit(solution)/shard_map/ppermute | solution.py:788
  2.6 7.4 %collective-permute-start.1 = (bf16[128,768]{1,0:T(8,128)(2,1)S(1)}, bf16[128,768]{1,0:T(8,128)(2,1)S(1)}, u32[]{:S(2)}, u32[]{:S(2)}) collective-permute-start(bf16[128,768]{1,0:T(8,128)(2,1)S(1)} %pad_maximum_fusion.2), channel_id=1, source_target_pairs={{0,2},{1,3},{2,0},{3,1},{4,6},{5,7},{6,4},{7,5},{8,10},{9,11},{10,... | collective-permute-start | bytes 589832 | tf_op jit(solution)/shard_map/ppermute | solution.py:788
  9.9 2.4 %collective-permute-start.2 = (bf16[128,768]{1,0:T(8,128)(2,1)S(1)}, bf16[128,768]{1,0:T(8,128)(2,1)S(1)}, u32[]{:S(2)}, u32[]{:S(2)}) collective-permute-start(bf16[128,768]{1,0:T(8,128)(2,1)S(1)} %collective-permute-done.1.far_ref), channel_id=1, source_target_pairs={{0,1},{1,0},{2,3},{3,2},{4,5},{5,4},{6,7},{7,6},{8,9},{9,8},{10,11... | collective-permute-start | bytes 589832 | tf_op jit(solution)/shard_map/ppermute | solution.py:788
  22.2 1.5 %collective-permute-start.3 = (bf16[4,72,384]{2,1,0:T(8,128)(2,1)S(1)}, bf16[4,72,384]{2,1,0:T(8,128)(2,1)S(1)}, u32[]{:S(2)}, u32[]{:S(2)}) collective-permute-start(bf16[4,72,384]{2,1,0:T(8,128)(2,1)S(1)} %get-tuple-element.129), channel_id=1, source_target_pairs={{0,1},{1,0},{2,3},{3,2},{4,5},{5,4},{6,7},{7,6},{8,9},{9,8},{10,11... | collective-permute-start | bytes 663560 | tf_op jit(solution)/shard_map/ppermute | solution.py:791
  23.8 6.0 %collective-permute-start.7 = (bf16[224,768]{1,0:T(8,128)(2,1)S(1)}, bf16[224,768]{1,0:T(8,128)(2,1)S(1)}, u32[]{:S(2)}, u32[]{:S(2)}) collective-permute-start(bf16[224,768]{1,0:T(8,128)(2,1)S(1)} %get-tuple-element.148.pack_ref.own_ref), channel_id=1, source_target_pairs={{0,1},{1,0},{2,3},{3,2},{4,5},{5,4},{6,7},{7,6},{8,9},{9,8},{10,11... | collective-permute-start | bytes 1032200 | tf_op jit(solution)/shard_map/ppermute | solution.py:788
  24.1 4.9 %collective-permute-start.6 = (bf16[72,384]{1,0:T(8,128)(2,1)S(1)}, bf16[72,384]{1,0:T(8,128)(2,1)S(1)}, u32[]{:S(2)}, u32[]{:S(2)}) collective-permute-start(bf16[72,384]{1,0:T(8,128)(2,1)S(1)} %get-tuple-element.184), channel_id=1, source_target_pairs={{0,6},{1,7},{2,4},{3,5},{4,2},{5,3},{6,0},{7,1},{8,14},{9,15},{10,... | collective-permute-start | bytes 165896 | tf_op jit(solution)/shard_map/ppermute | solution.py:791
  26.5 3.2 %collective-permute-start.5 = (bf16[72,384]{1,0:T(8,128)(2,1)S(1)}, bf16[72,384]{1,0:T(8,128)(2,1)S(1)}, u32[]{:S(2)}, u32[]{:S(2)}) collective-permute-start(bf16[72,384]{1,0:T(8,128)(2,1)S(1)} %get-tuple-element.185), channel_id=1, source_target_pairs={{0,2},{1,3},{2,0},{3,1},{4,6},{5,7},{6,4},{7,5},{8,10},{9,11},{10,... | collective-permute-start | bytes 165896 | tf_op jit(solution)/shard_map/ppermute | solution.py:791
  26.8 3.0 %collective-permute-start.4 = (bf16[72,384]{1,0:T(8,128)(2,1)S(1)}, bf16[72,384]{1,0:T(8,128)(2,1)S(1)}, u32[]{:S(2)}, u32[]{:S(2)}) collective-permute-start(bf16[72,384]{1,0:T(8,128)(2,1)S(1)} %get-tuple-element.186), channel_id=1, source_target_pairs={{0,4},{1,5},{2,6},{3,7},{4,0},{5,1},{6,2},{7,3},{8,12},{9,13},{10,... | collective-permute-start | bytes 165896 | tf_op jit(solution)/shard_map/ppermute | solution.py:791
  29.8 3.2 %collective-permute-start.8 = (bf16[72,384]{1,0:T(8,128)(2,1)S(1)}, bf16[72,384]{1,0:T(8,128)(2,1)S(1)}, u32[]{:S(2)}, u32[]{:S(2)}) collective-permute-start(bf16[72,384]{1,0:T(8,128)(2,1)S(1)} %fusion.2), channel_id=1, source_target_pairs={{0,8},{1,9},{2,10},{3,11},{4,12},{5,13},{6,14},{7,15},{8,0},{9,1},... | collective-permute-start | bytes 165896 | tf_op jit(solution)/shard_map/ppermute | solution.py:791
  31.3 5.7 %collective-permute-start.10 = (bf16[160,768]{1,0:T(8,128)(2,1)S(1)}, bf16[160,768]{1,0:T(8,128)(2,1)S(1)}, u32[]{:S(2)}, u32[]{:S(2)}) collective-permute-start(bf16[160,768]{1,0:T(8,128)(2,1)S(1)} %pad_maximum_fusion), channel_id=1, source_target_pairs={{0,2},{1,3},{2,0},{3,1},{4,6},{5,7},{6,4},{7,5},{8,10},{9,11},{10,... | collective-permute-start | bytes 737288 | tf_op jit(solution)/shard_map/ppermute | solution.py:788
  33.1 7.4 %collective-permute-start.9 = (bf16[72,384]{1,0:T(8,128)(2,1)S(1)}, bf16[72,384]{1,0:T(8,128)(2,1)S(1)}, u32[]{:S(2)}, u32[]{:S(2)}) collective-permute-start(bf16[72,384]{1,0:T(8,128)(2,1)S(1)} %add_convert_fusion.2), channel_id=1, source_target_pairs={{0,16},{1,17},{2,18},{3,19},{4,20},{5,21},{6,22},{7,23},{8,24},{9,... | collective-permute-start | bytes 165896 | tf_op jit(solution)/shard_map/ppermute | solution.py:791
  37.0 6.2 %collective-permute-start.14 = (bf16[160,768]{1,0:T(8,128)(2,1)S(1)}, bf16[160,768]{1,0:T(8,128)(2,1)S(1)}, u32[]{:S(2)}, u32[]{:S(2)}) collective-permute-start(bf16[160,768]{1,0:T(8,128)(2,1)S(1)} %collective-permute-done.10.far_ref), channel_id=1, source_target_pairs={{0,1},{1,0},{2,3},{3,2},{4,5},{5,4},{6,7},{7,6},{8,9},{9,8},{10,11... | collective-permute-start | bytes 737288 | tf_op jit(solution)/shard_map/ppermute | solution.py:788
  40.5 5.5 %collective-permute-start.13 = (bf16[72,384]{1,0:T(8,128)(2,1)S(1)}, bf16[72,384]{1,0:T(8,128)(2,1)S(1)}, u32[]{:S(2)}, u32[]{:S(2)}) collective-permute-start(bf16[72,384]{1,0:T(8,128)(2,1)S(1)} %add_convert_fusion.1), channel_id=1, source_target_pairs={{0,6},{1,7},{2,4},{3,5},{4,2},{5,3},{6,0},{7,1},{8,14},{9,15},{10,... | collective-permute-start | bytes 165896 | tf_op jit(solution)/shard_map/ppermute | solution.py:791
  41.7 4.3 %collective-permute-start.12 = (bf16[72,384]{1,0:T(8,128)(2,1)S(1)}, bf16[72,384]{1,0:T(8,128)(2,1)S(1)}, u32[]{:S(2)}, u32[]{:S(2)}) collective-permute-start(bf16[72,384]{1,0:T(8,128)(2,1)S(1)} %add_convert_fusion.1), channel_id=1, source_target_pairs={{0,2},{1,3},{2,0},{3,1},{4,6},{5,7},{6,4},{7,5},{8,10},{9,11},{10,... | collective-permute-start | bytes 165896 | tf_op jit(solution)/shard_map/ppermute | solution.py:791
  42.2 3.9 %collective-permute-start.11 = (bf16[72,384]{1,0:T(8,128)(2,1)S(1)}, bf16[72,384]{1,0:T(8,128)(2,1)S(1)}, u32[]{:S(2)}, u32[]{:S(2)}) collective-permute-start(bf16[72,384]{1,0:T(8,128)(2,1)S(1)} %add_convert_fusion.1), channel_id=1, source_target_pairs={{0,4},{1,5},{2,6},{3,7},{4,0},{5,1},{6,2},{7,3},{8,12},{9,13},{10,... | collective-permute-start | bytes 165896 | tf_op jit(solution)/shard_map/ppermute | solution.py:791
  46.1 3.1 %collective-permute-start.15 = (bf16[4,72,384]{2,1,0:T(8,128)(2,1)S(1)}, bf16[4,72,384]{2,1,0:T(8,128)(2,1)S(1)}, u32[]{:S(2)}, u32[]{:S(2)}) collective-permute-start(bf16[4,72,384]{2,1,0:T(8,128)(2,1)S(1)} %pad_maximum_fusion.1.here_ref), channel_id=1, source_target_pairs={{0,1},{1,0},{2,3},{3,2},{4,5},{5,4},{6,7},{7,6},{8,9},{9,8},{10,11... | collective-permute-start | bytes 663560 | tf_op jit(solution)/shard_map/ppermute | solution.py:791

commit v6 on v5

--- a/solution.py
+++ b/solution.py
@@ -16,7 +16,6 @@
 HALF = 256
 SHARE = 128
 CHUNK = 768
-SMALL = 8
 ROWS_B = 128
 NEG = -1e30
 F32 = jnp.float32
@@ -506,22 +505,23 @@
         (grad_up2, grad_ubias2, blank),
         (grad_down2, grad_gain2, grad_shift2),
     )
-    filler = jnp.zeros((SMALL - 2, width), F32)
-    wholes = [
-        jnp.concatenate([matrix, one, two, filler], axis=0).astype(BF16)
-        for matrix, one, two in quarters
-    ]
+    filler = jnp.zeros((2, 128), F32)
+
+    def part_of(quarter, side):
+        pieces = [
+            array[:, at : at + 128]
+            for array in quarter
+            for at in range(side * width // 2, (side + 1) * width // 2, 128)
+        ]
+        return jnp.concatenate(pieces + [filler], axis=0).astype(BF16)
+
     side_here = lax.axis_index("dp") % 2
     for chip_of in range(2):
-        even, odd = wholes[2 * chip_of], wholes[2 * chip_of + 1]
-        kept = jnp.where(core == 0, even, odd)
-        sent = jnp.where(core == 0, odd, even)
         for side in range(2):
-            half = slice(side * width // 2, (side + 1) * width // 2)
+            even, odd = (part_of(quarters[2 * chip_of + index], side) for index in range(2))
             place = 2 * (chip ^ chip_of) + (side_here ^ side)
-            keep_ref[place] = kept[:, half]
-            send_ref[place] = sent[:, half]
-
+            keep_ref[place] = jnp.where(core == 0, even, odd)
+            send_ref[place] = jnp.where(core == 0, odd, even)
     mixed_copy.wait()
 
 
@@ -706,20 +706,21 @@
     copies[0].start()
     matrices = (2, 0, 8, 6)
     vectors = ((3,), (4, 5), (9,), (10, 11))
+    width = outs[0].shape[1]
+    blocks = width // 256
     for index in range(4):
-        halves = []
         for side in range(2):
             place = 2 * (chip ^ (index // 2)) + (side_here ^ side)
-            halves.append(jnp.where(core == index % 2, here_ref[place], other_ref[place]))
-        whole = jnp.concatenate(halves, axis=1).astype(F32)
-        outs[matrices[index]][...] = whole[:adapt]
-        ready = [matrices[index], *vectors[index]]
-        for row, vector in enumerate(vectors[index]):
-            outs[vector][...] = whole[adapt + row]
-        if index == 0:
-            outs[1][...] = whole[adapt + 1, :adapt]
-            outs[7][...] = whole[adapt + 1, 128 : 128 + adapt]
-            ready += [1, 7]
+            part = jnp.where(core == index % 2, here_ref[place], other_ref[place]).astype(F32)
+            for block_at in range(blocks):
+                lanes = slice(side * width // 2 + 128 * block_at, side * width // 2 + 128 * (block_at + 1))
+                outs[matrices[index]][:, lanes] = part[adapt * block_at : adapt * (block_at + 1)]
+                for number, vector in enumerate(vectors[index]):
+                    outs[vector][lanes] = part[blocks * (adapt + number) + block_at]
+            if index == 0 and side == 0:
+                outs[1][...] = part[blocks * (adapt + 1), :adapt]
+                outs[7][...] = part[blocks * (adapt + 1) + 1, :adapt]
+        ready = [matrices[index], *vectors[index]] + ([1, 7] if index == 0 else [])
         for out in ready:
             copies[1 + out].start()
     for copy in copies:
@@ -891,7 +892,7 @@
         name="near",
     )(far, q, kpair, vpair, near_a, near_b, wk_here, wv_here)
 
-    part_rows = adapt + SMALL
+    part_rows = width // 256 * (adapt + 2) + 2
     mixed, kbuf, vbuf, lse, du1, attended, grad_pre, keep, send = pl.pallas_call(
         main_kernel,
         in_specs=[VMEM] * 29 + [HBM],
@@ -904,8 +905,8 @@
             vmem((rows, width), F32),
             vmem((rows, width), F32),
             vmem((rows, adapt), BF16),
-            vmem((4, part_rows, width // 2), BF16),
-            vmem((4, part_rows, width // 2), BF16),
+            vmem((4, part_rows, 128), BF16),
+            vmem((4, part_rows, 128), BF16),
         ],
         scratch_shapes=[
             pltpu.VMEM((hidden, width), BF16),

time: 50.7 us -> 50.5 us (level)
  no operation moved by 1% of the time
where the time goes in v6:
time: 50.5 us; the launch traced here: 50.4 us
  Pallas kernels  27 us (53%)
  starting transfers between devices  19.9 us (39%)
  waiting for transfers between devices  2.17 us (4%)
  between operations  1.02 us (2%)
    ppermute x10, starting transfers between devices, swap_all(): lax.ppermute(array, ('dp', 'blk'), [(i, i ^ mask) for i in range(4 * dp_s...  10.9 us
    pallas_call x1, Pallas kernels, body(): pl.pallas_call(main_kernel, in_specs=[VMEM] * 29 + [HBM], out_specs=[HBM]...  9.83 us
    ppermute x6, starting transfers between devices, swap(): return lax.ppermute(array, 'blk', [(i, i ^ mask) for i in range(4)])  8.98 us
    pallas_call x1, Pallas kernels, body(): pl.pallas_call(project_kernel, in_specs=[SMEM] * 2 + [VMEM] * 2 + [HBM] *...  4.69 us
    pallas_call x2, Pallas kernels, key_back(): pl.pallas_call(functools.partial(key_back_kernel, groups), in_specs=[VMEM...  4.04 us
    pallas_call x2, Pallas kernels, query_back(): pl.pallas_call(functools.partial(query_back_kernel, groups), in_specs=[VM...  3.53 us
    pallas_call x1, Pallas kernels, body(): pl.pallas_call(near_kernel, in_specs=[VMEM] * 8, out_specs=[VMEM] * 5, ou...  1.54 us
    pallas_call x1, Pallas kernels, body(): pl.pallas_call(attended_back_kernel, in_specs=[VMEM] * 6, out_specs=[VMEM...  1.12 us
  transfers between devices with their start and end apart: 16, of which 5 were waited for; matrix products, arithmetic and copies ran while one was open for 0% of the time, Pallas kernels for 32%

profile of v6, /device:TPU:1, one launch (start us, length us, event | category | flops | bytes accessed | tf_op | source)
XLA Modules:
  0.0 50.4 jit_solution(12345452273284963214)
XLA Ops:
  0.8 1.0 %fetch.1.own_ref = bf16[192,768]{1,0:T(8,128)(2,1)S(1)} custom-call(bf16[192,768]{1,0:T(8,128)(2,1)} %bitcast.25), custom_call_target="tpu_custom_call" | custom-call | flops 100000000 | bytes 1000000 | tf_op jit(solution)/shard_map/fetch/pallas_call | solution.py:797
  1.7 0.8 %collective-permute-done.mate_ref = bf16[192,768]{1,0:T(8,128)(2,1)S(1)} collective-permute-done((bf16[192,768]{1,0:T(8,128)(2,1)}, bf16[192,768]{1,0:T(8,128)(2,1)S(1)}, u32[]{:S(2)}, u32[]{:S(2)}) %collective-permute-start) | collective-permute-done | bytes 294944 | tf_op jit(solution)/shard_map/ppermute | solution.py:789
  2.6 2.4 %collective-permute-start.1 = (bf16[128,768]{1,0:T(8,128)(2,1)S(1)}, bf16[128,768]{1,0:T(8,128)(2,1)S(1)}, u32[]{:S(2)}, u32[]{:S(2)}) collective-permute-start(bf16[128,768]{1,0:T(8,128)(2,1)S(1)} %pad_maximum_fusion.2), channel_id=1, source_target_pairs={{0,2},{1,3},{2,0},{3,1},{4,6},{5,7},{6,4},{7,5},{8,10},{9,11},{10,... | collective-permute-start | bytes 589832 | tf_op jit(solution)/shard_map/ppermute | solution.py:789
  5.0 4.7 %project.1 = (bf16[384,768]{1,0:T(8,128)(2,1)S(1)}, bf16[384,768]{1,0:T(8,128)(2,1)S(1)}, bf16[384,768]{1,0:T(8,128)(2,1)S(1)}, f32[64,512]{1,0:T(8,128)S(1)}, f...) custom-call(s32[1,6]{1,0:T(1,128)} %len_ref.1, ...), custom_call_target="tpu_custom_call" | custom-call | flops 2000000000 | bytes 12000000 | tf_op jit(solution)/shard_map/project/pallas_call | solution.py:856
  9.9 0.9 %collective-permute-start.2 = (bf16[128,768]{1,0:T(8,128)(2,1)S(1)}, bf16[128,768]{1,0:T(8,128)(2,1)S(1)}, u32[]{:S(2)}, u32[]{:S(2)}) collective-permute-start(bf16[128,768]{1,0:T(8,128)(2,1)S(1)} %collective-permute-done.1.far_ref), channel_id=1, source_target_pairs={{0,1},{1,0},{2,3},{3,2},{4,5},{5,4},{6,7},{7,6},{8,9},{9,8},{10,11... | collective-permute-start | bytes 589832 | tf_op jit(solution)/shard_map/ppermute | solution.py:789
  10.8 1.5 %near.1 = (bf16[128,768]{1,0:T(8,128)(2,1)S(1)}, bf16[128,768]{1,0:T(8,128)(2,1)S(1)}, f32[192,768]{1,0:T(8,128)S(1)}, f32[3,768,128]{2,1,0:T(8,128)S(1)}, f32[3,768,128]{2,1,0:T(8,128)S(1)}) custom-call(bf16[128,768]{1,0:T(8,128)(2,1)S(1)} %collective-permute-done.1.far_ref, bf16[384,768]{1,0:T(8,128)(2,1)S(1)} %get-tuple-element.97.q_ref, ...), custom_call_target="tpu_custom_call" | custom-call | flops 1000000000 | bytes 2000000 | tf_op jit(solution)/shard_map/near/pallas_call | solution.py:883
  12.4 9.8 %layer.1 = (bf16[192,768]{1,0:T(8,128)(2,1)}, bf16[768,768]{1,0:T(8,128)(2,1)S(1)}, bf16[768,768]{1,0:T(8,128)(2,1)S(1)}, f32[192,128]{1,0:T(8,128)S(1)}, f32[19...) custom-call(bf16[192,768]{1,0:T(8,128)(2,1)S(1)} %fetch.1.own_ref, ...), custom_call_target="tpu_custom_call" | custom-call | flops 8000000000 | bytes 20000000 | tf_op jit(solution)/shard_map/layer/pallas_call | solution.py:896
  22.3 1.1 %attended_back.1 = (bf16[224,768]{1,0:T(8,128)(2,1)S(1)}, f32[192,128]{1,0:T(8,128)S(1)}) custom-call(f32[192,768]{1,0:T(8,128)S(1)} %get-tuple-element.141.du1_ref.part_in_ref, bf16[192,64]{1,0:T(8,128)(2,1)S(1)} %get-tuple-element.131.grad_pre_ref, bf16[64,768]{1,0:T(8,128)(2,1)S(1)} %get-tuple-element.113.down1_ref, ...), custom_call_target="tpu_custom_call" | custom-call | flops 500000000 | bytes 2000000 | tf_op jit(solution)/shard_map/attended_back/pallas_call | solution.py:946
  23.4 0.3 collective-permute-done.3
  24.1 2.5 %collective-permute-start.6 = (bf16[200,128]{1,0:T(8,128)(2,1)S(1)}, bf16[200,128]{1,0:T(8,128)(2,1)S(1)}, u32[]{:S(2)}, u32[]{:S(2)}) collective-permute-start(bf16[200,128]{1,0:T(8,128)(2,1)S(1)} %get-tuple-element.184), channel_id=1, source_target_pairs={{0,6},{1,7},{2,4},{3,5},{4,2},{5,3},{6,0},{7,1},{8,14},{9,15},{10,... | collective-permute-start | bytes 153608 | tf_op jit(solution)/shard_map/ppermute | solution.py:792
  26.9 2.0 %query_back_0.1 = (bf16[768,256]{1,0:T(8,128)(2,1)S(1)}, bf16[768,256]{1,0:T(8,128)(2,1)S(1)}, f32[192,768]{1,0:T(8,128)S(1)}) custom-call(bf16[128,768]{1,0:T(8,128)(2,1)S(1)} %collective-permute-done.1.far_ref, bf16[128,768]{1,0:T(8,128)(2,1)S(1)} %collective-permute-done.2.far_mate_ref, bf16[384,768]{1,0:T(8,128)(2,1)S(1)} %get-tuple-element.97.q_ref, ...), custom_call_target="tpu_custom_call" | custom-call | flops 2000000000 | bytes 3000000 | tf_op jit(solution)/shard_map/query_back_0/pallas_call | solution.py:957
  29.0 0.6 %collective-permute-done.5 = bf16[200,128]{1,0:T(8,128)(2,1)S(1)} collective-permute-done((bf16[200,128]{1,0:T(8,128)(2,1)S(1)}, bf16[200,128]{1,0:T(8,128)(2,1)S(1)}, u32[]{:S(2)}, u32[]{:S(2)}) %collective-permute-start.5) | collective-permute-done | bytes 51232 | tf_op jit(solution)/shard_map/ppermute | solution.py:792
  29.8 1.4 %collective-permute-start.8 = (bf16[200,128]{1,0:T(8,128)(2,1)S(1)}, bf16[200,128]{1,0:T(8,128)(2,1)S(1)}, u32[]{:S(2)}, u32[]{:S(2)}) collective-permute-start(bf16[200,128]{1,0:T(8,128)(2,1)S(1)} %fusion.2), channel_id=1, source_target_pairs={{0,8},{1,9},{2,10},{3,11},{4,12},{5,13},{6,14},{7,15},{8,0},{9,1},... | collective-permute-start | bytes 153608 | tf_op jit(solution)/shard_map/ppermute | solution.py:792
  31.2 1.7 %collective-permute-start.10 = (bf16[160,768]{1,0:T(8,128)(2,1)S(1)}, bf16[160,768]{1,0:T(8,128)(2,1)S(1)}, u32[]{:S(2)}, u32[]{:S(2)}) collective-permute-start(bf16[160,768]{1,0:T(8,128)(2,1)S(1)} %pad_maximum_fusion), channel_id=1, source_target_pairs={{0,2},{1,3},{2,0},{3,1},{4,6},{5,7},{6,4},{7,5},{8,10},{9,11},{10,... | collective-permute-start | bytes 737288 | tf_op jit(solution)/shard_map/ppermute | solution.py:789
  32.9 2.4 %collective-permute-start.9 = (bf16[200,128]{1,0:T(8,128)(2,1)S(1)}, bf16[200,128]{1,0:T(8,128)(2,1)S(1)}, u32[]{:S(2)}, u32[]{:S(2)}) collective-permute-start(bf16[200,128]{1,0:T(8,128)(2,1)S(1)} %add_convert_fusion.2), channel_id=1, source_target_pairs={{0,16},{1,17},{2,18},{3,19},{4,20},{5,21},{6,22},{7,23},{8,24},{9,... | collective-permute-start | bytes 153608 | tf_op jit(solution)/shard_map/ppermute | solution.py:792
  35.3 1.5 %query_back_2.1 = (bf16[768,256]{1,0:T(8,128)(2,1)S(1)}, f32[192,768]{1,0:T(8,128)S(1)}) custom-call(bf16[128,768]{1,0:T(8,128)(2,1)S(1)} %collective-permute-done.1.far_ref, bf16[128,768]{1,0:T(8,128)(2,1)S(1)} %collective-permute-done.2.far_mate_ref, bf16[384,768]{1,0:T(8,128)(2,1)S(1)} %get-tuple-element.97.q_ref, ...), custom_call_target="tpu_custom_call" | custom-call | flops 1000000000 | bytes 3000000 | tf_op jit(solution)/shard_map/query_back_2/pallas_call | solution.py:957
  36.8 3.6 %collective-permute-start.14 = (bf16[160,768]{1,0:T(8,128)(2,1)S(1)}, bf16[160,768]{1,0:T(8,128)(2,1)S(1)}, u32[]{:S(2)}, u32[]{:S(2)}) collective-permute-start(bf16[160,768]{1,0:T(8,128)(2,1)S(1)} %collective-permute-done.10.far_ref), channel_id=1, source_target_pairs={{0,1},{1,0},{2,3},{3,2},{4,5},{5,4},{6,7},{7,6},{8,9},{9,8},{10,11... | collective-permute-start | bytes 737288 | tf_op jit(solution)/shard_map/ppermute | solution.py:789
  40.5 1.1 %collective-permute-start.13 = (bf16[200,128]{1,0:T(8,128)(2,1)S(1)}, bf16[200,128]{1,0:T(8,128)(2,1)S(1)}, u32[]{:S(2)}, u32[]{:S(2)}) collective-permute-start(bf16[200,128]{1,0:T(8,128)(2,1)S(1)} %add_convert_fusion.1), channel_id=1, source_target_pairs={{0,6},{1,7},{2,4},{3,5},{4,2},{5,3},{6,0},{7,1},{8,14},{9,15},{10,... | collective-permute-start | bytes 153608 | tf_op jit(solution)/shard_map/ppermute | solution.py:792
  41.6 0.5 collective-permute-start.12
  42.0 1.1 %collective-permute-start.11 = (bf16[200,128]{1,0:T(8,128)(2,1)S(1)}, bf16[200,128]{1,0:T(8,128)(2,1)S(1)}, u32[]{:S(2)}, u32[]{:S(2)}) collective-permute-start(bf16[200,128]{1,0:T(8,128)(2,1)S(1)} %add_convert_fusion.1), channel_id=1, source_target_pairs={{0,4},{1,5},{2,6},{3,7},{4,0},{5,1},{6,2},{7,3},{8,12},{9,13},{10,... | collective-permute-start | bytes 153608 | tf_op jit(solution)/shard_map/ppermute | solution.py:792
  43.4 2.6 %key_back_0.1.part_ref = f32[192,768]{1,0:T(8,128)S(1)} custom-call(bf16[768,768]{1,0:T(8,128)(2,1)S(1)} %get-tuple-element.155.grads_ref, f32[64,512]{1,0:T(8,128)S(1)} %get-tuple-element.156.stats_ref, bf16[768,768]{1,0:T(8,128)(2,1)S(1)} %get-tuple-element.136.kbuf, bf16[768,768]{1,0:T(8,128)(2,1)S(1)} %get-tuple-element.137.vbuf, ...), custom_call_target="tpu_custom_call" | custom-call | flops 2000000000 | bytes 3000000 | tf_op jit(solution)/shard_map/key_back_0/pallas_call | solution.py:968
  46.0 1.6 %collective-permute-start.15 = (bf16[4,200,128]{2,1,0:T(8,128)(2,1)S(1)}, bf16[4,200,128]{2,1,0:T(8,128)(2,1)S(1)}, u32[]{:S(2)}, u32[]{:S(2)}) collective-permute-start(bf16[4,200,128]{2,1,0:T(8,128)(2,1)S(1)} %pad_maximum_fusion.1.here_ref), channel_id=1, source_target_pairs={{0,1},{1,0},{2,3},{3,2},{4,5},{5,4},{6,7},{7,6},{8,9},{9,8},{10,11... | collective-permute-start | bytes 614408 | tf_op jit(solution)/shard_map/ppermute | solution.py:792
  47.6 1.4 %key_back_2.1.grad_ref = bf16[192,768]{1,0:T(8,128)(2,1)S(1)} custom-call(bf16[768,768]{1,0:T(8,128)(2,1)S(1)} %get-tuple-element.155.grads_ref, f32[64,512]{1,0:T(8,128)S(1)} %get-tuple-element.156.stats_ref, bf16[768,768]{1,0:T(8,128)(2,1)S(1)} %get-tuple-element.136.kbuf, bf16[768,768]{1,0:T(8,128)(2,1)S(1)} %get-tuple-element.137.vbuf, ...), custom_call_target="tpu_custom_call" | custom-call | flops 1000000000 | bytes 3000000 | tf_op jit(solution)/shard_map/key_back_2/pallas_call | solution.py:968
  49.1 1.1 %unpack.1 = (bf16[192,768]{1,0:T(8,128)(2,1)}, f32[64,768]{1,0:T(8,128)}, f32[64]{0:T(128)}, f32[64,768]{1,0:T(8,128)}, f32[768]{0:T(1024)}, /*index=5*/f32[768]...) custom-call(bf16[4,200,128]{2,1,0:T(8,128)(2,1)S(1)} %pad_maximum_fu, ...), custom_call_target="tpu_custom_call" | custom-call | tf_op jit(solution)/shard_map/unpack/pallas_call | solution.py:1014
  (30 shorter events, 1.7 us)
Async XLA Ops:
  0.6 1.9 %collective-permute-start = (bf16[192,768]{1,0:T(8,128)(2,1)}, bf16[192,768]{1,0:T(8,128)(2,1)S(1)}, u32[]{:S(2)}, u32[]{:S(2)}) collective-permute-start(bf16[192,768]{1,0:T(8,128)(2,1)} %bitcast.24), channel_id=1, source_target_pairs={{0,1},{1,0},{2,3},{3,2},{4,5},{5,4},{6,7},{7,6},{8,9},{9,8},{10,11... | collective-permute-start | bytes 884744 | tf_op jit(solution)/shard_map/ppermute | solution.py:789
  2.6 7.4 %collective-permute-start.1 = (bf16[128,768]{1,0:T(8,128)(2,1)S(1)}, bf16[128,768]{1,0:T(8,128)(2,1)S(1)}, u32[]{:S(2)}, u32[]{:S(2)}) collective-permute-start(bf16[128,768]{1,0:T(8,128)(2,1)S(1)} %pad_maximum_fusion.2), channel_id=1, source_target_pairs={{0,2},{1,3},{2,0},{3,1},{4,6},{5,7},{6,4},{7,5},{8,10},{9,11},{10,... | collective-permute-start | bytes 589832 | tf_op jit(solution)/shard_map/ppermute | solution.py:789
  9.9 2.4 %collective-permute-start.2 = (bf16[128,768]{1,0:T(8,128)(2,1)S(1)}, bf16[128,768]{1,0:T(8,128)(2,1)S(1)}, u32[]{:S(2)}, u32[]{:S(2)}) collective-permute-start(bf16[128,768]{1,0:T(8,128)(2,1)S(1)} %collective-permute-done.1.far_ref), channel_id=1, source_target_pairs={{0,1},{1,0},{2,3},{3,2},{4,5},{5,4},{6,7},{7,6},{8,9},{9,8},{10,11... | collective-permute-start | bytes 589832 | tf_op jit(solution)/shard_map/ppermute | solution.py:789
  22.2 1.5 %collective-permute-start.3 = (bf16[4,200,128]{2,1,0:T(8,128)(2,1)S(1)}, bf16[4,200,128]{2,1,0:T(8,128)(2,1)S(1)}, u32[]{:S(2)}, u32[]{:S(2)}) collective-permute-start(bf16[4,200,128]{2,1,0:T(8,128)(2,1)S(1)} %get-tuple-element.129), channel_id=1, source_target_pairs={{0,1},{1,0},{2,3},{3,2},{4,5},{5,4},{6,7},{7,6},{8,9},{9,8},{10,11... | collective-permute-start | bytes 614408 | tf_op jit(solution)/shard_map/ppermute | solution.py:792
  23.8 6.0 %collective-permute-start.7 = (bf16[224,768]{1,0:T(8,128)(2,1)S(1)}, bf16[224,768]{1,0:T(8,128)(2,1)S(1)}, u32[]{:S(2)}, u32[]{:S(2)}) collective-permute-start(bf16[224,768]{1,0:T(8,128)(2,1)S(1)} %get-tuple-element.148.pack_ref.own_ref), channel_id=1, source_target_pairs={{0,1},{1,0},{2,3},{3,2},{4,5},{5,4},{6,7},{7,6},{8,9},{9,8},{10,11... | collective-permute-start | bytes 1032200 | tf_op jit(solution)/shard_map/ppermute | solution.py:789
  24.1 4.9 %collective-permute-start.6 = (bf16[200,128]{1,0:T(8,128)(2,1)S(1)}, bf16[200,128]{1,0:T(8,128)(2,1)S(1)}, u32[]{:S(2)}, u32[]{:S(2)}) collective-permute-start(bf16[200,128]{1,0:T(8,128)(2,1)S(1)} %get-tuple-element.184), channel_id=1, source_target_pairs={{0,6},{1,7},{2,4},{3,5},{4,2},{5,3},{6,0},{7,1},{8,14},{9,15},{10,... | collective-permute-start | bytes 153608 | tf_op jit(solution)/shard_map/ppermute | solution.py:792
  26.5 3.1 %collective-permute-start.5 = (bf16[200,128]{1,0:T(8,128)(2,1)S(1)}, bf16[200,128]{1,0:T(8,128)(2,1)S(1)}, u32[]{:S(2)}, u32[]{:S(2)}) collective-permute-start(bf16[200,128]{1,0:T(8,128)(2,1)S(1)} %get-tuple-element.185), channel_id=1, source_target_pairs={{0,2},{1,3},{2,0},{3,1},{4,6},{5,7},{6,4},{7,5},{8,10},{9,11},{10,... | collective-permute-start | bytes 153608 | tf_op jit(solution)/shard_map/ppermute | solution.py:792
  26.8 3.0 %collective-permute-start.4 = (bf16[200,128]{1,0:T(8,128)(2,1)S(1)}, bf16[200,128]{1,0:T(8,128)(2,1)S(1)}, u32[]{:S(2)}, u32[]{:S(2)}) collective-permute-start(bf16[200,128]{1,0:T(8,128)(2,1)S(1)} %get-tuple-element.186), channel_id=1, source_target_pairs={{0,4},{1,5},{2,6},{3,7},{4,0},{5,1},{6,2},{7,3},{8,12},{9,13},{10,... | collective-permute-start | bytes 153608 | tf_op jit(solution)/shard_map/ppermute | solution.py:792
  29.8 3.1 %collective-permute-start.8 = (bf16[200,128]{1,0:T(8,128)(2,1)S(1)}, bf16[200,128]{1,0:T(8,128)(2,1)S(1)}, u32[]{:S(2)}, u32[]{:S(2)}) collective-permute-start(bf16[200,128]{1,0:T(8,128)(2,1)S(1)} %fusion.2), channel_id=1, source_target_pairs={{0,8},{1,9},{2,10},{3,11},{4,12},{5,13},{6,14},{7,15},{8,0},{9,1},... | collective-permute-start | bytes 153608 | tf_op jit(solution)/shard_map/ppermute | solution.py:792
  31.2 5.6 %collective-permute-start.10 = (bf16[160,768]{1,0:T(8,128)(2,1)S(1)}, bf16[160,768]{1,0:T(8,128)(2,1)S(1)}, u32[]{:S(2)}, u32[]{:S(2)}) collective-permute-start(bf16[160,768]{1,0:T(8,128)(2,1)S(1)} %pad_maximum_fusion), channel_id=1, source_target_pairs={{0,2},{1,3},{2,0},{3,1},{4,6},{5,7},{6,4},{7,5},{8,10},{9,11},{10,... | collective-permute-start | bytes 737288 | tf_op jit(solution)/shard_map/ppermute | solution.py:789
  32.9 7.5 %collective-permute-start.9 = (bf16[200,128]{1,0:T(8,128)(2,1)S(1)}, bf16[200,128]{1,0:T(8,128)(2,1)S(1)}, u32[]{:S(2)}, u32[]{:S(2)}) collective-permute-start(bf16[200,128]{1,0:T(8,128)(2,1)S(1)} %add_convert_fusion.2), channel_id=1, source_target_pairs={{0,16},{1,17},{2,18},{3,19},{4,20},{5,21},{6,22},{7,23},{8,24},{9,... | collective-permute-start | bytes 153608 | tf_op jit(solution)/shard_map/ppermute | solution.py:792
  36.8 6.4 %collective-permute-start.14 = (bf16[160,768]{1,0:T(8,128)(2,1)S(1)}, bf16[160,768]{1,0:T(8,128)(2,1)S(1)}, u32[]{:S(2)}, u32[]{:S(2)}) collective-permute-start(bf16[160,768]{1,0:T(8,128)(2,1)S(1)} %collective-permute-done.10.far_ref), channel_id=1, source_target_pairs={{0,1},{1,0},{2,3},{3,2},{4,5},{5,4},{6,7},{7,6},{8,9},{9,8},{10,11... | collective-permute-start | bytes 737288 | tf_op jit(solution)/shard_map/ppermute | solution.py:789
  40.5 5.5 %collective-permute-start.13 = (bf16[200,128]{1,0:T(8,128)(2,1)S(1)}, bf16[200,128]{1,0:T(8,128)(2,1)S(1)}, u32[]{:S(2)}, u32[]{:S(2)}) collective-permute-start(bf16[200,128]{1,0:T(8,128)(2,1)S(1)} %add_convert_fusion.1), channel_id=1, source_target_pairs={{0,6},{1,7},{2,4},{3,5},{4,2},{5,3},{6,0},{7,1},{8,14},{9,15},{10,... | collective-permute-start | bytes 153608 | tf_op jit(solution)/shard_map/ppermute | solution.py:792
  41.6 4.4 %collective-permute-start.12 = (bf16[200,128]{1,0:T(8,128)(2,1)S(1)}, bf16[200,128]{1,0:T(8,128)(2,1)S(1)}, u32[]{:S(2)}, u32[]{:S(2)}) collective-permute-start(bf16[200,128]{1,0:T(8,128)(2,1)S(1)} %add_convert_fusion.1), channel_id=1, source_target_pairs={{0,2},{1,3},{2,0},{3,1},{4,6},{5,7},{6,4},{7,5},{8,10},{9,11},{10,... | collective-permute-start | bytes 153608 | tf_op jit(solution)/shard_map/ppermute | solution.py:792
  42.0 3.9 %collective-permute-start.11 = (bf16[200,128]{1,0:T(8,128)(2,1)S(1)}, bf16[200,128]{1,0:T(8,128)(2,1)S(1)}, u32[]{:S(2)}, u32[]{:S(2)}) collective-permute-start(bf16[200,128]{1,0:T(8,128)(2,1)S(1)} %add_convert_fusion.1), channel_id=1, source_target_pairs={{0,4},{1,5},{2,6},{3,7},{4,0},{5,1},{6,2},{7,3},{8,12},{9,13},{10,... | collective-permute-start | bytes 153608 | tf_op jit(solution)/shard_map/ppermute | solution.py:792
  46.0 3.0 %collective-permute-start.15 = (bf16[4,200,128]{2,1,0:T(8,128)(2,1)S(1)}, bf16[4,200,128]{2,1,0:T(8,128)(2,1)S(1)}, u32[]{:S(2)}, u32[]{:S(2)}) collective-permute-start(bf16[4,200,128]{2,1,0:T(8,128)(2,1)S(1)} %pad_maximum_fusion.1.here_ref), channel_id=1, source_target_pairs={{0,1},{1,0},{2,3},{3,2},{4,5},{5,4},{6,7},{7,6},{8,9},{9,8},{10,11... | collective-permute-start | bytes 614408 | tf_op jit(solution)/shard_map/ppermute | solution.py:792

commit v7 on v6

--- a/solution.py
+++ b/solution.py
@@ -171,7 +171,7 @@
     winner_hbm,
     *refs,
 ):
-    rest = (len(refs) - 17) // 2
+    rest = (len(refs) - 20) // 2
     smalls_hbm, refs, sems = refs[:rest], refs[rest:-1], refs[-1]
     project_rows(
         len_ref,
@@ -179,8 +179,8 @@
         own_ref,
         mate_ref,
         (wq_hbm, wk_hbm, wv_hbm, wout_hbm, winner_hbm),
-        *refs[:16],
-        tuple(zip(smalls_hbm, refs[16:])),
+        *refs[:19],
+        tuple(zip(smalls_hbm, refs[19:])),
         sems,
     )
 
@@ -207,6 +207,9 @@
     wv_ref,
     wout_ref,
     winner_ref,
+    sums_ref,
+    tops_ref,
+    totals_ref,
     smalls,
     sems,
 ):
@@ -254,6 +257,9 @@
         product = (nn(both, weight[...]) * scale).astype(BF16)
         out[pl.ds(mine, rows), :] = product[:rows]
         out[pl.ds(other, rows), :] = product[rows:]
+    near_attention(
+        (0,), q_ref, k_ref, v_ref, (near_a_ref, near_b_ref), sums_ref, tops_ref, totals_ref
+    )
     for copy in copies[3:]:
         copy.wait()
 
@@ -265,6 +271,31 @@
     return jnp.concatenate(
         [jnp.where(left, parts[0], parts[1]), jnp.where(left, parts[2], parts[3])], axis=1
     )
+
+
+def near_attention(groups, q_ref, kpair_ref, vpair_ref, masks, sums_ref, tops_ref, totals_ref):
+    block = lax.axis_index("blk")
+    rows = sums_ref.shape[0]
+    core = block % 2
+    at_a, at_b = own_rows(block)
+    near_a, near_b = near_places(block)
+    near_a_ref, near_b_ref = masks
+    for at, count, near, bias_ref, at_stat in (
+        (at_a, ROWS_A, near_a, near_a_ref, 0),
+        (at_b, ROWS_B, near_b, near_b_ref, GROUP * ROWS_A),
+    ):
+        stacked = pl.ds(at_stat, GROUP * count)
+        for index, group in enumerate(groups):
+            columns = slice(group * WIDE, (group + 1) * WIDE)
+            queries = spread_heads(q_ref[pl.ds(core * rows + at, count), columns])
+            scores = masked(nt(queries, kpair_ref[pl.ds(near, HALF), columns]), bias_ref[...])
+            top = jnp.max(scores, axis=-1, keepdims=True)
+            weights = jnp.exp(scores - top)
+            total = jnp.sum(weights, axis=-1, keepdims=True)
+            sums = nn(weights.astype(BF16), vpair_ref[pl.ds(near, HALF), columns])
+            sums_ref[pl.ds(at, count), index * WIDE : (index + 1) * WIDE] = join_heads(sums)
+            tops_ref[index, stacked, :] = jnp.broadcast_to(top, (GROUP * count, 128))
+            totals_ref[index, stacked, :] = jnp.broadcast_to(total, (GROUP * count, 128))
 
 
 def near_kernel(
@@ -284,27 +315,16 @@
 ):
     kfar_ref[...] = nn(far_ref[...], wk_ref[...]).astype(BF16)
     vfar_ref[...] = nn(far_ref[...], wv_ref[...]).astype(BF16)
-    block = lax.axis_index("blk")
-    rows, width = sums_ref.shape
-    core = block % 2
-    at_a, at_b = own_rows(block)
-    near_a, near_b = near_places(block)
-    for at, count, near, bias_ref, at_stat in (
-        (at_a, ROWS_A, near_a, near_a_ref, 0),
-        (at_b, ROWS_B, near_b, near_b_ref, GROUP * ROWS_A),
-    ):
-        stacked = pl.ds(at_stat, GROUP * count)
-        for group in range(width // WIDE):
-            columns = slice(group * WIDE, (group + 1) * WIDE)
-            queries = spread_heads(q_ref[pl.ds(core * rows + at, count), columns])
-            scores = masked(nt(queries, kpair_ref[pl.ds(near, HALF), columns]), bias_ref[...])
-            top = jnp.max(scores, axis=-1, keepdims=True)
-            weights = jnp.exp(scores - top)
-            total = jnp.sum(weights, axis=-1, keepdims=True)
-            sums = nn(weights.astype(BF16), vpair_ref[pl.ds(near, HALF), columns])
-            sums_ref[pl.ds(at, count), columns] = join_heads(sums)
-            tops_ref[group, stacked, :] = jnp.broadcast_to(top, (GROUP * count, 128))
-            totals_ref[group, stacked, :] = jnp.broadcast_to(total, (GROUP * count, 128))
+    near_attention(
+        tuple(range(1, q_ref.shape[1] // WIDE)),
+        q_ref,
+        kpair_ref,
+        vpair_ref,
+        (near_a_ref, near_b_ref),
+        sums_ref,
+        tops_ref,
+        totals_ref,
+    )
 
 
 def main_kernel(
@@ -315,6 +335,9 @@
     vpair_ref,
     kfar_ref,
     vfar_ref,
+    sums0_ref,
+    tops0_ref,
+    totals0_ref,
     sums_ref,
     tops_ref,
     totals_ref,
@@ -403,15 +426,21 @@
             columns = slice(group * WIDE, (group + 1) * WIDE)
             queries = spread_heads(q_ref[pl.ds(core * rows + at, count), columns])
             scores = masked(nt(queries, kbuf[pl.ds(far_at, HALF), columns]), bias_ref[...])
-            top_near = tops_ref[group, stacked, :]
+            near_sums = sums0_ref if group == 0 else sums_ref
+            near_tops = tops0_ref if group == 0 else tops_ref
+            near_totals = totals0_ref if group == 0 else totals_ref
+            held = max(group - 1, 0)
+            top_near = near_tops[held, stacked, :]
             top = jnp.maximum(top_near, jnp.max(scores, axis=-1, keepdims=True))
             weights = jnp.exp(scores - jnp.concatenate([top, top], axis=1))
             shrink = jnp.exp(top_near - top)
-            total = shrink * totals_ref[group, stacked, :] + jnp.sum(
+            total = shrink * near_totals[held, stacked, :] + jnp.sum(
                 weights, axis=-1, keepdims=True
             )
             sums = join_heads(nn(weights.astype(BF16), vbuf[pl.ds(far_at, HALF), columns]))
-            sums = sums + sums_ref[pl.ds(at, count), columns] * over_heads(shrink)
+            sums = sums + near_sums[
+                pl.ds(at, count), held * WIDE : (held + 1) * WIDE
+            ] * over_heads(shrink)
             pieces.append(sums * over_heads(1.0 / total))
             log_total = top + jnp.log(total)
             for head in range(GROUP):
@@ -852,16 +881,21 @@
         wv_here,
         wout_here,
         winner_here,
+        sums0,
+        tops0,
+        totals0,
         *smalls_here,
     ) = pl.pallas_call(
         project_kernel,
         in_specs=[SMEM] * 2 + [VMEM] * 2 + [HBM] * (5 + len(smalls)),
-        out_specs=[VMEM] * (16 + len(smalls)),
+        out_specs=[VMEM] * (19 + len(smalls)),
         out_shape=[vmem((2 * rows, width), BF16)] * 3
         + mask_shapes
         + half_mask_shapes
         + [vmem((width, width), BF16)] * 4
         + [vmem((width, hidden), BF16)]
+        + [vmem((rows, WIDE), F32)]
+        + [vmem((1, GROUP * rows, 128), F32)] * 2
         + [vmem(small.shape, small.dtype) for small in smalls],
         scratch_shapes=[pltpu.SemaphoreType.DMA((5 + len(smalls),))],
         compiler_params=params(4),
@@ -885,8 +919,8 @@
         in_specs=[VMEM] * 8,
         out_specs=[VMEM] * 5,
         out_shape=[vmem((SHARE, width), BF16)] * 2
-        + [vmem((rows, width), F32)]
-        + [vmem((width // WIDE, GROUP * rows, 128), F32)] * 2,
+        + [vmem((rows, width - WIDE), F32)]
+        + [vmem((width // WIDE - 1, GROUP * rows, 128), F32)] * 2,
         compiler_params=params(5),
         cost_estimate=cost(1.0, 2.0),
         name="near",
@@ -895,7 +929,7 @@
     part_rows = width // 256 * (adapt + 2) + 2
     mixed, kbuf, vbuf, lse, du1, attended, grad_pre, keep, send = pl.pallas_call(
         main_kernel,
-        in_specs=[VMEM] * 29 + [HBM],
+        in_specs=[VMEM] * 32 + [HBM],
         out_specs=[HBM] + [VMEM] * 8,
         out_shape=[
             shape((rows, width), BF16),
@@ -927,6 +961,9 @@
         vpair,
         kfar,
         vfar,
+        sums0,
+        tops0,
+        totals0,
         sums,
         tops,
         totals,

time: 50.5 us -> 50.3 us (level)
  transfers between devices with their start and end apart: 16 -> 16, of which waited for: 5 -> 4; matrix products, arithmetic and copies ran while one was open for 0% -> 0% of each run, Pallas kernels for 32% -> 32%
where the time goes in v7:
time: 50.3 us; the launch traced here: 50.2 us
  Pallas kernels  27.2 us (54%)
  starting transfers between devices  19.8 us (39%)
  waiting for transfers between devices  1.9 us (4%)
  between operations  1.03 us (2%)
    ppermute x10, starting transfers between devices, swap_all(): lax.ppermute(array, ('dp', 'blk'), [(i, i ^ mask) for i in range(4 * dp_s...  10.9 us
    pallas_call x1, Pallas kernels, body(): pl.pallas_call(main_kernel, in_specs=[VMEM] * 32 + [HBM], out_specs=[HBM]...  9.83 us
    ppermute x6, starting transfers between devices, swap(): return lax.ppermute(array, 'blk', [(i, i ^ mask) for i in range(4)])  8.88 us
    pallas_call x1, Pallas kernels, body(): pl.pallas_call(project_kernel, in_specs=[SMEM] * 2 + [VMEM] * 2 + [HBM] *...  5.05 us
    pallas_call x2, Pallas kernels, key_back(): pl.pallas_call(functools.partial(key_back_kernel, groups), in_specs=[VMEM...  4.05 us
    pallas_call x2, Pallas kernels, query_back(): pl.pallas_call(functools.partial(query_back_kernel, groups), in_specs=[VM...  3.53 us
    pallas_call x1, Pallas kernels, body(): pl.pallas_call(near_kernel, in_specs=[VMEM] * 8, out_specs=[VMEM] * 5, ou...  1.32 us
    ppermute x10, waiting for transfers between devices, swap_all(): lax.ppermute(array, ('dp', 'blk'), [(i, i ^ mask) for i in range(4 * dp_s...  1.12 us
  transfers between devices with their start and end apart: 16, of which 4 were waited for; matrix products, arithmetic and copies ran while one was open for 0% of the time, Pallas kernels for 32%

profile of v7, /device:TPU:1, one launch (start us, length us, event | category | flops | bytes accessed | tf_op | source)
XLA Modules:
  0.0 50.2 jit_solution(1696857395253838453)
XLA Ops:
  0.8 1.0 %fetch.1.own_ref = bf16[192,768]{1,0:T(8,128)(2,1)S(1)} custom-call(bf16[192,768]{1,0:T(8,128)(2,1)} %bitcast.25), custom_call_target="tpu_custom_call" | custom-call | flops 100000000 | bytes 1000000 | tf_op jit(solution)/shard_map/fetch/pallas_call | solution.py:826
  1.7 0.8 %collective-permute-done.mate_ref = bf16[192,768]{1,0:T(8,128)(2,1)S(1)} collective-permute-done((bf16[192,768]{1,0:T(8,128)(2,1)}, bf16[192,768]{1,0:T(8,128)(2,1)S(1)}, u32[]{:S(2)}, u32[]{:S(2)}) %collective-permute-start) | collective-permute-done | bytes 294944 | tf_op jit(solution)/shard_map/ppermute | solution.py:818
  2.6 2.4 %collective-permute-start.1 = (bf16[128,768]{1,0:T(8,128)(2,1)S(1)}, bf16[128,768]{1,0:T(8,128)(2,1)S(1)}, u32[]{:S(2)}, u32[]{:S(2)}) collective-permute-start(bf16[128,768]{1,0:T(8,128)(2,1)S(1)} %pad_maximum_fusion.2), channel_id=1, source_target_pairs={{0,2},{1,3},{2,0},{3,1},{4,6},{5,7},{6,4},{7,5},{8,10},{9,11},{10,... | collective-permute-start | bytes 589832 | tf_op jit(solution)/shard_map/ppermute | solution.py:818
  5.0 5.0 %project.1 = (bf16[384,768]{1,0:T(8,128)(2,1)S(1)}, bf16[384,768]{1,0:T(8,128)(2,1)S(1)}, bf16[384,768]{1,0:T(8,128)(2,1)S(1)}, f32[64,512]{1,0:T(8,128)S(1)}, f...) custom-call(s32[1,6]{1,0:T(1,128)} %len_ref.1, ...), custom_call_target="tpu_custom_call" | custom-call | flops 2000000000 | bytes 12000000 | tf_op jit(solution)/shard_map/project/pallas_call | solution.py:888
  10.0 0.8 %collective-permute-start.2 = (bf16[128,768]{1,0:T(8,128)(2,1)S(1)}, bf16[128,768]{1,0:T(8,128)(2,1)S(1)}, u32[]{:S(2)}, u32[]{:S(2)}) collective-permute-start(bf16[128,768]{1,0:T(8,128)(2,1)S(1)} %collective-permute-done.1.far_ref), channel_id=1, source_target_pairs={{0,1},{1,0},{2,3},{3,2},{4,5},{5,4},{6,7},{7,6},{8,9},{9,8},{10,11... | collective-permute-start | bytes 589832 | tf_op jit(solution)/shard_map/ppermute | solution.py:818
  10.8 1.3 %near.1 = (bf16[128,768]{1,0:T(8,128)(2,1)S(1)}, bf16[128,768]{1,0:T(8,128)(2,1)S(1)}, f32[192,512]{1,0:T(8,128)S(1)}, f32[2,768,128]{2,1,0:T(8,128)S(1)}, f32[2,768,128]{2,1,0:T(8,128)S(1)}) custom-call(bf16[128,768]{1,0:T(8,128)(2,1)S(1)} %collective-permute-done.1.far_ref, bf16[384,768]{1,0:T(8,128)(2,1)S(1)} %get-tuple-element.100.q_ref, ...), custom_call_target="tpu_custom_call" | custom-call | flops 1000000000 | bytes 2000000 | tf_op jit(solution)/shard_map/near/pallas_call | solution.py:917
  12.2 9.8 %layer.1 = (bf16[192,768]{1,0:T(8,128)(2,1)}, bf16[768,768]{1,0:T(8,128)(2,1)S(1)}, bf16[768,768]{1,0:T(8,128)(2,1)S(1)}, f32[192,128]{1,0:T(8,128)S(1)}, f32[19...) custom-call(bf16[192,768]{1,0:T(8,128)(2,1)S(1)} %fetch.1.own_ref, ...), custom_call_target="tpu_custom_call" | custom-call | flops 8000000000 | bytes 20000000 | tf_op jit(solution)/shard_map/layer/pallas_call | solution.py:930
  22.1 1.1 %attended_back.1 = (bf16[224,768]{1,0:T(8,128)(2,1)S(1)}, f32[192,128]{1,0:T(8,128)S(1)}) custom-call(f32[192,768]{1,0:T(8,128)S(1)} %get-tuple-element.147.du1_ref.part_in_ref, bf16[192,64]{1,0:T(8,128)(2,1)S(1)} %get-tuple-element.137.grad_pre_ref, bf16[64,768]{1,0:T(8,128)(2,1)S(1)} %get-tuple-element.119.down1_ref, ...), custom_call_target="tpu_custom_call" | custom-call | flops 500000000 | bytes 2000000 | tf_op jit(solution)/shard_map/attended_back/pallas_call | solution.py:983
  23.2 0.3 collective-permute-done.3
  23.8 2.5 %collective-permute-start.6 = (bf16[200,128]{1,0:T(8,128)(2,1)S(1)}, bf16[200,128]{1,0:T(8,128)(2,1)S(1)}, u32[]{:S(2)}, u32[]{:S(2)}) collective-permute-start(bf16[200,128]{1,0:T(8,128)(2,1)S(1)} %get-tuple-element.190), channel_id=1, source_target_pairs={{0,6},{1,7},{2,4},{3,5},{4,2},{5,3},{6,0},{7,1},{8,14},{9,15},{10,... | collective-permute-start | bytes 153608 | tf_op jit(solution)/shard_map/ppermute | solution.py:821
  26.7 2.0 %query_back_0.1 = (bf16[768,256]{1,0:T(8,128)(2,1)S(1)}, bf16[768,256]{1,0:T(8,128)(2,1)S(1)}, f32[192,768]{1,0:T(8,128)S(1)}) custom-call(bf16[128,768]{1,0:T(8,128)(2,1)S(1)} %collective-permute-done.1.far_ref, bf16[128,768]{1,0:T(8,128)(2,1)S(1)} %collective-permute-done.2.far_mate_ref, bf16[384,768]{1,0:T(8,128)(2,1)S(1)} %get-tuple-element.100.q_ref, ...), custom_call_target="tpu_custom_call" | custom-call | flops 2000000000 | bytes 3000000 | tf_op jit(solution)/shard_map/query_back_0/pallas_call | solution.py:994
  28.8 0.7 %collective-permute-done.5 = bf16[200,128]{1,0:T(8,128)(2,1)S(1)} collective-permute-done((bf16[200,128]{1,0:T(8,128)(2,1)S(1)}, bf16[200,128]{1,0:T(8,128)(2,1)S(1)}, u32[]{:S(2)}, u32[]{:S(2)}) %collective-permute-start.5) | collective-permute-done | bytes 51232 | tf_op jit(solution)/shard_map/ppermute | solution.py:821
  29.6 1.4 %collective-permute-start.8 = (bf16[200,128]{1,0:T(8,128)(2,1)S(1)}, bf16[200,128]{1,0:T(8,128)(2,1)S(1)}, u32[]{:S(2)}, u32[]{:S(2)}) collective-permute-start(bf16[200,128]{1,0:T(8,128)(2,1)S(1)} %fusion.2), channel_id=1, source_target_pairs={{0,8},{1,9},{2,10},{3,11},{4,12},{5,13},{6,14},{7,15},{8,0},{9,1},... | collective-permute-start | bytes 153608 | tf_op jit(solution)/shard_map/ppermute | solution.py:821
  31.0 1.7 %collective-permute-start.10 = (bf16[160,768]{1,0:T(8,128)(2,1)S(1)}, bf16[160,768]{1,0:T(8,128)(2,1)S(1)}, u32[]{:S(2)}, u32[]{:S(2)}) collective-permute-start(bf16[160,768]{1,0:T(8,128)(2,1)S(1)} %pad_maximum_fusion), channel_id=1, source_target_pairs={{0,2},{1,3},{2,0},{3,1},{4,6},{5,7},{6,4},{7,5},{8,10},{9,11},{10,... | collective-permute-start | bytes 737288 | tf_op jit(solution)/shard_map/ppermute | solution.py:818
  32.7 2.4 %collective-permute-start.9 = (bf16[200,128]{1,0:T(8,128)(2,1)S(1)}, bf16[200,128]{1,0:T(8,128)(2,1)S(1)}, u32[]{:S(2)}, u32[]{:S(2)}) collective-permute-start(bf16[200,128]{1,0:T(8,128)(2,1)S(1)} %add_convert_fusion.2), channel_id=1, source_target_pairs={{0,16},{1,17},{2,18},{3,19},{4,20},{5,21},{6,22},{7,23},{8,24},{9,... | collective-permute-start | bytes 153608 | tf_op jit(solution)/shard_map/ppermute | solution.py:821
  35.1 1.5 %query_back_2.1 = (bf16[768,256]{1,0:T(8,128)(2,1)S(1)}, f32[192,768]{1,0:T(8,128)S(1)}) custom-call(bf16[128,768]{1,0:T(8,128)(2,1)S(1)} %collective-permute-done.1.far_ref, bf16[128,768]{1,0:T(8,128)(2,1)S(1)} %collective-permute-done.2.far_mate_ref, bf16[384,768]{1,0:T(8,128)(2,1)S(1)} %get-tuple-element.100.q_ref, ...), custom_call_target="tpu_custom_call" | custom-call | flops 1000000000 | bytes 3000000 | tf_op jit(solution)/shard_map/query_back_2/pallas_call | solution.py:994
  36.6 3.6 %collective-permute-start.14 = (bf16[160,768]{1,0:T(8,128)(2,1)S(1)}, bf16[160,768]{1,0:T(8,128)(2,1)S(1)}, u32[]{:S(2)}, u32[]{:S(2)}) collective-permute-start(bf16[160,768]{1,0:T(8,128)(2,1)S(1)} %collective-permute-done.10.far_ref), channel_id=1, source_target_pairs={{0,1},{1,0},{2,3},{3,2},{4,5},{5,4},{6,7},{7,6},{8,9},{9,8},{10,11... | collective-permute-start | bytes 737288 | tf_op jit(solution)/shard_map/ppermute | solution.py:818
  40.2 1.1 %collective-permute-start.13 = (bf16[200,128]{1,0:T(8,128)(2,1)S(1)}, bf16[200,128]{1,0:T(8,128)(2,1)S(1)}, u32[]{:S(2)}, u32[]{:S(2)}) collective-permute-start(bf16[200,128]{1,0:T(8,128)(2,1)S(1)} %add_convert_fusion.1), channel_id=1, source_target_pairs={{0,6},{1,7},{2,4},{3,5},{4,2},{5,3},{6,0},{7,1},{8,14},{9,15},{10,... | collective-permute-start | bytes 153608 | tf_op jit(solution)/shard_map/ppermute | solution.py:821
  41.4 0.5 collective-permute-start.12
  41.8 1.1 %collective-permute-start.11 = (bf16[200,128]{1,0:T(8,128)(2,1)S(1)}, bf16[200,128]{1,0:T(8,128)(2,1)S(1)}, u32[]{:S(2)}, u32[]{:S(2)}) collective-permute-start(bf16[200,128]{1,0:T(8,128)(2,1)S(1)} %add_convert_fusion.1), channel_id=1, source_target_pairs={{0,4},{1,5},{2,6},{3,7},{4,0},{5,1},{6,2},{7,3},{8,12},{9,13},{10,... | collective-permute-start | bytes 153608 | tf_op jit(solution)/shard_map/ppermute | solution.py:821
  43.1 2.6 %key_back_0.1.part_ref = f32[192,768]{1,0:T(8,128)S(1)} custom-call(bf16[768,768]{1,0:T(8,128)(2,1)S(1)} %get-tuple-element.161.grads_ref, f32[64,512]{1,0:T(8,128)S(1)} %get-tuple-element.162.stats_ref, bf16[768,768]{1,0:T(8,128)(2,1)S(1)} %get-tuple-element.142.kbuf, bf16[768,768]{1,0:T(8,128)(2,1)S(1)} %get-tuple-element.143.vbuf, ...), custom_call_target="tpu_custom_call" | custom-call | flops 2000000000 | bytes 3000000 | tf_op jit(solution)/shard_map/key_back_0/pallas_call | solution.py:1005
  45.8 1.6 %collective-permute-start.15 = (bf16[4,200,128]{2,1,0:T(8,128)(2,1)S(1)}, bf16[4,200,128]{2,1,0:T(8,128)(2,1)S(1)}, u32[]{:S(2)}, u32[]{:S(2)}) collective-permute-start(bf16[4,200,128]{2,1,0:T(8,128)(2,1)S(1)} %pad_maximum_fusion.1.here_ref), channel_id=1, source_target_pairs={{0,1},{1,0},{2,3},{3,2},{4,5},{5,4},{6,7},{7,6},{8,9},{9,8},{10,11... | collective-permute-start | bytes 614408 | tf_op jit(solution)/shard_map/ppermute | solution.py:821
  47.4 1.5 %key_back_2.1.grad_ref = bf16[192,768]{1,0:T(8,128)(2,1)S(1)} custom-call(bf16[768,768]{1,0:T(8,128)(2,1)S(1)} %get-tuple-element.161.grads_ref, f32[64,512]{1,0:T(8,128)S(1)} %get-tuple-element.162.stats_ref, bf16[768,768]{1,0:T(8,128)(2,1)S(1)} %get-tuple-element.142.kbuf, bf16[768,768]{1,0:T(8,128)(2,1)S(1)} %get-tuple-element.143.vbuf, ...), custom_call_target="tpu_custom_call" | custom-call | flops 1000000000 | bytes 3000000 | tf_op jit(solution)/shard_map/key_back_2/pallas_call | solution.py:1005
  48.9 1.1 %unpack.1 = (bf16[192,768]{1,0:T(8,128)(2,1)}, f32[64,768]{1,0:T(8,128)}, f32[64]{0:T(128)}, f32[64,768]{1,0:T(8,128)}, f32[768]{0:T(1024)}, /*index=5*/f32[768]...) custom-call(bf16[4,200,128]{2,1,0:T(8,128)(2,1)S(1)} %pad_maximum_fu, ...), custom_call_target="tpu_custom_call" | custom-call | tf_op jit(solution)/shard_map/unpack/pallas_call | solution.py:1051
  (30 shorter events, 1.4 us)
Async XLA Ops:
  0.6 1.9 %collective-permute-start = (bf16[192,768]{1,0:T(8,128)(2,1)}, bf16[192,768]{1,0:T(8,128)(2,1)S(1)}, u32[]{:S(2)}, u32[]{:S(2)}) collective-permute-start(bf16[192,768]{1,0:T(8,128)(2,1)} %bitcast.24), channel_id=1, source_target_pairs={{0,1},{1,0},{2,3},{3,2},{4,5},{5,4},{6,7},{7,6},{8,9},{9,8},{10,11... | collective-permute-start | bytes 884744 | tf_op jit(solution)/shard_map/ppermute | solution.py:818
  2.6 7.5 %collective-permute-start.1 = (bf16[128,768]{1,0:T(8,128)(2,1)S(1)}, bf16[128,768]{1,0:T(8,128)(2,1)S(1)}, u32[]{:S(2)}, u32[]{:S(2)}) collective-permute-start(bf16[128,768]{1,0:T(8,128)(2,1)S(1)} %pad_maximum_fusion.2), channel_id=1, source_target_pairs={{0,2},{1,3},{2,0},{3,1},{4,6},{5,7},{6,4},{7,5},{8,10},{9,11},{10,... | collective-permute-start | bytes 589832 | tf_op jit(solution)/shard_map/ppermute | solution.py:818
  10.0 2.1 %collective-permute-start.2 = (bf16[128,768]{1,0:T(8,128)(2,1)S(1)}, bf16[128,768]{1,0:T(8,128)(2,1)S(1)}, u32[]{:S(2)}, u32[]{:S(2)}) collective-permute-start(bf16[128,768]{1,0:T(8,128)(2,1)S(1)} %collective-permute-done.1.far_ref), channel_id=1, source_target_pairs={{0,1},{1,0},{2,3},{3,2},{4,5},{5,4},{6,7},{7,6},{8,9},{9,8},{10,11... | collective-permute-start | bytes 589832 | tf_op jit(solution)/shard_map/ppermute | solution.py:818
  22.0 1.5 %collective-permute-start.3 = (bf16[4,200,128]{2,1,0:T(8,128)(2,1)S(1)}, bf16[4,200,128]{2,1,0:T(8,128)(2,1)S(1)}, u32[]{:S(2)}, u32[]{:S(2)}) collective-permute-start(bf16[4,200,128]{2,1,0:T(8,128)(2,1)S(1)} %get-tuple-element.135), channel_id=1, source_target_pairs={{0,1},{1,0},{2,3},{3,2},{4,5},{5,4},{6,7},{7,6},{8,9},{9,8},{10,11... | collective-permute-start | bytes 614408 | tf_op jit(solution)/shard_map/ppermute | solution.py:821
  23.6 6.0 %collective-permute-start.7 = (bf16[224,768]{1,0:T(8,128)(2,1)S(1)}, bf16[224,768]{1,0:T(8,128)(2,1)S(1)}, u32[]{:S(2)}, u32[]{:S(2)}) collective-permute-start(bf16[224,768]{1,0:T(8,128)(2,1)S(1)} %get-tuple-element.154.pack_ref.own_ref), channel_id=1, source_target_pairs={{0,1},{1,0},{2,3},{3,2},{4,5},{5,4},{6,7},{7,6},{8,9},{9,8},{10,11... | collective-permute-start | bytes 1032200 | tf_op jit(solution)/shard_map/ppermute | solution.py:818
  23.8 4.9 %collective-permute-start.6 = (bf16[200,128]{1,0:T(8,128)(2,1)S(1)}, bf16[200,128]{1,0:T(8,128)(2,1)S(1)}, u32[]{:S(2)}, u32[]{:S(2)}) collective-permute-start(bf16[200,128]{1,0:T(8,128)(2,1)S(1)} %get-tuple-element.190), channel_id=1, source_target_pairs={{0,6},{1,7},{2,4},{3,5},{4,2},{5,3},{6,0},{7,1},{8,14},{9,15},{10,... | collective-permute-start | bytes 153608 | tf_op jit(solution)/shard_map/ppermute | solution.py:821
  26.3 3.1 %collective-permute-start.5 = (bf16[200,128]{1,0:T(8,128)(2,1)S(1)}, bf16[200,128]{1,0:T(8,128)(2,1)S(1)}, u32[]{:S(2)}, u32[]{:S(2)}) collective-permute-start(bf16[200,128]{1,0:T(8,128)(2,1)S(1)} %get-tuple-element.191), channel_id=1, source_target_pairs={{0,2},{1,3},{2,0},{3,1},{4,6},{5,7},{6,4},{7,5},{8,10},{9,11},{10,... | collective-permute-start | bytes 153608 | tf_op jit(solution)/shard_map/ppermute | solution.py:821
  26.6 3.0 %collective-permute-start.4 = (bf16[200,128]{1,0:T(8,128)(2,1)S(1)}, bf16[200,128]{1,0:T(8,128)(2,1)S(1)}, u32[]{:S(2)}, u32[]{:S(2)}) collective-permute-start(bf16[200,128]{1,0:T(8,128)(2,1)S(1)} %get-tuple-element.192), channel_id=1, source_target_pairs={{0,4},{1,5},{2,6},{3,7},{4,0},{5,1},{6,2},{7,3},{8,12},{9,13},{10,... | collective-permute-start | bytes 153608 | tf_op jit(solution)/shard_map/ppermute | solution.py:821
  29.6 3.1 %collective-permute-start.8 = (bf16[200,128]{1,0:T(8,128)(2,1)S(1)}, bf16[200,128]{1,0:T(8,128)(2,1)S(1)}, u32[]{:S(2)}, u32[]{:S(2)}) collective-permute-start(bf16[200,128]{1,0:T(8,128)(2,1)S(1)} %fusion.2), channel_id=1, source_target_pairs={{0,8},{1,9},{2,10},{3,11},{4,12},{5,13},{6,14},{7,15},{8,0},{9,1},... | collective-permute-start | bytes 153608 | tf_op jit(solution)/shard_map/ppermute | solution.py:821
  31.0 5.6 %collective-permute-start.10 = (bf16[160,768]{1,0:T(8,128)(2,1)S(1)}, bf16[160,768]{1,0:T(8,128)(2,1)S(1)}, u32[]{:S(2)}, u32[]{:S(2)}) collective-permute-start(bf16[160,768]{1,0:T(8,128)(2,1)S(1)} %pad_maximum_fusion), channel_id=1, source_target_pairs={{0,2},{1,3},{2,0},{3,1},{4,6},{5,7},{6,4},{7,5},{8,10},{9,11},{10,... | collective-permute-start | bytes 737288 | tf_op jit(solution)/shard_map/ppermute | solution.py:818
  32.7 7.5 %collective-permute-start.9 = (bf16[200,128]{1,0:T(8,128)(2,1)S(1)}, bf16[200,128]{1,0:T(8,128)(2,1)S(1)}, u32[]{:S(2)}, u32[]{:S(2)}) collective-permute-start(bf16[200,128]{1,0:T(8,128)(2,1)S(1)} %add_convert_fusion.2), channel_id=1, source_target_pairs={{0,16},{1,17},{2,18},{3,19},{4,20},{5,21},{6,22},{7,23},{8,24},{9,... | collective-permute-start | bytes 153608 | tf_op jit(solution)/shard_map/ppermute | solution.py:821
  36.6 6.4 %collective-permute-start.14 = (bf16[160,768]{1,0:T(8,128)(2,1)S(1)}, bf16[160,768]{1,0:T(8,128)(2,1)S(1)}, u32[]{:S(2)}, u32[]{:S(2)}) collective-permute-start(bf16[160,768]{1,0:T(8,128)(2,1)S(1)} %collective-permute-done.10.far_ref), channel_id=1, source_target_pairs={{0,1},{1,0},{2,3},{3,2},{4,5},{5,4},{6,7},{7,6},{8,9},{9,8},{10,11... | collective-permute-start | bytes 737288 | tf_op jit(solution)/shard_map/ppermute | solution.py:818
  40.2 5.5 %collective-permute-start.13 = (bf16[200,128]{1,0:T(8,128)(2,1)S(1)}, bf16[200,128]{1,0:T(8,128)(2,1)S(1)}, u32[]{:S(2)}, u32[]{:S(2)}) collective-permute-start(bf16[200,128]{1,0:T(8,128)(2,1)S(1)} %add_convert_fusion.1), channel_id=1, source_target_pairs={{0,6},{1,7},{2,4},{3,5},{4,2},{5,3},{6,0},{7,1},{8,14},{9,15},{10,... | collective-permute-start | bytes 153608 | tf_op jit(solution)/shard_map/ppermute | solution.py:821
  41.4 4.4 %collective-permute-start.12 = (bf16[200,128]{1,0:T(8,128)(2,1)S(1)}, bf16[200,128]{1,0:T(8,128)(2,1)S(1)}, u32[]{:S(2)}, u32[]{:S(2)}) collective-permute-start(bf16[200,128]{1,0:T(8,128)(2,1)S(1)} %add_convert_fusion.1), channel_id=1, source_target_pairs={{0,2},{1,3},{2,0},{3,1},{4,6},{5,7},{6,4},{7,5},{8,10},{9,11},{10,... | collective-permute-start | bytes 153608 | tf_op jit(solution)/shard_map/ppermute | solution.py:821
  41.8 3.9 %collective-permute-start.11 = (bf16[200,128]{1,0:T(8,128)(2,1)S(1)}, bf16[200,128]{1,0:T(8,128)(2,1)S(1)}, u32[]{:S(2)}, u32[]{:S(2)}) collective-permute-start(bf16[200,128]{1,0:T(8,128)(2,1)S(1)} %add_convert_fusion.1), channel_id=1, source_target_pairs={{0,4},{1,5},{2,6},{3,7},{4,0},{5,1},{6,2},{7,3},{8,12},{9,13},{10,... | collective-permute-start | bytes 153608 | tf_op jit(solution)/shard_map/ppermute | solution.py:821
  45.8 3.0 %collective-permute-start.15 = (bf16[4,200,128]{2,1,0:T(8,128)(2,1)S(1)}, bf16[4,200,128]{2,1,0:T(8,128)(2,1)S(1)}, u32[]{:S(2)}, u32[]{:S(2)}) collective-permute-start(bf16[4,200,128]{2,1,0:T(8,128)(2,1)S(1)} %pad_maximum_fusion.1.here_ref), channel_id=1, source_target_pairs={{0,1},{1,0},{2,3},{3,2},{4,5},{5,4},{6,7},{7,6},{8,9},{9,8},{10,11... | collective-permute-start | bytes 614408 | tf_op jit(solution)/shard_map/ppermute | solution.py:821

commit v8 on v7

--- a/solution.py
+++ b/solution.py
@@ -1032,7 +1032,7 @@
     total = add(total, after(arrived, part))
     for mask in masks[2:]:
         total = add(total, swap_all(total, mask))
-    others = [swap_all(total, mask) for mask in (4, 2, 6)]
+    others = [swap_all(total, mask) for mask in (6, 4, 2)]
     grads_row, stats_row = pl.pallas_call(
         gather_kernel,
         in_specs=[VMEM] * 4,
@@ -1043,6 +1043,7 @@
         name="gather",
     )(pack, pack_mate, pack_far, after(pack_far_mate, total))
     part = key_back((0, 1), (qbuf0, qbuf1), after(part, total), F32)
+    others = [others[1], others[2], others[0]]
     here = jnp.stack([total, *lax.optimization_barrier((*others, part))[:3]])
     other = swap_all(here, 1)
     input_grad = key_back((2,), (qbuf2,), after(part, here), BF16)

time: 50.3 us -> 50.3 us (level)
  no operation moved by 1% of the time
where the time goes in v8:
time: 50.3 us; the launch traced here: 50.2 us
  Pallas kernels  27.2 us (54%)
  starting transfers between devices  19.8 us (39%)
  waiting for transfers between devices  1.9 us (4%)
  between operations  1.03 us (2%)
    ppermute x10, starting transfers between devices, swap_all(): lax.ppermute(array, ('dp', 'blk'), [(i, i ^ mask) for i in range(4 * dp_s...  10.9 us
    pallas_call x1, Pallas kernels, body(): pl.pallas_call(main_kernel, in_specs=[VMEM] * 32 + [HBM], out_specs=[HBM]...  9.83 us
    ppermute x6, starting transfers between devices, swap(): return lax.ppermute(array, 'blk', [(i, i ^ mask) for i in range(4)])  8.88 us
    pallas_call x1, Pallas kernels, body(): pl.pallas_call(project_kernel, in_specs=[SMEM] * 2 + [VMEM] * 2 + [HBM] *...  5.05 us
    pallas_call x2, Pallas kernels, key_back(): pl.pallas_call(functools.partial(key_back_kernel, groups), in_specs=[VMEM...  4.05 us
    pallas_call x2, Pallas kernels, query_back(): pl.pallas_call(functools.partial(query_back_kernel, groups), in_specs=[VM...  3.53 us
    pallas_call x1, Pallas kernels, body(): pl.pallas_call(near_kernel, in_specs=[VMEM] * 8, out_specs=[VMEM] * 5, ou...  1.32 us
    ppermute x10, waiting for transfers between devices, swap_all(): lax.ppermute(array, ('dp', 'blk'), [(i, i ^ mask) for i in range(4 * dp_s...  1.12 us
  transfers between devices with their start and end apart: 16, of which 4 were waited for; matrix products, arithmetic and copies ran while one was open for 0% of the time, Pallas kernels for 32%

profile of v8, /device:TPU:1, one launch (start us, length us, event | category | flops | bytes accessed | tf_op | source)
XLA Modules:
  0.0 50.2 jit_solution(1696857395253838453)
XLA Ops:
  0.8 1.0 %fetch.1.own_ref = bf16[192,768]{1,0:T(8,128)(2,1)S(1)} custom-call(bf16[192,768]{1,0:T(8,128)(2,1)} %bitcast.25), custom_call_target="tpu_custom_call" | custom-call | flops 100000000 | bytes 1000000 | tf_op jit(solution)/shard_map/fetch/pallas_call | solution.py:826
  1.7 0.8 %collective-permute-done.mate_ref = bf16[192,768]{1,0:T(8,128)(2,1)S(1)} collective-permute-done((bf16[192,768]{1,0:T(8,128)(2,1)}, bf16[192,768]{1,0:T(8,128)(2,1)S(1)}, u32[]{:S(2)}, u32[]{:S(2)}) %collective-permute-start) | collective-permute-done | bytes 294944 | tf_op jit(solution)/shard_map/ppermute | solution.py:818
  2.6 2.4 %collective-permute-start.1 = (bf16[128,768]{1,0:T(8,128)(2,1)S(1)}, bf16[128,768]{1,0:T(8,128)(2,1)S(1)}, u32[]{:S(2)}, u32[]{:S(2)}) collective-permute-start(bf16[128,768]{1,0:T(8,128)(2,1)S(1)} %pad_maximum_fusion.2), channel_id=1, source_target_pairs={{0,2},{1,3},{2,0},{3,1},{4,6},{5,7},{6,4},{7,5},{8,10},{9,11},{10,... | collective-permute-start | bytes 589832 | tf_op jit(solution)/shard_map/ppermute | solution.py:818
  5.0 5.0 %project.1 = (bf16[384,768]{1,0:T(8,128)(2,1)S(1)}, bf16[384,768]{1,0:T(8,128)(2,1)S(1)}, bf16[384,768]{1,0:T(8,128)(2,1)S(1)}, f32[64,512]{1,0:T(8,128)S(1)}, f...) custom-call(s32[1,6]{1,0:T(1,128)} %len_ref.1, ...), custom_call_target="tpu_custom_call" | custom-call | flops 2000000000 | bytes 12000000 | tf_op jit(solution)/shard_map/project/pallas_call | solution.py:888
  10.0 0.8 %collective-permute-start.2 = (bf16[128,768]{1,0:T(8,128)(2,1)S(1)}, bf16[128,768]{1,0:T(8,128)(2,1)S(1)}, u32[]{:S(2)}, u32[]{:S(2)}) collective-permute-start(bf16[128,768]{1,0:T(8,128)(2,1)S(1)} %collective-permute-done.1.far_ref), channel_id=1, source_target_pairs={{0,1},{1,0},{2,3},{3,2},{4,5},{5,4},{6,7},{7,6},{8,9},{9,8},{10,11... | collective-permute-start | bytes 589832 | tf_op jit(solution)/shard_map/ppermute | solution.py:818
  10.8 1.3 %near.1 = (bf16[128,768]{1,0:T(8,128)(2,1)S(1)}, bf16[128,768]{1,0:T(8,128)(2,1)S(1)}, f32[192,512]{1,0:T(8,128)S(1)}, f32[2,768,128]{2,1,0:T(8,128)S(1)}, f32[2,768,128]{2,1,0:T(8,128)S(1)}) custom-call(bf16[128,768]{1,0:T(8,128)(2,1)S(1)} %collective-permute-done.1.far_ref, bf16[384,768]{1,0:T(8,128)(2,1)S(1)} %get-tuple-element.100.q_ref, ...), custom_call_target="tpu_custom_call" | custom-call | flops 1000000000 | bytes 2000000 | tf_op jit(solution)/shard_map/near/pallas_call | solution.py:917
  12.2 9.8 %layer.1 = (bf16[192,768]{1,0:T(8,128)(2,1)}, bf16[768,768]{1,0:T(8,128)(2,1)S(1)}, bf16[768,768]{1,0:T(8,128)(2,1)S(1)}, f32[192,128]{1,0:T(8,128)S(1)}, f32[19...) custom-call(bf16[192,768]{1,0:T(8,128)(2,1)S(1)} %fetch.1.own_ref, ...), custom_call_target="tpu_custom_call" | custom-call | flops 8000000000 | bytes 20000000 | tf_op jit(solution)/shard_map/layer/pallas_call | solution.py:930
  22.1 1.1 %attended_back.1 = (bf16[224,768]{1,0:T(8,128)(2,1)S(1)}, f32[192,128]{1,0:T(8,128)S(1)}) custom-call(f32[192,768]{1,0:T(8,128)S(1)} %get-tuple-element.147.du1_ref.part_in_ref, bf16[192,64]{1,0:T(8,128)(2,1)S(1)} %get-tuple-element.137.grad_pre_ref, bf16[64,768]{1,0:T(8,128)(2,1)S(1)} %get-tuple-element.119.down1_ref, ...), custom_call_target="tpu_custom_call" | custom-call | flops 500000000 | bytes 2000000 | tf_op jit(solution)/shard_map/attended_back/pallas_call | solution.py:983
  23.2 0.3 collective-permute-done.3
  23.8 2.5 %collective-permute-start.6 = (bf16[200,128]{1,0:T(8,128)(2,1)S(1)}, bf16[200,128]{1,0:T(8,128)(2,1)S(1)}, u32[]{:S(2)}, u32[]{:S(2)}) collective-permute-start(bf16[200,128]{1,0:T(8,128)(2,1)S(1)} %get-tuple-element.190), channel_id=1, source_target_pairs={{0,6},{1,7},{2,4},{3,5},{4,2},{5,3},{6,0},{7,1},{8,14},{9,15},{10,... | collective-permute-start | bytes 153608 | tf_op jit(solution)/shard_map/ppermute | solution.py:821
  26.7 2.0 %query_back_0.1 = (bf16[768,256]{1,0:T(8,128)(2,1)S(1)}, bf16[768,256]{1,0:T(8,128)(2,1)S(1)}, f32[192,768]{1,0:T(8,128)S(1)}) custom-call(bf16[128,768]{1,0:T(8,128)(2,1)S(1)} %collective-permute-done.1.far_ref, bf16[128,768]{1,0:T(8,128)(2,1)S(1)} %collective-permute-done.2.far_mate_ref, bf16[384,768]{1,0:T(8,128)(2,1)S(1)} %get-tuple-element.100.q_ref, ...), custom_call_target="tpu_custom_call" | custom-call | flops 2000000000 | bytes 3000000 | tf_op jit(solution)/shard_map/query_back_0/pallas_call | solution.py:994
  28.8 0.7 %collective-permute-done.5 = bf16[200,128]{1,0:T(8,128)(2,1)S(1)} collective-permute-done((bf16[200,128]{1,0:T(8,128)(2,1)S(1)}, bf16[200,128]{1,0:T(8,128)(2,1)S(1)}, u32[]{:S(2)}, u32[]{:S(2)}) %collective-permute-start.5) | collective-permute-done | bytes 51232 | tf_op jit(solution)/shard_map/ppermute | solution.py:821
  29.6 1.4 %collective-permute-start.8 = (bf16[200,128]{1,0:T(8,128)(2,1)S(1)}, bf16[200,128]{1,0:T(8,128)(2,1)S(1)}, u32[]{:S(2)}, u32[]{:S(2)}) collective-permute-start(bf16[200,128]{1,0:T(8,128)(2,1)S(1)} %fusion.2), channel_id=1, source_target_pairs={{0,8},{1,9},{2,10},{3,11},{4,12},{5,13},{6,14},{7,15},{8,0},{9,1},... | collective-permute-start | bytes 153608 | tf_op jit(solution)/shard_map/ppermute | solution.py:821
  31.0 1.7 %collective-permute-start.10 = (bf16[160,768]{1,0:T(8,128)(2,1)S(1)}, bf16[160,768]{1,0:T(8,128)(2,1)S(1)}, u32[]{:S(2)}, u32[]{:S(2)}) collective-permute-start(bf16[160,768]{1,0:T(8,128)(2,1)S(1)} %pad_maximum_fusion), channel_id=1, source_target_pairs={{0,2},{1,3},{2,0},{3,1},{4,6},{5,7},{6,4},{7,5},{8,10},{9,11},{10,... | collective-permute-start | bytes 737288 | tf_op jit(solution)/shard_map/ppermute | solution.py:818
  32.7 2.4 %collective-permute-start.9 = (bf16[200,128]{1,0:T(8,128)(2,1)S(1)}, bf16[200,128]{1,0:T(8,128)(2,1)S(1)}, u32[]{:S(2)}, u32[]{:S(2)}) collective-permute-start(bf16[200,128]{1,0:T(8,128)(2,1)S(1)} %add_convert_fusion.2), channel_id=1, source_target_pairs={{0,16},{1,17},{2,18},{3,19},{4,20},{5,21},{6,22},{7,23},{8,24},{9,... | collective-permute-start | bytes 153608 | tf_op jit(solution)/shard_map/ppermute | solution.py:821
  35.1 1.5 %query_back_2.1 = (bf16[768,256]{1,0:T(8,128)(2,1)S(1)}, f32[192,768]{1,0:T(8,128)S(1)}) custom-call(bf16[128,768]{1,0:T(8,128)(2,1)S(1)} %collective-permute-done.1.far_ref, bf16[128,768]{1,0:T(8,128)(2,1)S(1)} %collective-permute-done.2.far_mate_ref, bf16[384,768]{1,0:T(8,128)(2,1)S(1)} %get-tuple-element.100.q_ref, ...), custom_call_target="tpu_custom_call" | custom-call | flops 1000000000 | bytes 3000000 | tf_op jit(solution)/shard_map/query_back_2/pallas_call | solution.py:994
  36.6 3.6 %collective-permute-start.14 = (bf16[160,768]{1,0:T(8,128)(2,1)S(1)}, bf16[160,768]{1,0:T(8,128)(2,1)S(1)}, u32[]{:S(2)}, u32[]{:S(2)}) collective-permute-start(bf16[160,768]{1,0:T(8,128)(2,1)S(1)} %collective-permute-done.10.far_ref), channel_id=1, source_target_pairs={{0,1},{1,0},{2,3},{3,2},{4,5},{5,4},{6,7},{7,6},{8,9},{9,8},{10,11... | collective-permute-start | bytes 737288 | tf_op jit(solution)/shard_map/ppermute | solution.py:818
  40.2 1.1 %collective-permute-start.13 = (bf16[200,128]{1,0:T(8,128)(2,1)S(1)}, bf16[200,128]{1,0:T(8,128)(2,1)S(1)}, u32[]{:S(2)}, u32[]{:S(2)}) collective-permute-start(bf16[200,128]{1,0:T(8,128)(2,1)S(1)} %add_convert_fusion.1), channel_id=1, source_target_pairs={{0,6},{1,7},{2,4},{3,5},{4,2},{5,3},{6,0},{7,1},{8,14},{9,15},{10,... | collective-permute-start | bytes 153608 | tf_op jit(solution)/shard_map/ppermute | solution.py:821
  41.4 0.5 collective-permute-start.12
  41.8 1.1 %collective-permute-start.11 = (bf16[200,128]{1,0:T(8,128)(2,1)S(1)}, bf16[200,128]{1,0:T(8,128)(2,1)S(1)}, u32[]{:S(2)}, u32[]{:S(2)}) collective-permute-start(bf16[200,128]{1,0:T(8,128)(2,1)S(1)} %add_convert_fusion.1), channel_id=1, source_target_pairs={{0,4},{1,5},{2,6},{3,7},{4,0},{5,1},{6,2},{7,3},{8,12},{9,13},{10,... | collective-permute-start | bytes 153608 | tf_op jit(solution)/shard_map/ppermute | solution.py:821
  43.1 2.6 %key_back_0.1.part_ref = f32[192,768]{1,0:T(8,128)S(1)} custom-call(bf16[768,768]{1,0:T(8,128)(2,1)S(1)} %get-tuple-element.161.grads_ref, f32[64,512]{1,0:T(8,128)S(1)} %get-tuple-element.162.stats_ref, bf16[768,768]{1,0:T(8,128)(2,1)S(1)} %get-tuple-element.142.kbuf, bf16[768,768]{1,0:T(8,128)(2,1)S(1)} %get-tuple-element.143.vbuf, ...), custom_call_target="tpu_custom_call" | custom-call | flops 2000000000 | bytes 3000000 | tf_op jit(solution)/shard_map/key_back_0/pallas_call | solution.py:1005
  45.8 1.6 %collective-permute-start.15 = (bf16[4,200,128]{2,1,0:T(8,128)(2,1)S(1)}, bf16[4,200,128]{2,1,0:T(8,128)(2,1)S(1)}, u32[]{:S(2)}, u32[]{:S(2)}) collective-permute-start(bf16[4,200,128]{2,1,0:T(8,128)(2,1)S(1)} %pad_maximum_fusion.1.here_ref), channel_id=1, source_target_pairs={{0,1},{1,0},{2,3},{3,2},{4,5},{5,4},{6,7},{7,6},{8,9},{9,8},{10,11... | collective-permute-start | bytes 614408 | tf_op jit(solution)/shard_map/ppermute | solution.py:821
  47.4 1.5 %key_back_2.1.grad_ref = bf16[192,768]{1,0:T(8,128)(2,1)S(1)} custom-call(bf16[768,768]{1,0:T(8,128)(2,1)S(1)} %get-tuple-element.161.grads_ref, f32[64,512]{1,0:T(8,128)S(1)} %get-tuple-element.162.stats_ref, bf16[768,768]{1,0:T(8,128)(2,1)S(1)} %get-tuple-element.142.kbuf, bf16[768,768]{1,0:T(8,128)(2,1)S(1)} %get-tuple-element.143.vbuf, ...), custom_call_target="tpu_custom_call" | custom-call | flops 1000000000 | bytes 3000000 | tf_op jit(solution)/shard_map/key_back_2/pallas_call | solution.py:1005
  48.9 1.1 %unpack.1 = (bf16[192,768]{1,0:T(8,128)(2,1)}, f32[64,768]{1,0:T(8,128)}, f32[64]{0:T(128)}, f32[64,768]{1,0:T(8,128)}, f32[768]{0:T(1024)}, /*index=5*/f32[768]...) custom-call(bf16[4,200,128]{2,1,0:T(8,128)(2,1)S(1)} %pad_maximum_fu, ...), custom_call_target="tpu_custom_call" | custom-call | tf_op jit(solution)/shard_map/unpack/pallas_call | solution.py:1052
  (30 shorter events, 1.4 us)
Async XLA Ops:
  0.6 1.9 %collective-permute-start = (bf16[192,768]{1,0:T(8,128)(2,1)}, bf16[192,768]{1,0:T(8,128)(2,1)S(1)}, u32[]{:S(2)}, u32[]{:S(2)}) collective-permute-start(bf16[192,768]{1,0:T(8,128)(2,1)} %bitcast.24), channel_id=1, source_target_pairs={{0,1},{1,0},{2,3},{3,2},{4,5},{5,4},{6,7},{7,6},{8,9},{9,8},{10,11... | collective-permute-start | bytes 884744 | tf_op jit(solution)/shard_map/ppermute | solution.py:818
  2.6 7.5 %collective-permute-start.1 = (bf16[128,768]{1,0:T(8,128)(2,1)S(1)}, bf16[128,768]{1,0:T(8,128)(2,1)S(1)}, u32[]{:S(2)}, u32[]{:S(2)}) collective-permute-start(bf16[128,768]{1,0:T(8,128)(2,1)S(1)} %pad_maximum_fusion.2), channel_id=1, source_target_pairs={{0,2},{1,3},{2,0},{3,1},{4,6},{5,7},{6,4},{7,5},{8,10},{9,11},{10,... | collective-permute-start | bytes 589832 | tf_op jit(solution)/shard_map/ppermute | solution.py:818
  10.0 2.1 %collective-permute-start.2 = (bf16[128,768]{1,0:T(8,128)(2,1)S(1)}, bf16[128,768]{1,0:T(8,128)(2,1)S(1)}, u32[]{:S(2)}, u32[]{:S(2)}) collective-permute-start(bf16[128,768]{1,0:T(8,128)(2,1)S(1)} %collective-permute-done.1.far_ref), channel_id=1, source_target_pairs={{0,1},{1,0},{2,3},{3,2},{4,5},{5,4},{6,7},{7,6},{8,9},{9,8},{10,11... | collective-permute-start | bytes 589832 | tf_op jit(solution)/shard_map/ppermute | solution.py:818
  22.0 1.5 %collective-permute-start.3 = (bf16[4,200,128]{2,1,0:T(8,128)(2,1)S(1)}, bf16[4,200,128]{2,1,0:T(8,128)(2,1)S(1)}, u32[]{:S(2)}, u32[]{:S(2)}) collective-permute-start(bf16[4,200,128]{2,1,0:T(8,128)(2,1)S(1)} %get-tuple-element.135), channel_id=1, source_target_pairs={{0,1},{1,0},{2,3},{3,2},{4,5},{5,4},{6,7},{7,6},{8,9},{9,8},{10,11... | collective-permute-start | bytes 614408 | tf_op jit(solution)/shard_map/ppermute | solution.py:821
  23.6 6.0 %collective-permute-start.7 = (bf16[224,768]{1,0:T(8,128)(2,1)S(1)}, bf16[224,768]{1,0:T(8,128)(2,1)S(1)}, u32[]{:S(2)}, u32[]{:S(2)}) collective-permute-start(bf16[224,768]{1,0:T(8,128)(2,1)S(1)} %get-tuple-element.154.pack_ref.own_ref), channel_id=1, source_target_pairs={{0,1},{1,0},{2,3},{3,2},{4,5},{5,4},{6,7},{7,6},{8,9},{9,8},{10,11... | collective-permute-start | bytes 1032200 | tf_op jit(solution)/shard_map/ppermute | solution.py:818
  23.8 4.9 %collective-permute-start.6 = (bf16[200,128]{1,0:T(8,128)(2,1)S(1)}, bf16[200,128]{1,0:T(8,128)(2,1)S(1)}, u32[]{:S(2)}, u32[]{:S(2)}) collective-permute-start(bf16[200,128]{1,0:T(8,128)(2,1)S(1)} %get-tuple-element.190), channel_id=1, source_target_pairs={{0,6},{1,7},{2,4},{3,5},{4,2},{5,3},{6,0},{7,1},{8,14},{9,15},{10,... | collective-permute-start | bytes 153608 | tf_op jit(solution)/shard_map/ppermute | solution.py:821
  26.3 3.1 %collective-permute-start.5 = (bf16[200,128]{1,0:T(8,128)(2,1)S(1)}, bf16[200,128]{1,0:T(8,128)(2,1)S(1)}, u32[]{:S(2)}, u32[]{:S(2)}) collective-permute-start(bf16[200,128]{1,0:T(8,128)(2,1)S(1)} %get-tuple-element.191), channel_id=1, source_target_pairs={{0,2},{1,3},{2,0},{3,1},{4,6},{5,7},{6,4},{7,5},{8,10},{9,11},{10,... | collective-permute-start | bytes 153608 | tf_op jit(solution)/shard_map/ppermute | solution.py:821
  26.6 3.0 %collective-permute-start.4 = (bf16[200,128]{1,0:T(8,128)(2,1)S(1)}, bf16[200,128]{1,0:T(8,128)(2,1)S(1)}, u32[]{:S(2)}, u32[]{:S(2)}) collective-permute-start(bf16[200,128]{1,0:T(8,128)(2,1)S(1)} %get-tuple-element.192), channel_id=1, source_target_pairs={{0,4},{1,5},{2,6},{3,7},{4,0},{5,1},{6,2},{7,3},{8,12},{9,13},{10,... | collective-permute-start | bytes 153608 | tf_op jit(solution)/shard_map/ppermute | solution.py:821
  29.6 3.1 %collective-permute-start.8 = (bf16[200,128]{1,0:T(8,128)(2,1)S(1)}, bf16[200,128]{1,0:T(8,128)(2,1)S(1)}, u32[]{:S(2)}, u32[]{:S(2)}) collective-permute-start(bf16[200,128]{1,0:T(8,128)(2,1)S(1)} %fusion.2), channel_id=1, source_target_pairs={{0,8},{1,9},{2,10},{3,11},{4,12},{5,13},{6,14},{7,15},{8,0},{9,1},... | collective-permute-start | bytes 153608 | tf_op jit(solution)/shard_map/ppermute | solution.py:821
  31.0 5.6 %collective-permute-start.10 = (bf16[160,768]{1,0:T(8,128)(2,1)S(1)}, bf16[160,768]{1,0:T(8,128)(2,1)S(1)}, u32[]{:S(2)}, u32[]{:S(2)}) collective-permute-start(bf16[160,768]{1,0:T(8,128)(2,1)S(1)} %pad_maximum_fusion), channel_id=1, source_target_pairs={{0,2},{1,3},{2,0},{3,1},{4,6},{5,7},{6,4},{7,5},{8,10},{9,11},{10,... | collective-permute-start | bytes 737288 | tf_op jit(solution)/shard_map/ppermute | solution.py:818
  32.7 7.5 %collective-permute-start.9 = (bf16[200,128]{1,0:T(8,128)(2,1)S(1)}, bf16[200,128]{1,0:T(8,128)(2,1)S(1)}, u32[]{:S(2)}, u32[]{:S(2)}) collective-permute-start(bf16[200,128]{1,0:T(8,128)(2,1)S(1)} %add_convert_fusion.2), channel_id=1, source_target_pairs={{0,16},{1,17},{2,18},{3,19},{4,20},{5,21},{6,22},{7,23},{8,24},{9,... | collective-permute-start | bytes 153608 | tf_op jit(solution)/shard_map/ppermute | solution.py:821
  36.6 6.4 %collective-permute-start.14 = (bf16[160,768]{1,0:T(8,128)(2,1)S(1)}, bf16[160,768]{1,0:T(8,128)(2,1)S(1)}, u32[]{:S(2)}, u32[]{:S(2)}) collective-permute-start(bf16[160,768]{1,0:T(8,128)(2,1)S(1)} %collective-permute-done.10.far_ref), channel_id=1, source_target_pairs={{0,1},{1,0},{2,3},{3,2},{4,5},{5,4},{6,7},{7,6},{8,9},{9,8},{10,11... | collective-permute-start | bytes 737288 | tf_op jit(solution)/shard_map/ppermute | solution.py:818
  40.2 5.5 %collective-permute-start.13 = (bf16[200,128]{1,0:T(8,128)(2,1)S(1)}, bf16[200,128]{1,0:T(8,128)(2,1)S(1)}, u32[]{:S(2)}, u32[]{:S(2)}) collective-permute-start(bf16[200,128]{1,0:T(8,128)(2,1)S(1)} %add_convert_fusion.1), channel_id=1, source_target_pairs={{0,6},{1,7},{2,4},{3,5},{4,2},{5,3},{6,0},{7,1},{8,14},{9,15},{10,... | collective-permute-start | bytes 153608 | tf_op jit(solution)/shard_map/ppermute | solution.py:821
  41.4 4.4 %collective-permute-start.12 = (bf16[200,128]{1,0:T(8,128)(2,1)S(1)}, bf16[200,128]{1,0:T(8,128)(2,1)S(1)}, u32[]{:S(2)}, u32[]{:S(2)}) collective-permute-start(bf16[200,128]{1,0:T(8,128)(2,1)S(1)} %add_convert_fusion.1), channel_id=1, source_target_pairs={{0,2},{1,3},{2,0},{3,1},{4,6},{5,7},{6,4},{7,5},{8,10},{9,11},{10,... | collective-permute-start | bytes 153608 | tf_op jit(solution)/shard_map/ppermute | solution.py:821
  41.8 3.9 %collective-permute-start.11 = (bf16[200,128]{1,0:T(8,128)(2,1)S(1)}, bf16[200,128]{1,0:T(8,128)(2,1)S(1)}, u32[]{:S(2)}, u32[]{:S(2)}) collective-permute-start(bf16[200,128]{1,0:T(8,128)(2,1)S(1)} %add_convert_fusion.1), channel_id=1, source_target_pairs={{0,4},{1,5},{2,6},{3,7},{4,0},{5,1},{6,2},{7,3},{8,12},{9,13},{10,... | collective-permute-start | bytes 153608 | tf_op jit(solution)/shard_map/ppermute | solution.py:821
  45.8 3.0 %collective-permute-start.15 = (bf16[4,200,128]{2,1,0:T(8,128)(2,1)S(1)}, bf16[4,200,128]{2,1,0:T(8,128)(2,1)S(1)}, u32[]{:S(2)}, u32[]{:S(2)}) collective-permute-start(bf16[4,200,128]{2,1,0:T(8,128)(2,1)S(1)} %pad_maximum_fusion.1.here_ref), channel_id=1, source_target_pairs={{0,1},{1,0},{2,3},{3,2},{4,5},{5,4},{6,7},{7,6},{8,9},{9,8},{10,11... | collective-permute-start | bytes 614408 | tf_op jit(solution)/shard_map/ppermute | solution.py:821
